TPU v7x, 32 devices: a whole 2x2x4 slice. The times are simulated.
32 devices in a mesh: groups: 2 (over y), src: 4 (over z), blk: 4 (over x, core).
Axes of the slice: x: 2, y: 2, z: 4, core: 2. Of those that a mesh axis runs over, the one named last changes fastest.
Arguments:
- pupils: float32 [8192, 2, 128], P(('groups', 'src', 'blk')), parts along dimension 0, may hold values from -6 to 6
- starts: int32 [8192], P(('groups', 'src', 'blk')), parts along dimension 0, may hold values from 0 to 127, as said below
- counts: int32 [8192], P(('groups', 'src', 'blk')), parts along dimension 0, may hold values from 0 to 2, as said below
- weights: float32 [8192], P(('groups', 'src', 'blk')), parts along dimension 0, may hold values from 0.25 to 2.5
- start_block: float32 [4, 8192, 128], P('groups', 'blk'), parts along dimension 0, may hold values from -6 to 6
Outputs:
- kernels: float32 [4, 8192, 128], P('groups', 'blk'), parts along dimension 0
There are 2 independent parts, one for each index of `groups`. A program takes and returns all parts, laid end to end along the dimension named above; each array names one. Nothing has to cross between parts.
Inputs may be any that keep to these rules, and one draw needn't show every extreme that they name: starts[j] // 32 = (j // 256) % 4: every source begins in the region of the aligned block of 256 slots that holds it. In each aligned block of 256 slots the slots with counts > 0 come first; in every block whose index modulo 4 is 3 all slots have counts > 0.
All inputs are finite; a program needn't handle non-finite values.
Results may differ from a plain program's by a relative error of at most 0.00012.
Values sent between devices are 32-bit elements; how exact they have to be, the bound alone decides.
No kernel may reach another device: no remote copies, remote signals or barrier semaphores. Data moves between devices by JAX's collectives and lax.ppermute only.
A program may use at most 64 MiB of HBM per device.

v0:
```python
from functools import partial

import jax
import jax.numpy as jnp
from jax import lax
from jax.sharding import PartitionSpec as P

BLOCK = 64
RB = 32
ITERS = 2


HIGH_ACCURACY = lax.Precision.HIGHEST


def padded_2(cells, sides, width):
    for axis, dim in sides:
        count = lax.axis_size(axis)
        ends = count - 1
        head = lax.slice_in_dim(cells, 0, width, axis=dim)
        tail = lax.slice_in_dim(cells, cells.shape[dim] - width, cells.shape[dim], axis=dim)
        cells = jnp.concatenate(
            [
                lax.ppermute(tail, axis, [(i, (i + 1) % count) for i in range(ends)]),
                cells,
                lax.ppermute(head, axis, [((i + 1) % count, i) for i in range(ends)]),
            ],
            axis=dim,
        )
    return cells


def shifted(x, axis, by):
    peers = lax.axis_size(axis)
    pairs = [(i, i + by) for i in range(peers) if 0 <= i + by < peers]
    return lax.ppermute(x, axis, pairs)


def locate(pupils, starts, counts, region):
    offset = jnp.arange(2, dtype=jnp.int32)
    places = starts[:, None] - region * RB + offset[None, :]
    living = (offset[None, :] < counts[:, None]).astype(jnp.float32)
    return (pupils * living[:, :, None], places)


def band_terms(live_pupil, places, weights, pairs, slot_count):
    source_count = live_pupil.shape[0]
    group_size = min(32, source_count)
    scaled = live_pupil * weights[:, None, None]
    members = (
        live_pupil.reshape(-1, group_size, 2, 2 * BLOCK),
        scaled.reshape(-1, group_size, 2, 2 * BLOCK),
        places.reshape(-1, group_size, 2),
    )

    def one_group(totals, member):
        plain_rows, left_row_block, block_at = member
        totals = list(totals)
        for row_part, col_part, diag_slot in pairs:
            left_real = left_row_block[:, row_part, :BLOCK]
            left_im = left_row_block[:, row_part, BLOCK:]
            right_re = plain_rows[:, col_part, :BLOCK]
            right_im = plain_rows[:, col_part, BLOCK:]
            real_part = (
                left_real[:, :, None] * right_re[:, None, :]
                + left_im[:, :, None] * right_im[:, None, :]
            )
            imag_part = (
                left_im[:, :, None] * right_re[:, None, :]
                - left_real[:, :, None] * right_im[:, None, :]
            )
            totals[diag_slot] = (
                totals[diag_slot]
                .at[block_at[:, row_part]]
                .add(jnp.concatenate([real_part, imag_part], axis=2))
            )
        return (tuple(totals), None)

    initial = tuple(
        (jnp.zeros((RB + 1, BLOCK, 2 * BLOCK), jnp.float32) for diag_slot in range(slot_count))
    )
    totals, unused = lax.scan(one_group, initial, members)
    return jnp.stack(totals, axis=2).reshape((RB + 1) * BLOCK, slot_count, 2 * BLOCK)


def apply_owned(tile_rows, subspace_step, src_index):
    segment_count = tile_rows.shape[0]
    rows_own = segment_count * BLOCK
    columns = subspace_step.shape[2]
    padded = padded_2(subspace_step, (("blk", 1),), BLOCK)
    window = lax.dynamic_slice_in_dim(padded, src_index * rows_own, (segment_count + 2) * BLOCK, 1)
    blocks = window.reshape(2, segment_count + 2, BLOCK, columns)
    nearby = jnp.stack(
        [blocks[:, shift_by : shift_by + segment_count] for shift_by in range(3)], axis=2
    )
    tile_re = tile_rows[..., :BLOCK]
    tile_im = tile_rows[..., BLOCK:]
    worker_member = partial(jnp.einsum, "snah,sahi->sni", precision=HIGH_ACCURACY)
    result_re = worker_member(tile_re, nearby[0]) - worker_member(tile_im, nearby[1])
    result_im = worker_member(tile_im, nearby[0]) + worker_member(tile_re, nearby[1])
    return jnp.stack([result_re, result_im]).reshape(2, rows_own, columns)


def gram_matrix(rows_block):
    return jnp.einsum("cfm,cfn->mn", rows_block, rows_block, precision=HIGH_ACCURACY)


def finish(product, gram_sum, row_total):
    factor = jnp.linalg.cholesky(gram_sum / row_total)
    flattened = product.reshape(-1, product.shape[2])
    solved = lax.linalg.triangular_solve(
        factor, flattened, left_side=False, lower=True, transpose_a=True
    )
    return solved.reshape(product.shape)


def normalize(product, row_total):
    gram_sum = lax.psum(gram_matrix(product), ("src", "blk"))
    result = lax.all_gather(finish(product, gram_sum, row_total), "src", axis=1, tiled=True)
    return result


def build_tiles(live_pupil, places, weights, row_count):
    segment_count = RB // lax.axis_size("src")
    band_rows = band_terms(
        live_pupil, places, weights, ((1, 0, 0), (0, 0, 1), (1, 1, 1), (0, 1, 2)), 3
    )
    spilled = shifted(band_rows[row_count:], "blk", 1)
    band_rows = band_rows[:row_count].at[:BLOCK].add(spilled)
    owned_rows = lax.psum_scatter(band_rows, "src", scatter_dimension=0, tiled=True)
    tile_rows = owned_rows.reshape(segment_count, BLOCK, 3, 2 * BLOCK)
    return tile_rows


def per_device(pupils, starts, counts, weights, start_block):
    region = lax.axis_index("blk")
    src_index = lax.axis_index("src")
    live_pupil, places = locate(pupils, starts, counts, region)
    subspace_step = start_block
    row_count = subspace_step.shape[1]
    row_total = 2.0 * row_count * lax.axis_size("blk")
    tile_rows = build_tiles(live_pupil, places, weights, row_count)
    for sweeps in range(ITERS):
        product = apply_owned(tile_rows, subspace_step, src_index)
        subspace_step = normalize(product, row_total)
    return subspace_step


def solution(mesh):
    placed = (
        P(("groups", "src", "blk"), None, None),
        P(("groups", "src", "blk")),
        P(("groups", "src", "blk")),
        P(("groups", "src", "blk")),
        P("groups", "blk", None),
    )
    return jax.shard_map(
        per_device, mesh=mesh, in_specs=placed, out_specs=P("groups", "blk", None), check_vma=False
    )
```

profile of v0, /device:TPU:0, one launch (start us, length us, event | category | flops | bytes accessed | tf_op | source)
XLA Modules:
  0.0 619.8 jit_solution(1636295830130865191)
XLA Ops:
  11.5 177.9 %while.15 = (s32[]{:T(128)}, f32[33,64,128]{2,1,0:T(8,128)}, f32[33,64,128]{2,1,0:T(8,128)S(1)}, f32[33,64,128]{2,1,0:T(8,128)}, s32[8,32,2]{1,2,0:T(2,128)S(1)}...) while((s32[]{:T(128)}, f32[33,64,128]{2,1,0:T(8,128)}, ...), condition=%wide.region_5.6_spmd, body=%wide.region_0.5_spmd.sunk | while | flops 5243074 | bytes 33883880 | solution.py:82
  12.2 3.5 multiply_add_fusion.5
  16.0 4.8 scatter_fusion.3
  28.9 4.8 scatter_fusion
  34.4 3.5 multiply_add_fusion.5
  38.2 4.8 scatter_fusion.3
  45.3 2.1 scatter_fusion.1
  47.4 2.1 scatter_fusion.2
  51.1 4.8 scatter_fusion
  56.6 3.5 multiply_add_fusion.5
  60.5 4.8 scatter_fusion.3
  67.5 2.1 scatter_fusion.1
  69.6 2.1 scatter_fusion.2
  73.4 4.8 scatter_fusion
  78.8 3.5 multiply_add_fusion.5
  82.7 4.9 scatter_fusion.3
  89.8 2.1 scatter_fusion.1
  91.9 2.1 scatter_fusion.2
  95.6 4.8 scatter_fusion
  101.1 3.5 multiply_add_fusion.5
  105.0 4.8 scatter_fusion.3
  117.8 4.8 scatter_fusion
  123.3 3.5 multiply_add_fusion.5
  127.2 4.8 scatter_fusion.3
  134.3 2.1 scatter_fusion.1
  136.4 2.1 scatter_fusion.2
  140.1 4.8 scatter_fusion
  145.6 3.5 multiply_add_fusion.5
  149.5 4.8 scatter_fusion.3
  162.3 4.8 scatter_fusion
  167.8 3.5 multiply_add_fusion.5
  171.7 4.9 scatter_fusion.3
  184.6 4.8 scatter_fusion
  190.3 2.7 collective-permute-start
  198.0 4.5 collective-permute-start.1
  203.8 2.6 collective-permute-done.2
  206.9 53.5 %reduce-scatter.2.cloned.1.call-done = f32[512,3,128]{2,0,1:T(8,128)} async-done(((f32[2048,3,128]{2,0,1:T(8,128)}), f32[512,3,128]{2,0,1:T(8,128)}) %reduce-scatter.2.cloned.1.call-update) | async-done | bytes 786448 | tf_op jit(solution)/shard_map/reduce_scatter | solution.py:130
  269.4 83.4 %all-reduce.3.cloned.1.call-done = f32[128,128]{0,1:T(8,128)} async-done(((f32[128,128]{0,1:T(8,128)}), f32[128,128]{0,1:T(8,128)}) %all-reduce.3.cloned.1.call-update) | async-done | bytes 65552 | tf_op jit(solution)/shard_map/psum | solution.py:118
  354.6 11.7 %cholesky.44 = f32[128,128]{1,0:T(8,128)S(1)} custom-call(f32[128,128]{1,0:T(8,128)S(1)} %fusion.27), custom_call_target="Cholesky" | custom-call | tf_op jit(solution)/shard_map/jit(cholesky)/cholesky | solution.py:109
  367.7 9.8 %custom-call.6 = f32[1,128,128]{1,2,0:T(8,128)S(1)} custom-call(f32[1,128,128]{2,1,0:T(8,128)S(1)} %fusion.22), custom_call_target="InvertDiagBlocksLowerTriangular" | custom-call | tf_op jit(solution)/shard_map/triangular_solve/custom-call.0 | solution.py:111
  379.4 47.9 %all-gather.3.cloned.1.call-done = f32[2,2048,128]{1,0,2:T(2,128)} async-done(((f32[2,512,128]{1,0,2:T(2,128)}), f32[2,2048,128]{1,0,2:T(2,128)}) %all-gather.3.cloned.1.call-update) | async-done | bytes 2097168 | tf_op jit(solution)/shard_map/all_gather | solution.py:119
  431.4 3.5 collective-permute-done.4
  434.8 8.6 %concatenate.21 = f32[2,2176,128]{1,0,2:T(2,128)} concatenate(f32[2,64,128]{1,0,2:T(2,128)S(1)} %collective-permute-done.3, f32[2,2048,128]{1,0,2:T(2,128)} %all-gather.3.cloned.1.call-done, f32[2,64,128]{1,0,2:T(2,128)S(1)} %collective-permute-done.4), dimensions={1} | concatenate | bytes 4456448 | tf_op jit(solution)/shard_map/concatenate | solution.py:22
  451.4 84.8 %all-reduce.5.cloned.1.call-done = f32[128,128]{0,1:T(8,128)} async-done(((f32[128,128]{0,1:T(8,128)}), f32[128,128]{0,1:T(8,128)}) %all-reduce.5.cloned.1.call-update) | async-done | bytes 65552 | tf_op jit(solution)/shard_map/psum | solution.py:118
  538.0 11.7 %cholesky.55 = f32[128,128]{1,0:T(8,128)S(1)} custom-call(f32[128,128]{1,0:T(8,128)S(1)} %fusion.25), custom_call_target="Cholesky" | custom-call | tf_op jit(solution)/shard_map/jit(cholesky)/cholesky | solution.py:109
  551.0 9.8 %custom-call.7 = f32[1,128,128]{1,2,0:T(8,128)S(1)} custom-call(f32[1,128,128]{2,1,0:T(8,128)S(1)} %fusion.23), custom_call_target="InvertDiagBlocksLowerTriangular" | custom-call | tf_op jit(solution)/shard_map/triangular_solve/custom-call.0 | solution.py:111
  562.5 47.7 %all-gather.5.cloned.1.call-done = f32[2,2048,128]{2,1,0:T(8,128)} async-done(((f32[2,512,128]{2,1,0:T(8,128)}), f32[2,2048,128]{2,1,0:T(8,128)}) %all-gather.5.cloned.1.call-update) | async-done | bytes 2097168 | tf_op jit(solution)/shard_map/all_gather | solution.py:119
  610.2 3.0 copy.103
  (235 shorter events, 98.6 us)
Async XLA Ops:
  6.5 253.9 %reduce-scatter.2.cloned.1.call-start = ((), (), s32[]{:S(2)}) async-start(), calls=%async_computation.1 | async-start | bytes 3932160 | tf_op jit(solution)/shard_map/reduce_scatter | solution.py:130
  20.8 1.7 copy-start.1
  20.8 1.9 copy-start.2
  25.2 2.1 copy-start
  28.9 4.8 copy-start.8
  33.7 0.7 copy-start.7
  43.1 1.7 copy-start.1
  43.1 1.9 copy-start.2
  47.4 2.1 copy-start
  51.1 4.8 copy-start.8
  65.3 1.7 copy-start.1
  65.3 1.9 copy-start.2
  69.6 2.1 copy-start
  73.3 4.8 copy-start.8
  78.1 0.7 copy-start.7
  87.6 1.7 copy-start.1
  87.6 1.9 copy-start.2
  91.9 2.1 copy-start
  95.6 4.8 copy-start.8
  100.4 0.7 copy-start.7
  109.8 1.7 copy-start.1
  109.8 1.9 copy-start.2
  114.1 2.1 copy-start
  117.8 4.8 copy-start.8
  132.1 1.7 copy-start.1
  132.1 1.9 copy-start.2
  136.4 2.1 copy-start
  140.1 4.8 copy-start.8
  154.3 1.7 copy-start.1
  154.3 1.9 copy-start.2
  158.6 2.1 copy-start
  162.3 4.8 copy-start.8
  176.5 1.7 copy-start.1
  176.5 1.9 copy-start.2
  180.8 2.1 copy-start
  184.6 4.8 copy-start.8
  189.4 3.6 copy-start.3
  189.4 3.6 copy-start.4
  190.3 5.4 collective-permute-start
  196.4 1.6 copy-start.5
  196.4 156.4 %all-reduce.3.cloned.1.call-start = ((), (), s32[]{:S(2)}) async-start(), calls=%async_computation.2 | async-start | bytes 131072 | tf_op jit(solution)/shard_map/psum | solution.py:118
  198.0 5.8 collective-permute-start.1
  202.5 3.9 collective-permute-start.2
  268.2 159.2 %all-gather.3.cloned.1.call-start = ((), (), s32[]{:S(2)}) async-start(), calls=%async_computation.3 | async-start | bytes 2621440 | tf_op jit(solution)/shard_map/all_gather | solution.py:119
  379.4 156.8 %all-reduce.5.cloned.1.call-start = ((), (), s32[]{:S(2)}) async-start(), calls=%async_computation.4 | async-start | bytes 131072 | tf_op jit(solution)/shard_map/psum | solution.py:118
  428.6 2.8 collective-permute-start.3
  429.9 5.0 collective-permute-start.4
  451.0 159.1 %all-gather.5.cloned.1.call-start = ((), (), s32[]{:S(2)}) async-start(), calls=%async_computation.5 | async-start | bytes 2621440 | tf_op jit(solution)/shard_map/all_gather | solution.py:119
  (6 other events, 4.2 us)
Sparse Core Ops, SparseCore 0:
  196.5 63.8 reduce-scatter.1
  268.3 84.4 all-reduce.2
  379.5 47.8 all-gather.2
  451.2 84.9 all-reduce.4
  562.6 47.5 all-gather.4
where the time goes:
time: 624 us; the launch traced here: 620 us
  waiting for transfers between devices  324 us (52%)
  other arithmetic  225 us (36%)
  local copies, waits for them, and re-layouts  32.8 us (5%)
  between operations  13.4 us (2%)
  starting transfers between devices  11.9 us (2%)
  matrix products  11.9 us (2%)
    psum x2, waiting for transfers between devices, normalize(): gram_sum = lax.psum(gram_matrix(product), ('src', 'blk'))  168 us
    scatter-add x32, other arithmetic, one_group(): totals[diag_slot] = totals[diag_slot].at[block_at[:, row_part]].add(jnp.c...  111 us
    all_gather x2, waiting for transfers between devices, normalize(): lax.all_gather(finish(product, gram_sum, row_total), 'src', axis=1, tiled...  95.6 us
    reduce_scatter x1, waiting for transfers between devices, build_tiles(): lax.psum_scatter(band_rows, 'src', scatter_dimension=0, tiled=True)  53.5 us
    concatenate x32, other arithmetic, one_group(): jnp.concatenate([real_part, imag_part], axis=2)  31.6 us
    add x8, other arithmetic, one_group(): left_real[:, :, None] * right_re[:, None, :]  27.9 us
    another operation x6, other arithmetic, finish(): factor = jnp.linalg.cholesky(gram_sum / row_total)  24.8 us
    another operation x4, other arithmetic, finish(): lax.linalg.triangular_solve(factor, flattened, left_side=False, lower=Tru...  20.9 us
  transfers between devices with their start and end apart: 10, of which 7 were waited for; matrix products, arithmetic and copies ran while one was open for 1% of the time, Pallas kernels for 0%

commit v1 on v0

v1 whole, which is shorter than its diff:
```python
from functools import partial

import jax
import jax.numpy as jnp
from jax import lax
from jax.experimental import pallas as pl
from jax.experimental.pallas import tpu as pltpu
from jax.sharding import PartitionSpec as P

BLOCK = 64
RB = 32
GROUP = 8
M = 128
F32 = jnp.float32
BF16 = jnp.bfloat16
HIGHEST = lax.Precision.HIGHEST
VMEM = pl.BlockSpec(memory_space=pltpu.VMEM)
PARAMS = pltpu.CompilerParams(vmem_limit_bytes=40 * 1024 * 1024)


def split(x):
    hi = x.astype(BF16)
    return hi, (x - hi.astype(F32)).astype(BF16)


def dot(a, b):
    return jnp.dot(a, b, preferred_element_type=F32)


def dot_t(a, b):
    return lax.dot_general(a, b, (((0,), (0,)), ((), ())), preferred_element_type=F32)


def dot_f32(a, b):
    return jnp.dot(a, b, precision=HIGHEST, preferred_element_type=F32)


def build_kernel(add, *refs):
    if add:
        pupils, live, rows, before, out, lhs_hi, lhs_lo = refs
    else:
        pupils, live, rows, out, lhs_hi, lhs_lo = refs
    count = pupils.shape[0] // 2
    lane = lax.broadcasted_iota(jnp.int32, (count, 2 * BLOCK), 1)
    first = pupils[pl.ds(0, count, stride=2), :] * live[pl.ds(0, count, stride=2), :]
    second = pupils[pl.ds(1, count, stride=2), :] * live[pl.ds(1, count, stride=2), :]
    real = jnp.where(lane < BLOCK, first, pltpu.roll(second, BLOCK, 1))
    imag = jnp.where(lane < BLOCK, pltpu.roll(first, BLOCK, 1), second)
    right = jnp.concatenate(
        [
            jnp.concatenate([real, -imag], axis=1),
            jnp.concatenate([imag, real], axis=1),
        ],
        axis=0,
    )
    right_hi, right_lo = split(right)
    left = jnp.concatenate([real.T, imag.T], axis=1) * rows[1:2, :]
    left_hi, left_lo = split(left)
    left_hi = left_hi.reshape(8, 16, 2 * count)
    left_lo = left_lo.reshape(8, 16, 2 * count)
    place = jnp.broadcast_to(rows[0:1, :], (16, 2 * count))

    def one_group(g, carry):
        for j in range(GROUP):
            b = (g * GROUP + j).astype(F32)
            mask = jnp.where(place == b, 1.0, 0.0).astype(BF16)[None]
            lhs_hi[j * 128 : (j + 1) * 128, :] = (left_hi * mask).reshape(128, 2 * count)
            lhs_lo[j * 128 : (j + 1) * 128, :] = (left_lo * mask).reshape(128, 2 * count)
        at = pl.ds(pl.multiple_of(g * GROUP * 128, GROUP * 128), GROUP * 128)
        hi = lhs_hi[...]
        total = dot(hi, right_hi) + dot(hi, right_lo) + dot(lhs_lo[...], right_hi)
        out[at, :] = before[at, :] + total if add else total
        return carry

    lax.fori_loop(0, RB // GROUP, one_group, 0)


def build(pupils, live, rows, before):
    count = pupils.shape[0] // 2
    args = (pupils, live, rows) + (() if before is None else (before,))
    return pl.pallas_call(
        partial(build_kernel, before is not None),
        out_shape=jax.ShapeDtypeStruct((RB * 128, 256), F32),
        in_specs=[VMEM] * len(args),
        out_specs=VMEM,
        scratch_shapes=[pltpu.VMEM((GROUP * 128, 2 * count), BF16)] * 2,
        input_output_aliases={} if before is None else {3: 0},
        compiler_params=PARAMS,
        cost_estimate=pl.CostEstimate(
            flops=6 * RB * 128 * 2 * count * 256, bytes_accessed=10 << 20, transcendentals=0
        ),
        name="band_terms",
    )(*args)


def swapped(x):
    return jnp.concatenate([-x[:, M:], x[:, :M]], axis=1)


def gram_of(hi, lo):
    a = dot_t(hi, hi)
    b = dot_t(hi, lo)
    a = a[:M, :M] + a[M:, M:]
    b = b[:M, :M] + b[M:, M:]
    return a + b + b.T


def apply_kernel(band, left_band, right_band, x, x_left, x_right, z, grams,
                 g_hi, g_lo, x_hi, x_lo, s_hi, s_lo, p, p_hi, p_lo):
    pairs = RB + 3
    zero = jnp.zeros((BLOCK, 256), BF16)

    def put_g(e_rows, value):
        hi, lo = split(value)
        g_hi[e_rows, :] = hi
        g_lo[e_rows, :] = lo

    g_hi[0:BLOCK, :] = zero
    g_lo[0:BLOCK, :] = zero
    put_g(pl.ds(BLOCK, 3 * BLOCK), left_band[...])
    put_g(pl.ds((RB + 2) * 128, BLOCK), right_band[...])
    g_hi[(RB + 2) * 128 + BLOCK :, :] = zero
    g_lo[(RB + 2) * 128 + BLOCK :, :] = zero

    def put_x(at, value):
        hi, lo = split(value)
        x_hi[at, :] = hi
        x_lo[at, :] = lo
        hi, lo = split(swapped(value))
        s_hi[at, :] = hi
        s_lo[at, :] = lo

    put_x(pl.ds(0, 2 * BLOCK), jnp.concatenate([x_left[0], x_left[1]], axis=1))
    put_x(pl.ds((RB + 2) * BLOCK, 2 * BLOCK), jnp.concatenate([x_right[0], x_right[1]], axis=1))

    def prepare(i, carry):
        at = pl.ds(pl.multiple_of(i * 256, 256), 256)
        put_g(pl.ds(pl.multiple_of(256 + i * 256, 256), 256), band[at, :])
        half = pl.ds(pl.multiple_of(i * 128, 128), 128)
        put_x(
            pl.ds(pl.multiple_of(i * 128 + 128, 128), 128),
            jnp.concatenate([x[0, half, :], x[1, half, :]], axis=1),
        )
        return carry

    lax.fori_loop(0, RB // 2, prepare, 0)

    def pair(e):
        at = pl.ds(pl.multiple_of(e * 128, 128), 128)
        win = pl.ds(pl.multiple_of(e * BLOCK, BLOCK), 128)
        w_hi = jnp.concatenate([x_hi[win, :], s_hi[win, :]], axis=0)
        w_lo = jnp.concatenate([x_lo[win, :], s_lo[win, :]], axis=0)
        hi = g_hi[at, :]
        return dot(hi, w_hi) + dot(hi, w_lo) + dot(g_lo[at, :], w_hi)

    def first(e, carry):
        both = pair(e)
        p[pl.ds(pl.multiple_of(e * BLOCK, BLOCK), BLOCK), :] = both[:BLOCK] + carry
        return both[BLOCK:]

    lax.fori_loop(0, pairs, first, jnp.zeros((BLOCK, 256), F32))

    def prepare_again(i, carry):
        at = pl.ds(pl.multiple_of(i * 128, 128), 128)
        put_x(at, p[at, :])
        return carry

    lax.fori_loop(0, (RB + 4) // 2, prepare_again, 0)
    rows = RB * BLOCK
    inner = pl.ds(2 * BLOCK, rows)
    grams[0:M, :] = gram_of(x_hi[inner, :], x_lo[inner, :])

    def second(e, carry):
        both = pair(e)
        z[pl.ds(pl.multiple_of((e - 2) * BLOCK, BLOCK), BLOCK), :] = both[:BLOCK] + carry
        return both[BLOCK:]

    lax.fori_loop(2, RB + 2, second, pair(1)[BLOCK:])

    top = jnp.max(jnp.abs(z[...]), axis=0, keepdims=True)
    top = jnp.maximum(top[:, :M], top[:, M:])
    scale = jnp.where(top > 0, 1.0 / jnp.where(top > 0, top, 1.0), 1.0)
    scale = jnp.concatenate([scale, scale], axis=1)

    def prepare_z(i, carry):
        at = pl.ds(pl.multiple_of(i * 128, 128), 128)
        hi, lo = split(z[at, :] * scale)
        p_hi[at, :] = hi
        p_lo[at, :] = lo
        return carry

    lax.fori_loop(0, rows // 128, prepare_z, 0)
    grams[M : 2 * M, :] = gram_of(p_hi[...], p_lo[...])
    grams[2 * M :, :] = jnp.broadcast_to(top, (8, M))


def apply_twice(band, left_band, right_band, x, x_left, x_right):
    rows = RB * BLOCK
    wide = (RB + 4) * BLOCK
    return pl.pallas_call(
        apply_kernel,
        out_shape=(
            jax.ShapeDtypeStruct((rows, 256), F32),
            jax.ShapeDtypeStruct((2 * M + 8, M), F32),
        ),
        in_specs=[VMEM] * 6,
        out_specs=(VMEM, VMEM),
        scratch_shapes=[pltpu.VMEM(((RB + 3) * 128, 256), BF16)] * 2
        + [pltpu.VMEM((wide, 256), BF16)] * 4
        + [pltpu.VMEM((wide, 256), F32)]
        + [pltpu.VMEM((rows, 256), BF16)] * 2,
        compiler_params=PARAMS,
        cost_estimate=pl.CostEstimate(
            flops=12 * RB * 128 * 256 * 256, bytes_accessed=12 << 20, transcendentals=0
        ),
        name="apply_twice",
    )(band, left_band, right_band, x, x_left, x_right)


def inverse_factor(a, work):
    row = lax.broadcasted_iota(jnp.int32, (M, M), 0)
    col = lax.broadcasted_iota(jnp.int32, (M, M), 1)
    work[:, :M] = a
    work[:, M:] = jnp.where(row == col, 1.0, 0.0)
    sub = lax.broadcasted_iota(jnp.int32, (8, M), 0)
    sub2 = lax.broadcasted_iota(jnp.int32, (8, 2 * M), 0)
    for p in range(M // 8):
        at = slice(8 * p, 8 * p + 8)
        panel = work[at, :]
        cols = [
            jnp.broadcast_to(panel[:, 8 * p + k : 8 * p + k + 1], (8, M)) for k in range(8)
        ]
        scales = jnp.zeros((8, M), F32)
        for j in range(8):
            pivot = jnp.broadcast_to(cols[j][j : j + 1, :], (8, M))
            root = lax.rsqrt(pivot)
            scales = jnp.where(sub == j, root, scales)
            if j < 7:
                part = jnp.where(sub > j, cols[j] * (root * root), 0.0)
                for k in range(j + 1, 8):
                    cols[k] = cols[k] - part * cols[k][j : j + 1, :]
                panel = panel - jnp.concatenate([part, part], axis=1) * panel[j : j + 1, :]
        panel = panel * jnp.concatenate([scales, scales], axis=1)
        work[at, :] = panel
        if p < M // 8 - 1:
            update = lax.dot_general(
                panel[:, :M], panel, (((0,), (0,)), ((), ())),
                precision=HIGHEST, preferred_element_type=F32,
            )
            work[8 * p + 8 :, :] = work[8 * p + 8 :, :] - update[8 * p + 8 :, :]
    return work[:, M:]


def finish_kernel(total_rows, grams, z, out, work):
    peers = grams.shape[0]
    row = lax.broadcasted_iota(jnp.int32, (M, M), 0)
    col = lax.broadcasted_iota(jnp.int32, (M, M), 1)
    eye = jnp.where(row == col, 1.0, 0.0)

    def as_column(v):
        return jnp.sum(eye * v, axis=1, keepdims=True)

    gram = grams[0, :M, :]
    for r in range(1, peers):
        gram = gram + grams[r, :M, :]
    norm = lax.rsqrt(jnp.sum(eye * gram, axis=0, keepdims=True))
    inverse = inverse_factor(gram * norm * as_column(norm), work)
    gram = jnp.zeros((M, M), F32)
    for r in range(peers):
        size = norm * grams[r, 2 * M : 2 * M + 1, :]
        gram = gram + grams[r, M : 2 * M, :] * size * as_column(size)
    gram = dot_f32(dot_f32(inverse, gram), inverse.T)
    inverse = dot_f32(inverse_factor(gram, work), inverse)
    change = (inverse * (norm * (total_rows**0.5))).T
    c_hi, c_lo = split(change)
    right = jnp.concatenate(
        [
            jnp.concatenate([c_hi, c_lo], axis=1),
            jnp.concatenate([c_hi, jnp.zeros_like(c_lo)], axis=1),
        ],
        axis=0,
    )
    step = 256

    def rows_of(i, carry):
        at = pl.ds(pl.multiple_of(i * step, step), step)
        value = z[at, :]
        for part in range(2):
            hi, lo = split(value[:, part * M : (part + 1) * M])
            both = dot(jnp.concatenate([hi, lo], axis=1), right)
            out[part, at, :] = both[:, :M] + both[:, M:]
        return carry

    lax.fori_loop(0, z.shape[0] // step, rows_of, 0)


def finish(grams, z, total_rows):
    return pl.pallas_call(
        partial(finish_kernel, total_rows),
        out_shape=jax.ShapeDtypeStruct((2, z.shape[0], M), F32),
        in_specs=[VMEM] * 2,
        out_specs=VMEM,
        scratch_shapes=[pltpu.VMEM((M, 2 * M), F32)],
        compiler_params=PARAMS,
        name="finish",
    )(grams, z)


def shifted(x, by):
    peers = lax.axis_size("blk")
    pairs = [(i, i + by) for i in range(peers) if 0 <= i + by < peers]
    return lax.ppermute(x, "blk", pairs)


def per_device(pupils, starts, counts, weights, start_block):
    region = lax.axis_index("blk")
    me = lax.axis_index("src")
    regions = lax.axis_size("blk")
    peers = lax.axis_size("src")
    slots = pupils.shape[0]

    own = pupils.reshape(slots * 2, 2 * BLOCK)
    chunks = [own]
    for k in range(1, peers):
        chunks.append(lax.ppermute(own, "src", [(i, (i + k) % peers) for i in range(peers)]))

    last = jnp.where(starts + 1 < regions * RB, counts, jnp.minimum(counts, 1))
    facts = jnp.stack([(starts - region * RB).astype(F32), weights, last.astype(F32)])
    facts = lax.all_gather(facts, "src", axis=0)
    rows = jnp.tile(facts[:, :2], (1, 1, 2))
    rows = jnp.pad(rows, ((0, 0), (0, 6), (0, 0)))
    live = (jnp.arange(2, dtype=F32)[None, None, :] < facts[:, 2, :, None]).astype(F32)
    live = jnp.broadcast_to(live.reshape(peers, slots * 2, 1), (peers, slots * 2, 2 * BLOCK))

    edge = 2 * BLOCK
    size = start_block.shape[1]
    x_left = shifted(start_block[:, size - edge :], 1)
    x_right = shifted(start_block[:, :edge], -1)

    band = None
    for k in range(peers):
        at = lax.rem(me + peers - k, peers)
        band = build(
            chunks[k],
            lax.dynamic_index_in_dim(live, at, 0, keepdims=False),
            lax.dynamic_index_in_dim(rows, at, 0, keepdims=False),
            band,
        )
    left_band = shifted(band[RB * 128 - 192 :], 1)
    right_band = shifted(band[:BLOCK], -1)
    z, grams = apply_twice(band, left_band, right_band, start_block, x_left, x_right)
    grams = lax.all_gather(grams, "blk", axis=0)
    return finish(grams, z, 2.0 * size * regions)


def solution(mesh):
    placed = (
        P(("groups", "src", "blk"), None, None),
        P(("groups", "src", "blk")),
        P(("groups", "src", "blk")),
        P(("groups", "src", "blk")),
        P("groups", "blk", None),
    )
    return jax.shard_map(
        per_device, mesh=mesh, in_specs=placed, out_specs=P("groups", "blk", None), check_vma=False
    )
```

time: 624 us -> 113 us (0.18)
  waiting for transfers between devices: 324 us -> 2.48 us
  other arithmetic: 225 us -> 1.52 us
  Pallas kernels: 0 us -> 56.8 us
  blocking collectives: 0 us -> 34.3 us
  local copies, waits for them, and re-layouts: 32.8 us -> 2.57 us
  between operations: 13.4 us -> 0.28 us
  matrix products: 11.9 us -> 0 us
    psum x2 -> x0, waiting for transfers between devices: 168 us -> none  [normalize(): gram_sum = lax.psum(gram_matrix(product), ('src', 'blk'))]
    scatter-add x33 -> x0, other arithmetic: 111 us -> none  [the longest x32 111 us: one_group(): totals[diag_slot] = totals[diag_slot].at[block_at[:, row_part]].add(jnp.c...]
    all_gather x2 -> x0, waiting for transfers between devices: 95.6 us -> none  [normalize(): lax.all_gather(finish(product, gram_sum, row_total), 'src', axis=1, tiled...]
    pallas_call x0 -> x6, Pallas kernels: none -> 56.8 us  [the longest x1 21.5 us: finish(): pl.pallas_call(partial(finish_kernel, total_rows), out_shape=jax.ShapeDty...]
    reduce_scatter x1 -> x0, waiting for transfers between devices: 53.5 us -> none  [build_tiles(): lax.psum_scatter(band_rows, 'src', scatter_dimension=0, tiled=True)]
    another operation x15 -> x0, other arithmetic: 47.5 us -> none  [the longest x6 24.8 us: finish(): factor = jnp.linalg.cholesky(gram_sum / row_total)]
    all_gather x0 -> x2, blocking collectives: none -> 34.3 us  [the longest x1 25.7 us: per_device(): facts = lax.all_gather(facts, 'src', axis=0)]
    concatenate x33 -> x0, other arithmetic: 31.7 us -> none  [the longest x32 31.6 us: one_group(): jnp.concatenate([real_part, imag_part], axis=2)]
  transfers between devices with their start and end apart: 10 -> 7, of which waited for: 7 -> 2; matrix products, arithmetic and copies ran while one was open for 1% -> 3% of each run, Pallas kernels for 0% -> 11%
where the time goes in v1:
time: 113 us
  Pallas kernels  56.8 us (50%)
  blocking collectives  34.3 us (30%)
  starting transfers between devices  15 us (13%)
  local copies, waits for them, and re-layouts  2.57 us (2%)
  waiting for transfers between devices  2.48 us (2%)
  other arithmetic  1.52 us (1%)
    all_gather x1, blocking collectives, per_device(): facts = lax.all_gather(facts, 'src', axis=0)  25.7 us
    pallas_call x1, Pallas kernels, finish(): pl.pallas_call(partial(finish_kernel, total_rows), out_shape=jax.ShapeDty...  21.5 us
    pallas_call x1, Pallas kernels, apply_twice(): pl.pallas_call(apply_kernel, out_shape=(jax.ShapeDtypeStruct((rows, 256),...  18.5 us
    pallas_call x4, Pallas kernels, build(): pl.pallas_call(partial(build_kernel, before is not None), out_shape=jax.S...  16.7 us
    all_gather x1, blocking collectives, per_device(): grams = lax.all_gather(grams, 'blk', axis=0)  8.61 us
    ppermute x4, starting transfers between devices, shifted(): return lax.ppermute(x, 'blk', pairs)  8.04 us
    ppermute x3, starting transfers between devices, per_device(): lax.ppermute(own, 'src', [(i, (i + k) % peers) for i in range(peers)])  6.96 us
    ppermute x4, waiting for transfers between devices, shifted(): return lax.ppermute(x, 'blk', pairs)  2.47 us
  transfers between devices with their start and end apart: 7, of which 2 were waited for; matrix products, arithmetic and copies ran while one was open for 3% of the time, Pallas kernels for 11%

profile of v1, /device:TPU:0, one launch (start us, length us, event | category | flops | bytes accessed | tf_op | source)
XLA Modules:
  0.0 112.9 jit_solution(6061149772000347610)
XLA Ops:
  0.0 3.0 %collective-permute-start.2 = (f32[512,128]{1,0:T(8,128)}, f32[512,128]{1,0:T(8,128)S(1)}, u32[]{:S(2)}, u32[]{:S(2)}) collective-permute-start(f32[512,128]{1,0:T(8,128)} %bitcast.18), channel_id=1, source_target_pairs={{0,4},{4,8},{8,12},{12,0},{1,5},{5,9},{9,13},{13,1},{2,6},{6,10},{... | collective-permute-start | bytes 786440 | tf_op jit(solution)/shard_map/ppermute | solution.py:325
  3.0 2.6 %collective-permute-start.1 = (f32[512,128]{1,0:T(8,128)}, f32[512,128]{1,0:T(8,128)S(1)}, u32[]{:S(2)}, u32[]{:S(2)}) collective-permute-start(f32[512,128]{1,0:T(8,128)} %bitcast.19), channel_id=1, source_target_pairs={{0,8},{4,12},{8,0},{12,4},{1,9},{5,13},{9,1},{13,5},{2,10},{6,14},... | collective-permute-start | bytes 786440 | tf_op jit(solution)/shard_map/ppermute | solution.py:325
  5.6 1.3 %collective-permute-start = (f32[512,128]{1,0:T(8,128)}, f32[512,128]{1,0:T(8,128)S(1)}, u32[]{:S(2)}, u32[]{:S(2)}) collective-permute-start(f32[512,128]{1,0:T(8,128)} %bitcast.20), channel_id=1, source_target_pairs={{0,12},{4,0},{8,4},{12,8},{1,13},{5,1},{9,5},{13,9},{2,14},{6,2},{... | collective-permute-start | bytes 786440 | tf_op jit(solution)/shard_map/ppermute | solution.py:325
  7.0 0.7 subtract_convert_fusion
  7.7 0.7 maximum_bitcast_fusion
  8.4 25.7 %all-gather.2 = f32[4,3,256]{2,1,0:T(4,128)S(1)} all-gather(f32[1,3,256]{2,1,0:T(4,128)S(1)} %maximum_bitcast_fusion), channel_id=2, replica_groups=mesh['groups'=2,'src'=4,'blk'=4] {'src'}, dimensions={0}, use_global_device_ids=true | all-gather | bytes 15360 | tf_op jit(solution)/shard_map/all_gather | solution.py:329
  34.0 0.1 copy.12
  34.2 0.1 lt.53
  34.4 0.1 lt.58
  34.5 0.1 compare_convert_fusion
  34.6 0.6 dynamic-slice_reduce_fusion
  35.3 0.1 broadcast_in_dim.27.refs_1_
  35.4 0.0 copy-start.1
  35.4 0.9 copy-done.1
  36.4 4.2 %band_terms.4.refs_3_ = f32[4096,256]{1,0:T(8,128)S(1)} custom-call(f32[512,128]{1,0:T(8,128)S(1)} %bitcast.21, f32[512,128]{1,0:T(8,128)S(1)} %broadcast_in_dim.27.refs_1_, f32[8,512]{1,0:T(8,128)S(1)} %get-tuple-element.15.refs_2_), custom_call_target="tpu_custom_call" | custom-call | flops 3221225472 | bytes 10485760 | tf_op jit(solution)/shard_map/band_terms/pallas_call | solution.py:81
  40.6 0.0 collective-permute-done.2.refs_0_
  40.6 0.1 broadcast_in_dim.25.refs_1_
  40.7 4.2 %band_terms.5.refs_3_ = f32[4096,256]{1,0:T(8,128)S(1)} custom-call(f32[512,128]{1,0:T(8,128)S(1)} %collective-permute-done.2.refs_0_, f32[512,128]{1,0:T(8,128)S(1)} %broadcast_in_dim.25.refs_1_, f32[8,512]{1,0:T(8,128)S(1)} %get-tuple-element.17.refs_2_, f32[4096,256]{1,0:T(8,128)S(1)} %band_terms.4.refs_3_), custom_call_target="tpu_custom_call", output_to_operand_aliasing={{}: (3, {})} | custom-call | flops 3221225472 | bytes 10485760 | tf_op jit(solution)/shard_map/band_terms/pallas_call | solution.py:81
  44.9 0.0 collective-permute-done.1.refs_0_
  44.9 0.1 broadcast_in_dim.23.refs_1_
  45.1 4.2 %band_terms.6.refs_3_ = f32[4096,256]{1,0:T(8,128)S(1)} custom-call(f32[512,128]{1,0:T(8,128)S(1)} %collective-permute-done.1.refs_0_, f32[512,128]{1,0:T(8,128)S(1)} %broadcast_in_dim.23.refs_1_, f32[8,512]{1,0:T(8,128)S(1)} %get-tuple-element.16.refs_2_, f32[4096,256]{1,0:T(8,128)S(1)} %band_terms.5.refs_3_), custom_call_target="tpu_custom_call", output_to_operand_aliasing={{}: (3, {})} | custom-call | flops 3221225472 | bytes 10485760 | tf_op jit(solution)/shard_map/band_terms/pallas_call | solution.py:81
  49.3 0.0 collective-permute-done.refs_0_
  49.3 0.1 broadcast_in_dim.21.refs_1_
  49.4 0.0 copy-start
  49.4 4.2 %band_terms.7.band = f32[4096,256]{1,0:T(8,128)S(1)} custom-call(f32[512,128]{1,0:T(8,128)S(1)} %collective-permute-done.refs_0_, f32[512,128]{1,0:T(8,128)S(1)} %broadcast_in_dim.21.refs_1_, f32[8,512]{1,0:T(8,128)S(1)} %get-tuple-element.18.refs_2_, f32[4096,256]{1,0:T(8,128)S(1)} %band_terms.6.refs_3_), custom_call_target="tpu_custom_call", output_to_operand_aliasing={{}: (3, {})} | custom-call | flops 3221225472 | bytes 10485760 | tf_op jit(solution)/shard_map/band_terms/pallas_call | solution.py:81
  53.6 1.3 %collective-permute-start.3 = (f32[192,256]{1,0:T(8,128)S(1)}, f32[192,256]{1,0:T(8,128)S(1)}, u32[]{:S(2)}, u32[]{:S(2)}) collective-permute-start(f32[192,256]{1,0:T(8,128)S(1)} %slice.26), channel_id=1, source_target_pairs={{0,1},{1,2},{2,3},{4,5},{5,6},{6,7},{8,9},{9,10},{10,11},{12,13},{... | collective-permute-start | bytes 589832 | tf_op jit(solution)/shard_map/ppermute | solution.py:312
  54.9 0.0 copy-done
  55.0 4.2 %collective-permute-start.5 = (f32[2,128,128]{2,1,0:T(8,128)S(1)}, f32[2,128,128]{2,1,0:T(8,128)S(1)}, u32[]{:S(2)}, u32[]{:S(2)}) collective-permute-start(f32[2,128,128]{2,1,0:T(8,128)S(1)} %get-tuple-element.14), channel_id=1, source_target_pairs={{0,1},{1,2},{2,3},{4,5},{5,6},{6,7},{8,9},{9,10},{10,11},{12,13},{... | collective-permute-start | bytes 393224 | tf_op jit(solution)/shard_map/ppermute | solution.py:312
  59.1 1.3 %collective-permute-start.6 = (f32[2,128,128]{2,1,0:T(8,128)S(1)}, f32[2,128,128]{2,1,0:T(8,128)S(1)}, u32[]{:S(2)}, u32[]{:S(2)}) collective-permute-start(f32[2,128,128]{2,1,0:T(8,128)S(1)} %get-tuple-element.13), channel_id=1, source_target_pairs={{1,0},{2,1},{3,2},{5,4},{6,5},{7,6},{9,8},{10,9},{11,10},{13,12},{... | collective-permute-start | bytes 393224 | tf_op jit(solution)/shard_map/ppermute | solution.py:312
  60.5 1.3 %collective-permute-start.4 = (f32[64,256]{1,0:T(8,128)S(1)}, f32[64,256]{1,0:T(8,128)S(1)}, u32[]{:S(2)}, u32[]{:S(2)}) collective-permute-start(f32[64,256]{1,0:T(8,128)S(1)} %slice.27), channel_id=1, source_target_pairs={{1,0},{2,1},{3,2},{5,4},{6,5},{7,6},{9,8},{10,9},{11,10},{13,12},{... | collective-permute-start | bytes 196616 | tf_op jit(solution)/shard_map/ppermute | solution.py:312
  61.8 0.0 collective-permute-done.5.x_left
  61.8 0.6 collective-permute-done.6.x_right
  62.4 1.8 %collective-permute-done.4.right_band = f32[64,256]{1,0:T(8,128)S(1)} collective-permute-done((f32[64,256]{1,0:T(8,128)S(1)}, f32[64,256]{1,0:T(8,128)S(1)}, u32[]{:S(2)}, u32[]{:S(2)}) %collective-permute-start.4) | collective-permute-done | bytes 65568 | tf_op jit(solution)/shard_map/ppermute | solution.py:312
  64.2 0.0 collective-permute-done.3.left_band
  64.2 18.5 %apply_twice.1 = (f32[2048,256]{1,0:T(8,128)S(1)}, f32[264,128]{1,0:T(8,128)S(1)}) custom-call(f32[4096,256]{1,0:T(8,128)S(1)} %band_terms.7.band, f32[192,256]{1,0:T(8,128)S(1)} %collective-permute-done.3.left_band, f32[64,256]{1,0:T(8,128)S(1)} %collective-permute-done.4.right_band, f32[2,2048,128]{2,1,0:T(8,128)S(1)} %copy-done, ...), custom_call_target="tpu_custom_call" | custom-call | flops 3221225472 | bytes 12582912 | tf_op jit(solution)/shard_map/apply_twice/pallas_call | solution.py:200
  82.8 8.6 %all-gather.1 = f32[1056,128]{1,0:T(8,128)S(1)} all-gather(f32[264,128]{1,0:T(8,128)S(1)} %get-tuple-element.7), channel_id=3, replica_groups=mesh['groups'=2,'src'=4,'blk'=4] {'blk'}, dimensions={0}, use_global_device_ids=true | all-gather | bytes 675840 | tf_op jit(solution)/shard_map/all_gather | solution.py:352
  91.4 21.5 %finish.1 = f32[2,2048,128]{2,1,0:T(8,128)} custom-call(f32[4,264,128]{2,1,0:T(8,128)S(1)} %bitcast.17, f32[2048,256]{1,0:T(8,128)S(1)} %get-tuple-element.8.z), custom_call_target="tpu_custom_call" | custom-call | tf_op jit(solution)/shard_map/finish/pallas_call | solution.py:298
  (9 shorter events, 0.1 us)
Async XLA Ops:
  0.0 40.6 %collective-permute-start.2 = (f32[512,128]{1,0:T(8,128)}, f32[512,128]{1,0:T(8,128)S(1)}, u32[]{:S(2)}, u32[]{:S(2)}) collective-permute-start(f32[512,128]{1,0:T(8,128)} %bitcast.18), channel_id=1, source_target_pairs={{0,4},{4,8},{8,12},{12,0},{1,5},{5,9},{9,13},{13,1},{2,6},{6,10},{... | collective-permute-start | bytes 786440 | tf_op jit(solution)/shard_map/ppermute | solution.py:325
  3.0 41.9 %collective-permute-start.1 = (f32[512,128]{1,0:T(8,128)}, f32[512,128]{1,0:T(8,128)S(1)}, u32[]{:S(2)}, u32[]{:S(2)}) collective-permute-start(f32[512,128]{1,0:T(8,128)} %bitcast.19), channel_id=1, source_target_pairs={{0,8},{4,12},{8,0},{12,4},{1,9},{5,13},{9,1},{13,5},{2,10},{6,14},... | collective-permute-start | bytes 786440 | tf_op jit(solution)/shard_map/ppermute | solution.py:325
  5.6 43.6 %collective-permute-start = (f32[512,128]{1,0:T(8,128)}, f32[512,128]{1,0:T(8,128)S(1)}, u32[]{:S(2)}, u32[]{:S(2)}) collective-permute-start(f32[512,128]{1,0:T(8,128)} %bitcast.20), channel_id=1, source_target_pairs={{0,12},{4,0},{8,4},{12,8},{1,13},{5,1},{9,5},{13,9},{2,14},{6,2},{... | collective-permute-start | bytes 786440 | tf_op jit(solution)/shard_map/ppermute | solution.py:325
  35.4 1.0 copy-start.1
  49.4 5.5 %copy-start = (f32[2,2048,128]{2,1,0:T(8,128)S(1)}, f32[2,2048,128]{2,1,0:T(8,128)}, u32[]{:S(2)}) copy-start(f32[2,2048,128]{2,1,0:T(8,128)} %x.3) | copy-start | bytes 6291460
  53.6 10.6 %collective-permute-start.3 = (f32[192,256]{1,0:T(8,128)S(1)}, f32[192,256]{1,0:T(8,128)S(1)}, u32[]{:S(2)}, u32[]{:S(2)}) collective-permute-start(f32[192,256]{1,0:T(8,128)S(1)} %slice.26), channel_id=1, source_target_pairs={{0,1},{1,2},{2,3},{4,5},{5,6},{6,7},{8,9},{9,10},{10,11},{12,13},{... | collective-permute-start | bytes 589832 | tf_op jit(solution)/shard_map/ppermute | solution.py:312
  55.0 6.8 %collective-permute-start.5 = (f32[2,128,128]{2,1,0:T(8,128)S(1)}, f32[2,128,128]{2,1,0:T(8,128)S(1)}, u32[]{:S(2)}, u32[]{:S(2)}) collective-permute-start(f32[2,128,128]{2,1,0:T(8,128)S(1)} %get-tuple-element.14), channel_id=1, source_target_pairs={{0,1},{1,2},{2,3},{4,5},{5,6},{6,7},{8,9},{9,10},{10,11},{12,13},{... | collective-permute-start | bytes 393224 | tf_op jit(solution)/shard_map/ppermute | solution.py:312
  59.1 3.2 %collective-permute-start.6 = (f32[2,128,128]{2,1,0:T(8,128)S(1)}, f32[2,128,128]{2,1,0:T(8,128)S(1)}, u32[]{:S(2)}, u32[]{:S(2)}) collective-permute-start(f32[2,128,128]{2,1,0:T(8,128)S(1)} %get-tuple-element.13), channel_id=1, source_target_pairs={{1,0},{2,1},{3,2},{5,4},{6,5},{7,6},{9,8},{10,9},{11,10},{13,12},{... | collective-permute-start | bytes 393224 | tf_op jit(solution)/shard_map/ppermute | solution.py:312
  60.5 3.8 %collective-permute-start.4 = (f32[64,256]{1,0:T(8,128)S(1)}, f32[64,256]{1,0:T(8,128)S(1)}, u32[]{:S(2)}, u32[]{:S(2)}) collective-permute-start(f32[64,256]{1,0:T(8,128)S(1)} %slice.27), channel_id=1, source_target_pairs={{1,0},{2,1},{3,2},{5,4},{6,5},{7,6},{9,8},{10,9},{11,10},{13,12},{... | collective-permute-start | bytes 196616 | tf_op jit(solution)/shard_map/ppermute | solution.py:312

commit v2 on v1

--- a/solution.py
+++ b/solution.py
@@ -35,17 +35,51 @@
     return jnp.dot(a, b, precision=HIGHEST, preferred_element_type=F32)
 
 
+def pack_kernel(total_blocks, pupils, starts, counts, weights, out):
+    tiles = starts.shape[0]
+    lane = lax.broadcasted_iota(jnp.int32, (128, 2 * BLOCK), 1)
+    start = starts[...]
+    root = jnp.sqrt(weights[...])
+    first_live = jnp.where(counts[...] > 0, root, 0.0)
+    second_live = jnp.where((counts[...] > 1) & (start + 1 < total_blocks), root, 0.0)
+    for t in range(tiles):
+        first_column = jnp.broadcast_to(first_live[t : t + 1, :], (128, 128)).T
+        second_column = jnp.broadcast_to(second_live[t : t + 1, :], (128, 128)).T
+        first = pupils[pl.ds(256 * t, 128, stride=2), :] * first_column
+        second = pupils[pl.ds(256 * t + 1, 128, stride=2), :] * second_column
+        real = jnp.where(lane < BLOCK, first, pltpu.roll(second, BLOCK, 1))
+        imag = jnp.where(lane < BLOCK, pltpu.roll(first, BLOCK, 1), second)
+        out[128 * t : 128 * t + 128, :] = real
+        out[128 * (tiles + t) : 128 * (tiles + t) + 128, :] = imag
+    out[256 * tiles :, :] = jnp.zeros((8, 128), F32)
+    out[256 * tiles : 256 * tiles + tiles, :] = lax.rem(start, RB).astype(F32)
+
+
+def pack(pupils, starts, counts, weights, total_blocks):
+    slots = pupils.shape[0]
+    return pl.pallas_call(
+        partial(pack_kernel, total_blocks),
+        out_shape=jax.ShapeDtypeStruct((2 * slots + 8, 128), F32),
+        in_specs=[VMEM] * 4,
+        out_specs=VMEM,
+        compiler_params=PARAMS,
+        name="pack",
+    )(
+        pupils.reshape(2 * slots, 128),
+        starts.reshape(-1, 128),
+        counts.reshape(-1, 128),
+        weights.reshape(-1, 128),
+    )
+
+
 def build_kernel(add, *refs):
     if add:
-        pupils, live, rows, before, out, lhs_hi, lhs_lo = refs
+        chunk, before, out, lhs_hi, lhs_lo = refs
     else:
-        pupils, live, rows, out, lhs_hi, lhs_lo = refs
-    count = pupils.shape[0] // 2
-    lane = lax.broadcasted_iota(jnp.int32, (count, 2 * BLOCK), 1)
-    first = pupils[pl.ds(0, count, stride=2), :] * live[pl.ds(0, count, stride=2), :]
-    second = pupils[pl.ds(1, count, stride=2), :] * live[pl.ds(1, count, stride=2), :]
-    real = jnp.where(lane < BLOCK, first, pltpu.roll(second, BLOCK, 1))
-    imag = jnp.where(lane < BLOCK, pltpu.roll(first, BLOCK, 1), second)
+        chunk, out, lhs_hi, lhs_lo = refs
+    count = (chunk.shape[0] - 8) // 2
+    real = chunk[:count, :]
+    imag = chunk[count : 2 * count, :]
     right = jnp.concatenate(
         [
             jnp.concatenate([real, -imag], axis=1),
@@ -54,11 +88,12 @@
         axis=0,
     )
     right_hi, right_lo = split(right)
-    left = jnp.concatenate([real.T, imag.T], axis=1) * rows[1:2, :]
+    left = jnp.concatenate([real.T, imag.T], axis=1)
     left_hi, left_lo = split(left)
     left_hi = left_hi.reshape(8, 16, 2 * count)
     left_lo = left_lo.reshape(8, 16, 2 * count)
-    place = jnp.broadcast_to(rows[0:1, :], (16, 2 * count))
+    places = [chunk[2 * count + t : 2 * count + t + 1, :] for t in range(count // 128)]
+    place = jnp.broadcast_to(jnp.concatenate(places + places, axis=1), (16, 2 * count))
 
     def one_group(g, carry):
         for j in range(GROUP):
@@ -75,16 +110,16 @@
     lax.fori_loop(0, RB // GROUP, one_group, 0)
 
 
-def build(pupils, live, rows, before):
-    count = pupils.shape[0] // 2
-    args = (pupils, live, rows) + (() if before is None else (before,))
+def build(chunk, before):
+    count = (chunk.shape[0] - 8) // 2
+    args = (chunk,) + (() if before is None else (before,))
     return pl.pallas_call(
         partial(build_kernel, before is not None),
         out_shape=jax.ShapeDtypeStruct((RB * 128, 256), F32),
         in_specs=[VMEM] * len(args),
         out_specs=VMEM,
         scratch_shapes=[pltpu.VMEM((GROUP * 128, 2 * count), BF16)] * 2,
-        input_output_aliases={} if before is None else {3: 0},
+        input_output_aliases={} if before is None else {1: 0},
         compiler_params=PARAMS,
         cost_estimate=pl.CostEstimate(
             flops=6 * RB * 128 * 2 * count * 256, bytes_accessed=10 << 20, transcendentals=0
@@ -313,39 +348,23 @@
 
 
 def per_device(pupils, starts, counts, weights, start_block):
-    region = lax.axis_index("blk")
-    me = lax.axis_index("src")
     regions = lax.axis_size("blk")
     peers = lax.axis_size("src")
-    slots = pupils.shape[0]
-
-    own = pupils.reshape(slots * 2, 2 * BLOCK)
+
+    own = pack(pupils, starts, counts, weights, regions * RB)
     chunks = [own]
     for k in range(1, peers):
         chunks.append(lax.ppermute(own, "src", [(i, (i + k) % peers) for i in range(peers)]))
-
-    last = jnp.where(starts + 1 < regions * RB, counts, jnp.minimum(counts, 1))
-    facts = jnp.stack([(starts - region * RB).astype(F32), weights, last.astype(F32)])
-    facts = lax.all_gather(facts, "src", axis=0)
-    rows = jnp.tile(facts[:, :2], (1, 1, 2))
-    rows = jnp.pad(rows, ((0, 0), (0, 6), (0, 0)))
-    live = (jnp.arange(2, dtype=F32)[None, None, :] < facts[:, 2, :, None]).astype(F32)
-    live = jnp.broadcast_to(live.reshape(peers, slots * 2, 1), (peers, slots * 2, 2 * BLOCK))
 
     edge = 2 * BLOCK
     size = start_block.shape[1]
     x_left = shifted(start_block[:, size - edge :], 1)
     x_right = shifted(start_block[:, :edge], -1)
 
-    band = None
-    for k in range(peers):
-        at = lax.rem(me + peers - k, peers)
-        band = build(
-            chunks[k],
-            lax.dynamic_index_in_dim(live, at, 0, keepdims=False),
-            lax.dynamic_index_in_dim(rows, at, 0, keepdims=False),
-            band,
-        )
+    band = build(own, None)
+    band, x_left, x_right = lax.optimization_barrier((band, x_left, x_right))
+    for k in range(1, peers):
+        band = build(chunks[k], band)
     left_band = shifted(band[RB * 128 - 192 :], 1)
     right_band = shifted(band[:BLOCK], -1)
     z, grams = apply_twice(band, left_band, right_band, start_block, x_left, x_right)

time: 113 us -> 92.7 us (0.82)
  the two profiles are of different devices: /device:TPU:0 before, /device:TPU:27 now
where the time goes in v2:
time: 92.7 us; the launch traced here: 92.5 us
  Pallas kernels  56.7 us (61%)
  starting transfers between devices  12.3 us (13%)
  blocking collectives  10.2 us (11%)
  waiting for transfers between devices  9.03 us (10%)
  local copies, waits for them, and re-layouts  4 us (4%)
    pallas_call x1, Pallas kernels, finish(): pl.pallas_call(partial(finish_kernel, total_rows), out_shape=jax.ShapeDty...  21.5 us
    pallas_call x1, Pallas kernels, apply_twice(): pl.pallas_call(apply_kernel, out_shape=(jax.ShapeDtypeStruct((rows, 256),...  18.6 us
    pallas_call x4, Pallas kernels, build(): pl.pallas_call(partial(build_kernel, before is not None), out_shape=jax.S...  16.4 us
    ppermute x4, starting transfers between devices, shifted(): return lax.ppermute(x, 'blk', pairs)  10.7 us
    all_gather x1, blocking collectives, per_device(): grams = lax.all_gather(grams, 'blk', axis=0)  10.2 us
    ppermute x3, waiting for transfers between devices, per_device(): lax.ppermute(own, 'src', [(i, (i + k) % peers) for i in range(peers)])  8.15 us
    unnamed x10, local copies, waits for them, and re-layouts  2.99 us
  transfers between devices with their start and end apart: 7, of which 2 were waited for; matrix products, arithmetic and copies ran while one was open for 1% of the time, Pallas kernels for 13%

profile of v2, /device:TPU:27, one launch (start us, length us, event | category | flops | bytes accessed | tf_op | source)
XLA Modules:
  0.0 92.5 jit_solution(5750302904002817330)
XLA Ops:
  0.0 0.0 copy-start
  0.0 0.9 %copy-done = f32[256,2,128]{2,1,0:T(2,128)S(1)} copy-done((f32[256,2,128]{2,1,0:T(2,128)S(1)}, f32[256,2,128]{2,1,0:T(2,128)}, u32[]{:S(2)}) %copy-start) | copy-done | bytes 262168
  1.0 0.0 copy-start.2
  1.0 0.7 copy-done.2
  1.6 0.0 copy-start.3
  1.6 0.7 copy-done.3
  2.3 0.0 copy-start.4
  2.3 0.7 copy-done.4
  3.0 0.2 pack.1.refs_0_
  3.2 0.1 collective-permute-start.2
  3.3 1.3 %collective-permute-start.1 = (f32[520,128]{1,0:T(8,128)S(1)}, f32[520,128]{1,0:T(8,128)S(1)}, u32[]{:S(2)}, u32[]{:S(2)}) collective-permute-start(f32[520,128]{1,0:T(8,128)S(1)} %pack.1.refs_0_), channel_id=1, source_target_pairs={{0,8},{4,12},{8,0},{12,4},{1,9},{5,13},{9,1},{13,5},{2,10},{6,14},... | collective-permute-start | bytes 798728 | tf_op jit(solution)/shard_map/ppermute | solution.py:357
  4.6 0.2 collective-permute-start
  4.8 1.0 %fusion = (f32[2,128,128]{2,1,0:T(8,128)S(1)}, f32[2,128,128]{2,1,0:T(8,128)S(1)}) fusion(f32[2,2048,128]{2,1,0:T(8,128)} %x.1), kind=kLoop, calls=%fused_computation | loop fusion | bytes 524288 | tf_op jit(solution)/shard_map/slice | solution.py:362
  5.8 1.3 %collective-permute-start.3 = (f32[2,128,128]{2,1,0:T(8,128)S(1)}, f32[2,128,128]{2,1,0:T(8,128)S(1)}, u32[]{:S(2)}, u32[]{:S(2)}) collective-permute-start(f32[2,128,128]{2,1,0:T(8,128)S(1)} %get-tuple-element.16), channel_id=1, source_target_pairs={{0,1},{1,2},{2,3},{4,5},{5,6},{6,7},{8,9},{9,10},{10,11},{12,13},{... | collective-permute-start | bytes 393224 | tf_op jit(solution)/shard_map/ppermute | solution.py:347
  7.1 4.1 %collective-permute-start.4 = (f32[2,128,128]{2,1,0:T(8,128)S(1)}, f32[2,128,128]{2,1,0:T(8,128)S(1)}, u32[]{:S(2)}, u32[]{:S(2)}) collective-permute-start(f32[2,128,128]{2,1,0:T(8,128)S(1)} %get-tuple-element.15), channel_id=1, source_target_pairs={{1,0},{2,1},{3,2},{5,4},{6,5},{7,6},{9,8},{10,9},{11,10},{13,12},{... | collective-permute-start | bytes 393224 | tf_op jit(solution)/shard_map/ppermute | solution.py:347
  11.1 4.1 %band_terms.4.refs_1_ = f32[4096,256]{1,0:T(8,128)S(1)} custom-call(f32[520,128]{1,0:T(8,128)S(1)} %pack.1.refs_0_), custom_call_target="tpu_custom_call" | custom-call | flops 3221225472 | bytes 10485760 | tf_op jit(solution)/shard_map/band_terms/pallas_call | solution.py:116
  15.2 0.0 collective-permute-done.3.x_left
  15.3 0.0 collective-permute-done.4.x_right
  15.3 0.0 collective-permute-done.2.refs_0_
  15.3 4.1 %band_terms.5.refs_1_ = f32[4096,256]{1,0:T(8,128)S(1)} custom-call(f32[520,128]{1,0:T(8,128)S(1)} %collective-permute-done.2.refs_0_, f32[4096,256]{1,0:T(8,128)S(1)} %band_terms.4.refs_1_), custom_call_target="tpu_custom_call", output_to_operand_aliasing={{}: (1, {})} | custom-call | flops 3221225472 | bytes 10485760 | tf_op jit(solution)/shard_map/band_terms/pallas_call | solution.py:116
  19.4 8.1 %collective-permute-done.1.refs_0_ = f32[520,128]{1,0:T(8,128)S(1)} collective-permute-done((f32[520,128]{1,0:T(8,128)S(1)}, f32[520,128]{1,0:T(8,128)S(1)}, u32[]{:S(2)}, u32[]{:S(2)}) %collective-permute-start.1) | collective-permute-done | bytes 266272 | tf_op jit(solution)/shard_map/ppermute | solution.py:357
  27.5 4.1 %band_terms.6.refs_1_ = f32[4096,256]{1,0:T(8,128)S(1)} custom-call(f32[520,128]{1,0:T(8,128)S(1)} %collective-permute-done.1.refs_0_, f32[4096,256]{1,0:T(8,128)S(1)} %band_terms.5.refs_1_), custom_call_target="tpu_custom_call", output_to_operand_aliasing={{}: (1, {})} | custom-call | flops 3221225472 | bytes 10485760 | tf_op jit(solution)/shard_map/band_terms/pallas_call | solution.py:116
  31.7 0.0 copy-start.1
  31.7 0.0 collective-permute-done.refs_0_
  31.7 4.1 %band_terms.7.band = f32[4096,256]{1,0:T(8,128)S(1)} custom-call(f32[520,128]{1,0:T(8,128)S(1)} %collective-permute-done.refs_0_, f32[4096,256]{1,0:T(8,128)S(1)} %band_terms.6.refs_1_), custom_call_target="tpu_custom_call", output_to_operand_aliasing={{}: (1, {})} | custom-call | flops 3221225472 | bytes 10485760 | tf_op jit(solution)/shard_map/band_terms/pallas_call | solution.py:116
  35.8 1.3 %collective-permute-start.5 = (f32[192,256]{1,0:T(8,128)S(1)}, f32[192,256]{1,0:T(8,128)S(1)}, u32[]{:S(2)}, u32[]{:S(2)}) collective-permute-start(f32[192,256]{1,0:T(8,128)S(1)} %slice.16), channel_id=1, source_target_pairs={{0,1},{1,2},{2,3},{4,5},{5,6},{6,7},{8,9},{9,10},{10,11},{12,13},{... | collective-permute-start | bytes 589832 | tf_op jit(solution)/shard_map/ppermute | solution.py:347
  37.1 4.1 %collective-permute-start.6 = (f32[64,256]{1,0:T(8,128)S(1)}, f32[64,256]{1,0:T(8,128)S(1)}, u32[]{:S(2)}, u32[]{:S(2)}) collective-permute-start(f32[64,256]{1,0:T(8,128)S(1)} %slice.17), channel_id=1, source_target_pairs={{1,0},{2,1},{3,2},{5,4},{6,5},{7,6},{9,8},{10,9},{11,10},{13,12},{... | collective-permute-start | bytes 196616 | tf_op jit(solution)/shard_map/ppermute | solution.py:347
  41.2 0.9 collective-permute-done.6.right_band
  42.1 0.0 collective-permute-done.5.left_band
  42.1 0.0 copy-done.1
  42.1 18.6 %apply_twice.1 = (f32[2048,256]{1,0:T(8,128)S(1)}, f32[264,128]{1,0:T(8,128)S(1)}) custom-call(f32[4096,256]{1,0:T(8,128)S(1)} %band_terms.7.band, f32[192,256]{1,0:T(8,128)S(1)} %collective-permute-done.5.left_band, f32[64,256]{1,0:T(8,128)S(1)} %collective-permute-done.6.right_band, f32[2,2048,128]{2,1,0:T(8,128)S(1)} %copy-done.1, ...), custom_call_target="tpu_custom_call" | custom-call | flops 3221225472 | bytes 12582912 | tf_op jit(solution)/shard_map/apply_twice/pallas_call | solution.py:235
  60.7 10.2 %all-gather = f32[1056,128]{1,0:T(8,128)S(1)} all-gather(f32[264,128]{1,0:T(8,128)S(1)} %get-tuple-element.13), channel_id=2, replica_groups=mesh['groups'=2,'src'=4,'blk'=4] {'blk'}, dimensions={0}, use_global_device_ids=true | all-gather | bytes 675840 | tf_op jit(solution)/shard_map/all_gather | solution.py:371
  70.9 21.5 %finish.1 = f32[2,2048,128]{2,1,0:T(8,128)} custom-call(f32[4,264,128]{2,1,0:T(8,128)S(1)} %bitcast.5, f32[2048,256]{1,0:T(8,128)S(1)} %get-tuple-element.14.z), custom_call_target="tpu_custom_call" | custom-call | tf_op jit(solution)/shard_map/finish/pallas_call | solution.py:333
  (2 shorter events, 0.0 us)
Async XLA Ops:
  0.0 0.9 %copy-start = (f32[256,2,128]{2,1,0:T(2,128)S(1)}, f32[256,2,128]{2,1,0:T(2,128)}, u32[]{:S(2)}) copy-start(f32[256,2,128]{2,1,0:T(2,128)} %param.5) | copy-start | bytes 786436
  1.0 0.7 copy-start.2
  1.6 0.7 copy-start.3
  2.3 0.7 copy-start.4
  3.2 12.0 %collective-permute-start.2 = (f32[520,128]{1,0:T(8,128)S(1)}, f32[520,128]{1,0:T(8,128)S(1)}, u32[]{:S(2)}, u32[]{:S(2)}) collective-permute-start(f32[520,128]{1,0:T(8,128)S(1)} %pack.1.refs_0_), channel_id=1, source_target_pairs={{0,4},{4,8},{8,12},{12,0},{1,5},{5,9},{9,13},{13,1},{2,6},{6,10},{... | collective-permute-start | bytes 798728 | tf_op jit(solution)/shard_map/ppermute | solution.py:357
  3.3 24.3 %collective-permute-start.1 = (f32[520,128]{1,0:T(8,128)S(1)}, f32[520,128]{1,0:T(8,128)S(1)}, u32[]{:S(2)}, u32[]{:S(2)}) collective-permute-start(f32[520,128]{1,0:T(8,128)S(1)} %pack.1.refs_0_), channel_id=1, source_target_pairs={{0,8},{4,12},{8,0},{12,4},{1,9},{5,13},{9,1},{13,5},{2,10},{6,14},... | collective-permute-start | bytes 798728 | tf_op jit(solution)/shard_map/ppermute | solution.py:357
  4.6 27.1 %collective-permute-start = (f32[520,128]{1,0:T(8,128)S(1)}, f32[520,128]{1,0:T(8,128)S(1)}, u32[]{:S(2)}, u32[]{:S(2)}) collective-permute-start(f32[520,128]{1,0:T(8,128)S(1)} %pack.1.refs_0_), channel_id=1, source_target_pairs={{0,12},{4,0},{8,4},{12,8},{1,13},{5,1},{9,5},{13,9},{2,14},{6,2},{... | collective-permute-start | bytes 798728 | tf_op jit(solution)/shard_map/ppermute | solution.py:357
  5.8 9.5 %collective-permute-start.3 = (f32[2,128,128]{2,1,0:T(8,128)S(1)}, f32[2,128,128]{2,1,0:T(8,128)S(1)}, u32[]{:S(2)}, u32[]{:S(2)}) collective-permute-start(f32[2,128,128]{2,1,0:T(8,128)S(1)} %get-tuple-element.16), channel_id=1, source_target_pairs={{0,1},{1,2},{2,3},{4,5},{5,6},{6,7},{8,9},{9,10},{10,11},{12,13},{... | collective-permute-start | bytes 393224 | tf_op jit(solution)/shard_map/ppermute | solution.py:347
  7.1 8.2 %collective-permute-start.4 = (f32[2,128,128]{2,1,0:T(8,128)S(1)}, f32[2,128,128]{2,1,0:T(8,128)S(1)}, u32[]{:S(2)}, u32[]{:S(2)}) collective-permute-start(f32[2,128,128]{2,1,0:T(8,128)S(1)} %get-tuple-element.15), channel_id=1, source_target_pairs={{1,0},{2,1},{3,2},{5,4},{6,5},{7,6},{9,8},{10,9},{11,10},{13,12},{... | collective-permute-start | bytes 393224 | tf_op jit(solution)/shard_map/ppermute | solution.py:347
  31.7 10.5 %copy-start.1 = (f32[2,2048,128]{2,1,0:T(8,128)S(1)}, f32[2,2048,128]{2,1,0:T(8,128)}, u32[]{:S(2)}) copy-start(f32[2,2048,128]{2,1,0:T(8,128)} %x.1) | copy-start | bytes 6291460
  35.8 6.3 %collective-permute-start.5 = (f32[192,256]{1,0:T(8,128)S(1)}, f32[192,256]{1,0:T(8,128)S(1)}, u32[]{:S(2)}, u32[]{:S(2)}) collective-permute-start(f32[192,256]{1,0:T(8,128)S(1)} %slice.16), channel_id=1, source_target_pairs={{0,1},{1,2},{2,3},{4,5},{5,6},{6,7},{8,9},{9,10},{10,11},{12,13},{... | collective-permute-start | bytes 589832 | tf_op jit(solution)/shard_map/ppermute | solution.py:347
  37.1 5.0 %collective-permute-start.6 = (f32[64,256]{1,0:T(8,128)S(1)}, f32[64,256]{1,0:T(8,128)S(1)}, u32[]{:S(2)}, u32[]{:S(2)}) collective-permute-start(f32[64,256]{1,0:T(8,128)S(1)} %slice.17), channel_id=1, source_target_pairs={{1,0},{2,1},{3,2},{5,4},{6,5},{7,6},{9,8},{10,9},{11,10},{13,12},{... | collective-permute-start | bytes 196616 | tf_op jit(solution)/shard_map/ppermute | solution.py:347

commit v3 on v2

--- a/solution.py
+++ b/solution.py
@@ -10,6 +10,8 @@
 BLOCK = 64
 RB = 32
 GROUP = 8
+UNROLL = 8
+OUTER = 64
 M = 128
 F32 = jnp.float32
 BF16 = jnp.bfloat16
@@ -35,7 +37,14 @@
     return jnp.dot(a, b, precision=HIGHEST, preferred_element_type=F32)
 
 
-def pack_kernel(total_blocks, pupils, starts, counts, weights, out):
+def pack_kernel(total_blocks, *refs):
+    sent, out, held, sems = refs[:4], refs[4], refs[5:9], refs[9]
+    copies = [pltpu.make_async_copy(sent[i], held[i], sems.at[i]) for i in range(4)]
+    for copy in copies:
+        copy.start()
+    for copy in copies:
+        copy.wait()
+    pupils, starts, counts, weights = held
     tiles = starts.shape[0]
     lane = lax.broadcasted_iota(jnp.int32, (128, 2 * BLOCK), 1)
     start = starts[...]
@@ -60,8 +69,15 @@
     return pl.pallas_call(
         partial(pack_kernel, total_blocks),
         out_shape=jax.ShapeDtypeStruct((2 * slots + 8, 128), F32),
-        in_specs=[VMEM] * 4,
+        in_specs=[pl.BlockSpec(memory_space=pltpu.HBM)] * 4,
         out_specs=VMEM,
+        scratch_shapes=[
+            pltpu.VMEM((2 * slots, 128), F32),
+            pltpu.VMEM((slots // 128, 128), jnp.int32),
+            pltpu.VMEM((slots // 128, 128), jnp.int32),
+            pltpu.VMEM((slots // 128, 128), F32),
+            pltpu.SemaphoreType.DMA((4,)),
+        ],
         compiler_params=PARAMS,
         name="pack",
     )(
@@ -193,7 +209,7 @@
         p[pl.ds(pl.multiple_of(e * BLOCK, BLOCK), BLOCK), :] = both[:BLOCK] + carry
         return both[BLOCK:]
 
-    lax.fori_loop(0, pairs, first, jnp.zeros((BLOCK, 256), F32))
+    lax.fori_loop(0, pairs, first, jnp.zeros((BLOCK, 256), F32), unroll=UNROLL)
 
     def prepare_again(i, carry):
         at = pl.ds(pl.multiple_of(i * 128, 128), 128)
@@ -203,14 +219,14 @@
     lax.fori_loop(0, (RB + 4) // 2, prepare_again, 0)
     rows = RB * BLOCK
     inner = pl.ds(2 * BLOCK, rows)
-    grams[0:M, :] = gram_of(x_hi[inner, :], x_lo[inner, :])
+    gram_1 = gram_of(x_hi[inner, :], x_lo[inner, :])
 
     def second(e, carry):
         both = pair(e)
         z[pl.ds(pl.multiple_of((e - 2) * BLOCK, BLOCK), BLOCK), :] = both[:BLOCK] + carry
         return both[BLOCK:]
 
-    lax.fori_loop(2, RB + 2, second, pair(1)[BLOCK:])
+    lax.fori_loop(2, RB + 2, second, pair(1)[BLOCK:], unroll=UNROLL)
 
     top = jnp.max(jnp.abs(z[...]), axis=0, keepdims=True)
     top = jnp.maximum(top[:, :M], top[:, M:])
@@ -225,8 +241,12 @@
         return carry
 
     lax.fori_loop(0, rows // 128, prepare_z, 0)
-    grams[M : 2 * M, :] = gram_of(p_hi[...], p_lo[...])
-    grams[2 * M :, :] = jnp.broadcast_to(top, (8, M))
+    gram_2 = gram_of(p_hi[...], p_lo[...])
+    row = lax.broadcasted_iota(jnp.int32, (M, M), 0)
+    col = lax.broadcasted_iota(jnp.int32, (M, M), 1)
+    grams[:M, :] = jnp.where(row >= col, gram_1, gram_2)
+    diagonal = jnp.sum(jnp.where(row == col, gram_2, 0.0), axis=0, keepdims=True)
+    grams[M:, :] = jnp.concatenate([diagonal, top, jnp.zeros((6, M), F32)], axis=0)
 
 
 def apply_twice(band, left_band, right_band, x, x_left, x_right):
@@ -236,7 +256,7 @@
         apply_kernel,
         out_shape=(
             jax.ShapeDtypeStruct((rows, 256), F32),
-            jax.ShapeDtypeStruct((2 * M + 8, M), F32),
+            jax.ShapeDtypeStruct((M + 8, M), F32),
         ),
         in_specs=[VMEM] * 6,
         out_specs=(VMEM, VMEM),
@@ -258,31 +278,62 @@
     work[:, :M] = a
     work[:, M:] = jnp.where(row == col, 1.0, 0.0)
     sub = lax.broadcasted_iota(jnp.int32, (8, M), 0)
-    sub2 = lax.broadcasted_iota(jnp.int32, (8, 2 * M), 0)
-    for p in range(M // 8):
-        at = slice(8 * p, 8 * p + 8)
-        panel = work[at, :]
-        cols = [
-            jnp.broadcast_to(panel[:, 8 * p + k : 8 * p + k + 1], (8, M)) for k in range(8)
-        ]
-        scales = jnp.zeros((8, M), F32)
-        for j in range(8):
-            pivot = jnp.broadcast_to(cols[j][j : j + 1, :], (8, M))
-            root = lax.rsqrt(pivot)
-            scales = jnp.where(sub == j, root, scales)
-            if j < 7:
-                part = jnp.where(sub > j, cols[j] * (root * root), 0.0)
-                for k in range(j + 1, 8):
-                    cols[k] = cols[k] - part * cols[k][j : j + 1, :]
-                panel = panel - jnp.concatenate([part, part], axis=1) * panel[j : j + 1, :]
-        panel = panel * jnp.concatenate([scales, scales], axis=1)
-        work[at, :] = panel
-        if p < M // 8 - 1:
+    groups = OUTER // 8
+
+    def line(x, j):
+        return x[j : j + 1, :]
+
+    def wide(x, j):
+        return jnp.broadcast_to(line(x, j), (8, M))
+
+    for top in range(0, M, OUTER):
+        left = [work[top + 8 * g : top + 8 * g + 8, :M] for g in range(groups)]
+        right = [work[top + 8 * g : top + 8 * g + 8, M:] for g in range(groups)]
+        for q in range(groups):
+            at = top + 8 * q
+            cols = {
+                g: [jnp.broadcast_to(left[g][:, at + k : at + k + 1], (8, M)) for k in range(8)]
+                for g in range(q, groups)
+            }
+            scales = jnp.zeros((8, M), F32)
+            for j in range(0, 8, 2):
+                a0, a1, a2 = wide(cols[q][j], j), wide(cols[q][j], j + 1), wide(cols[q][j + 1], j + 1)
+                det = a0 * a2 - a1 * a1
+                inverse = pltpu.reciprocal(det, approx=False)
+                root = lax.rsqrt(a0)
+                ratio = a1 * (root * root)
+                scales = jnp.where(sub == j, root, scales)
+                scales = jnp.where(sub == j + 1, lax.rsqrt(det) * (a0 * root), scales)
+                row_0 = [line(cols[q][k], j) for k in range(8)]
+                row_1 = [line(cols[q][k], j + 1) for k in range(8)]
+                left_0, left_1 = line(left[q], j), line(left[q], j + 1)
+                right_0, right_1 = line(right[q], j), line(right[q], j + 1)
+                for g in range(q, groups):
+                    c0, c1 = cols[g][j], cols[g][j + 1]
+                    y0 = a2 * c0 - a1 * c1
+                    y1 = a0 * c1 - a1 * c0
+                    if g == q:
+                        y0 = jnp.where(sub > j + 1, y0, 0.0)
+                        y1 = jnp.where(sub > j + 1, y1, 0.0)
+                    for k in range(j + 2, 8):
+                        cols[g][k] = cols[g][k] - (y0 * row_0[k] + y1 * row_1[k]) * inverse
+                    x0, x1 = y0 * inverse, y1 * inverse
+                    if g == q:
+                        x0 = jnp.where(sub == j + 1, ratio, x0)
+                    left[g] = left[g] - (x0 * left_0 + x1 * left_1)
+                    right[g] = right[g] - (x0 * right_0 + x1 * right_1)
+            left[q] = left[q] * scales
+            right[q] = right[q] * scales
+        for g in range(groups):
+            work[top + 8 * g : top + 8 * g + 8, :M] = left[g]
+            work[top + 8 * g : top + 8 * g + 8, M:] = right[g]
+        if top + OUTER < M:
+            panel = work[top : top + OUTER, :]
             update = lax.dot_general(
                 panel[:, :M], panel, (((0,), (0,)), ((), ())),
                 precision=HIGHEST, preferred_element_type=F32,
             )
-            work[8 * p + 8 :, :] = work[8 * p + 8 :, :] - update[8 * p + 8 :, :]
+            work[top + OUTER :, :] = work[top + OUTER :, :] - update[top + OUTER :, :]
     return work[:, M:]
 
 
@@ -295,17 +346,25 @@
     def as_column(v):
         return jnp.sum(eye * v, axis=1, keepdims=True)
 
-    gram = grams[0, :M, :]
+    def row_of(x):
+        return jnp.sum(eye * x, axis=0, keepdims=True)
+
+    total = grams[0, :M, :]
     for r in range(1, peers):
-        gram = gram + grams[r, :M, :]
-    norm = lax.rsqrt(jnp.sum(eye * gram, axis=0, keepdims=True))
+        total = total + grams[r, :M, :]
+    gram = jnp.where(row >= col, total, total.T)
+    norm = lax.rsqrt(row_of(gram))
     inverse = inverse_factor(gram * norm * as_column(norm), work)
-    gram = jnp.zeros((M, M), F32)
+    total = jnp.zeros((M, M), F32)
     for r in range(peers):
-        size = norm * grams[r, 2 * M : 2 * M + 1, :]
-        gram = gram + grams[r, M : 2 * M, :] * size * as_column(size)
+        size = norm * grams[r, M + 1 : M + 2, :]
+        second = jnp.where(row == col, grams[r, M : M + 1, :], grams[r, :M, :])
+        total = total + second * size * as_column(size)
+    gram = jnp.where(row <= col, total, total.T)
     gram = dot_f32(dot_f32(inverse, gram), inverse.T)
-    inverse = dot_f32(inverse_factor(gram, work), inverse)
+    scale = lax.rsqrt(row_of(gram))
+    second = inverse_factor(gram * scale * as_column(scale), work) * scale
+    inverse = dot_f32(second, inverse)
     change = (inverse * (norm * (total_rows**0.5))).T
     c_hi, c_lo = split(change)
     right = jnp.concatenate(
@@ -326,7 +385,7 @@
             out[part, at, :] = both[:, :M] + both[:, M:]
         return carry
 
-    lax.fori_loop(0, z.shape[0] // step, rows_of, 0)
+    lax.fori_loop(0, z.shape[0] // step, rows_of, 0, unroll=2)
 
 
 def finish(grams, z, total_rows):

time: 92.7 us -> 72.3 us (0.78)
  Pallas kernels: 56.7 us -> 37.7 us
  blocking collectives: 10.2 us -> 8.81 us
    pallas_call x1, Pallas kernels: 21.5 us -> 11.6 us  [finish(): pl.pallas_call(partial(finish_kernel, total_rows), out_shape=jax.ShapeDty...]
    pallas_call x1, Pallas kernels: 18.6 us -> 9.36 us  [apply_twice(): pl.pallas_call(apply_kernel, out_shape=(jax.ShapeDtypeStruct((rows, 256),...]
    all_gather x1, blocking collectives: 10.2 us -> 8.81 us  [per_device(): grams = lax.all_gather(grams, 'blk', axis=0)]
  transfers between devices with their start and end apart: 7 -> 7, of which waited for: 2 -> 2; matrix products, arithmetic and copies ran while one was open for 1% -> 1% of each run, Pallas kernels for 13% -> 17%
where the time goes in v3:
time: 72.3 us; the launch traced here: 72 us
  Pallas kernels  37.7 us (52%)
  starting transfers between devices  12.3 us (17%)
  waiting for transfers between devices  9.02 us (12%)
  blocking collectives  8.81 us (12%)
  local copies, waits for them, and re-layouts  4 us (6%)
    pallas_call x4, Pallas kernels, build(): pl.pallas_call(partial(build_kernel, before is not None), out_shape=jax.S...  16.4 us
    pallas_call x1, Pallas kernels, finish(): pl.pallas_call(partial(finish_kernel, total_rows), out_shape=jax.ShapeDty...  11.6 us
    ppermute x4, starting transfers between devices, shifted(): return lax.ppermute(x, 'blk', pairs)  10.7 us
    pallas_call x1, Pallas kernels, apply_twice(): pl.pallas_call(apply_kernel, out_shape=(jax.ShapeDtypeStruct((rows, 256),...  9.36 us
    all_gather x1, blocking collectives, per_device(): grams = lax.all_gather(grams, 'blk', axis=0)  8.81 us
    ppermute x3, waiting for transfers between devices, per_device(): lax.ppermute(own, 'src', [(i, (i + k) % peers) for i in range(peers)])  8.13 us
    unnamed x10, local copies, waits for them, and re-layouts  2.99 us
    ppermute x3, starting transfers between devices, per_device(): lax.ppermute(own, 'src', [(i, (i + k) % peers) for i in range(peers)])  1.57 us
  transfers between devices with their start and end apart: 7, of which 2 were waited for; matrix products, arithmetic and copies ran while one was open for 1% of the time, Pallas kernels for 17%

profile of v3, /device:TPU:27, one launch (start us, length us, event | category | flops | bytes accessed | tf_op | source)
XLA Modules:
  0.0 72.0 jit_solution(2605013012872388725)
XLA Ops:
  0.0 0.0 copy-start
  0.0 0.9 %copy-done = f32[256,2,128]{2,1,0:T(2,128)S(1)} copy-done((f32[256,2,128]{2,1,0:T(2,128)S(1)}, f32[256,2,128]{2,1,0:T(2,128)}, u32[]{:S(2)}) %copy-start) | copy-done | bytes 262168
  1.0 0.0 copy-start.2
  1.0 0.7 copy-done.2
  1.6 0.0 copy-start.3
  1.6 0.7 copy-done.3
  2.3 0.0 copy-start.4
  2.3 0.7 copy-done.4
  3.0 0.3 pack.1.refs_0_
  3.3 0.1 collective-permute-start.2
  3.4 1.3 %collective-permute-start.1 = (f32[520,128]{1,0:T(8,128)S(1)}, f32[520,128]{1,0:T(8,128)S(1)}, u32[]{:S(2)}, u32[]{:S(2)}) collective-permute-start(f32[520,128]{1,0:T(8,128)S(1)} %pack.1.refs_0_), channel_id=1, source_target_pairs={{0,8},{4,12},{8,0},{12,4},{1,9},{5,13},{9,1},{13,5},{2,10},{6,14},... | collective-permute-start | bytes 798728 | tf_op jit(solution)/shard_map/ppermute | solution.py:416
  4.7 0.2 collective-permute-start
  4.9 1.0 %fusion = (f32[2,128,128]{2,1,0:T(8,128)S(1)}, f32[2,128,128]{2,1,0:T(8,128)S(1)}) fusion(f32[2,2048,128]{2,1,0:T(8,128)} %x.1), kind=kLoop, calls=%fused_computation | loop fusion | bytes 524288 | tf_op jit(solution)/shard_map/slice | solution.py:421
  5.9 1.3 %collective-permute-start.3 = (f32[2,128,128]{2,1,0:T(8,128)S(1)}, f32[2,128,128]{2,1,0:T(8,128)S(1)}, u32[]{:S(2)}, u32[]{:S(2)}) collective-permute-start(f32[2,128,128]{2,1,0:T(8,128)S(1)} %get-tuple-element.16), channel_id=1, source_target_pairs={{0,1},{1,2},{2,3},{4,5},{5,6},{6,7},{8,9},{9,10},{10,11},{12,13},{... | collective-permute-start | bytes 393224 | tf_op jit(solution)/shard_map/ppermute | solution.py:406
  7.2 4.1 %collective-permute-start.4 = (f32[2,128,128]{2,1,0:T(8,128)S(1)}, f32[2,128,128]{2,1,0:T(8,128)S(1)}, u32[]{:S(2)}, u32[]{:S(2)}) collective-permute-start(f32[2,128,128]{2,1,0:T(8,128)S(1)} %get-tuple-element.15), channel_id=1, source_target_pairs={{1,0},{2,1},{3,2},{5,4},{6,5},{7,6},{9,8},{10,9},{11,10},{13,12},{... | collective-permute-start | bytes 393224 | tf_op jit(solution)/shard_map/ppermute | solution.py:406
  11.2 4.1 %band_terms.4.refs_1_ = f32[4096,256]{1,0:T(8,128)S(1)} custom-call(f32[520,128]{1,0:T(8,128)S(1)} %pack.1.refs_0_), custom_call_target="tpu_custom_call" | custom-call | flops 3221225472 | bytes 10485760 | tf_op jit(solution)/shard_map/band_terms/pallas_call | solution.py:132
  15.3 0.0 collective-permute-done.3.x_left
  15.3 0.0 collective-permute-done.4.x_right
  15.3 0.0 collective-permute-done.2.refs_0_
  15.4 4.1 %band_terms.5.refs_1_ = f32[4096,256]{1,0:T(8,128)S(1)} custom-call(f32[520,128]{1,0:T(8,128)S(1)} %collective-permute-done.2.refs_0_, f32[4096,256]{1,0:T(8,128)S(1)} %band_terms.4.refs_1_), custom_call_target="tpu_custom_call", output_to_operand_aliasing={{}: (1, {})} | custom-call | flops 3221225472 | bytes 10485760 | tf_op jit(solution)/shard_map/band_terms/pallas_call | solution.py:132
  19.5 8.1 %collective-permute-done.1.refs_0_ = f32[520,128]{1,0:T(8,128)S(1)} collective-permute-done((f32[520,128]{1,0:T(8,128)S(1)}, f32[520,128]{1,0:T(8,128)S(1)}, u32[]{:S(2)}, u32[]{:S(2)}) %collective-permute-start.1) | collective-permute-done | bytes 266272 | tf_op jit(solution)/shard_map/ppermute | solution.py:416
  27.6 4.1 %band_terms.6.refs_1_ = f32[4096,256]{1,0:T(8,128)S(1)} custom-call(f32[520,128]{1,0:T(8,128)S(1)} %collective-permute-done.1.refs_0_, f32[4096,256]{1,0:T(8,128)S(1)} %band_terms.5.refs_1_), custom_call_target="tpu_custom_call", output_to_operand_aliasing={{}: (1, {})} | custom-call | flops 3221225472 | bytes 10485760 | tf_op jit(solution)/shard_map/band_terms/pallas_call | solution.py:132
  31.7 0.0 copy-start.1
  31.7 0.0 collective-permute-done.refs_0_
  31.8 4.1 %band_terms.7.band = f32[4096,256]{1,0:T(8,128)S(1)} custom-call(f32[520,128]{1,0:T(8,128)S(1)} %collective-permute-done.refs_0_, f32[4096,256]{1,0:T(8,128)S(1)} %band_terms.6.refs_1_), custom_call_target="tpu_custom_call", output_to_operand_aliasing={{}: (1, {})} | custom-call | flops 3221225472 | bytes 10485760 | tf_op jit(solution)/shard_map/band_terms/pallas_call | solution.py:132
  35.9 1.3 %collective-permute-start.5 = (f32[192,256]{1,0:T(8,128)S(1)}, f32[192,256]{1,0:T(8,128)S(1)}, u32[]{:S(2)}, u32[]{:S(2)}) collective-permute-start(f32[192,256]{1,0:T(8,128)S(1)} %slice.16), channel_id=1, source_target_pairs={{0,1},{1,2},{2,3},{4,5},{5,6},{6,7},{8,9},{9,10},{10,11},{12,13},{... | collective-permute-start | bytes 589832 | tf_op jit(solution)/shard_map/ppermute | solution.py:406
  37.2 4.1 %collective-permute-start.6 = (f32[64,256]{1,0:T(8,128)S(1)}, f32[64,256]{1,0:T(8,128)S(1)}, u32[]{:S(2)}, u32[]{:S(2)}) collective-permute-start(f32[64,256]{1,0:T(8,128)S(1)} %slice.17), channel_id=1, source_target_pairs={{1,0},{2,1},{3,2},{5,4},{6,5},{7,6},{9,8},{10,9},{11,10},{13,12},{... | collective-permute-start | bytes 196616 | tf_op jit(solution)/shard_map/ppermute | solution.py:406
  41.3 0.9 %collective-permute-done.6.right_band = f32[64,256]{1,0:T(8,128)S(1)} collective-permute-done((f32[64,256]{1,0:T(8,128)S(1)}, f32[64,256]{1,0:T(8,128)S(1)}, u32[]{:S(2)}, u32[]{:S(2)}) %collective-permute-start.6) | collective-permute-done | bytes 65568 | tf_op jit(solution)/shard_map/ppermute | solution.py:406
  42.2 0.0 collective-permute-done.5.left_band
  42.2 0.0 copy-done.1
  42.2 9.4 %apply_twice.1 = (f32[2048,256]{1,0:T(8,128)S(1)}, f32[136,128]{1,0:T(8,128)S(1)}) custom-call(f32[4096,256]{1,0:T(8,128)S(1)} %band_terms.7.band, f32[192,256]{1,0:T(8,128)S(1)} %collective-permute-done.5.left_band, f32[64,256]{1,0:T(8,128)S(1)} %collective-permute-done.6.right_band, f32[2,2048,128]{2,1,0:T(8,128)S(1)} %copy-done.1, ...), custom_call_target="tpu_custom_call" | custom-call | flops 3221225472 | bytes 12582912 | tf_op jit(solution)/shard_map/apply_twice/pallas_call | solution.py:255
  51.6 8.8 %all-gather = f32[544,128]{1,0:T(8,128)S(1)} all-gather(f32[136,128]{1,0:T(8,128)S(1)} %get-tuple-element.13), channel_id=2, replica_groups=mesh['groups'=2,'src'=4,'blk'=4] {'blk'}, dimensions={0}, use_global_device_ids=true | all-gather | bytes 348160 | tf_op jit(solution)/shard_map/all_gather | solution.py:430
  60.4 11.6 %finish.1 = f32[2,2048,128]{2,1,0:T(8,128)} custom-call(f32[4,136,128]{2,1,0:T(8,128)S(1)} %bitcast.5, f32[2048,256]{1,0:T(8,128)S(1)} %get-tuple-element.14.z), custom_call_target="tpu_custom_call" | custom-call | tf_op jit(solution)/shard_map/finish/pallas_call | solution.py:392
  (2 shorter events, 0.0 us)
Async XLA Ops:
  0.0 0.9 %copy-start = (f32[256,2,128]{2,1,0:T(2,128)S(1)}, f32[256,2,128]{2,1,0:T(2,128)}, u32[]{:S(2)}) copy-start(f32[256,2,128]{2,1,0:T(2,128)} %param.5) | copy-start | bytes 786436
  1.0 0.7 copy-start.2
  1.6 0.7 copy-start.3
  2.3 0.7 copy-start.4
  3.3 12.1 %collective-permute-start.2 = (f32[520,128]{1,0:T(8,128)S(1)}, f32[520,128]{1,0:T(8,128)S(1)}, u32[]{:S(2)}, u32[]{:S(2)}) collective-permute-start(f32[520,128]{1,0:T(8,128)S(1)} %pack.1.refs_0_), channel_id=1, source_target_pairs={{0,4},{4,8},{8,12},{12,0},{1,5},{5,9},{9,13},{13,1},{2,6},{6,10},{... | collective-permute-start | bytes 798728 | tf_op jit(solution)/shard_map/ppermute | solution.py:416
  3.4 24.3 %collective-permute-start.1 = (f32[520,128]{1,0:T(8,128)S(1)}, f32[520,128]{1,0:T(8,128)S(1)}, u32[]{:S(2)}, u32[]{:S(2)}) collective-permute-start(f32[520,128]{1,0:T(8,128)S(1)} %pack.1.refs_0_), channel_id=1, source_target_pairs={{0,8},{4,12},{8,0},{12,4},{1,9},{5,13},{9,1},{13,5},{2,10},{6,14},... | collective-permute-start | bytes 798728 | tf_op jit(solution)/shard_map/ppermute | solution.py:416
  4.7 27.0 %collective-permute-start = (f32[520,128]{1,0:T(8,128)S(1)}, f32[520,128]{1,0:T(8,128)S(1)}, u32[]{:S(2)}, u32[]{:S(2)}) collective-permute-start(f32[520,128]{1,0:T(8,128)S(1)} %pack.1.refs_0_), channel_id=1, source_target_pairs={{0,12},{4,0},{8,4},{12,8},{1,13},{5,1},{9,5},{13,9},{2,14},{6,2},{... | collective-permute-start | bytes 798728 | tf_op jit(solution)/shard_map/ppermute | solution.py:416
  5.9 9.5 %collective-permute-start.3 = (f32[2,128,128]{2,1,0:T(8,128)S(1)}, f32[2,128,128]{2,1,0:T(8,128)S(1)}, u32[]{:S(2)}, u32[]{:S(2)}) collective-permute-start(f32[2,128,128]{2,1,0:T(8,128)S(1)} %get-tuple-element.16), channel_id=1, source_target_pairs={{0,1},{1,2},{2,3},{4,5},{5,6},{6,7},{8,9},{9,10},{10,11},{12,13},{... | collective-permute-start | bytes 393224 | tf_op jit(solution)/shard_map/ppermute | solution.py:406
  7.2 8.2 %collective-permute-start.4 = (f32[2,128,128]{2,1,0:T(8,128)S(1)}, f32[2,128,128]{2,1,0:T(8,128)S(1)}, u32[]{:S(2)}, u32[]{:S(2)}) collective-permute-start(f32[2,128,128]{2,1,0:T(8,128)S(1)} %get-tuple-element.15), channel_id=1, source_target_pairs={{1,0},{2,1},{3,2},{5,4},{6,5},{7,6},{9,8},{10,9},{11,10},{13,12},{... | collective-permute-start | bytes 393224 | tf_op jit(solution)/shard_map/ppermute | solution.py:406
  31.7 10.5 %copy-start.1 = (f32[2,2048,128]{2,1,0:T(8,128)S(1)}, f32[2,2048,128]{2,1,0:T(8,128)}, u32[]{:S(2)}) copy-start(f32[2,2048,128]{2,1,0:T(8,128)} %x.1) | copy-start | bytes 6291460
  35.9 6.3 %collective-permute-start.5 = (f32[192,256]{1,0:T(8,128)S(1)}, f32[192,256]{1,0:T(8,128)S(1)}, u32[]{:S(2)}, u32[]{:S(2)}) collective-permute-start(f32[192,256]{1,0:T(8,128)S(1)} %slice.16), channel_id=1, source_target_pairs={{0,1},{1,2},{2,3},{4,5},{5,6},{6,7},{8,9},{9,10},{10,11},{12,13},{... | collective-permute-start | bytes 589832 | tf_op jit(solution)/shard_map/ppermute | solution.py:406
  37.2 5.0 %collective-permute-start.6 = (f32[64,256]{1,0:T(8,128)S(1)}, f32[64,256]{1,0:T(8,128)S(1)}, u32[]{:S(2)}, u32[]{:S(2)}) collective-permute-start(f32[64,256]{1,0:T(8,128)S(1)} %slice.17), channel_id=1, source_target_pairs={{1,0},{2,1},{3,2},{5,4},{6,5},{7,6},{9,8},{10,9},{11,10},{13,12},{... | collective-permute-start | bytes 196616 | tf_op jit(solution)/shard_map/ppermute | solution.py:406

commit v4 on v3

--- a/solution.py
+++ b/solution.py
@@ -69,7 +69,7 @@
     return pl.pallas_call(
         partial(pack_kernel, total_blocks),
         out_shape=jax.ShapeDtypeStruct((2 * slots + 8, 128), F32),
-        in_specs=[pl.BlockSpec(memory_space=pltpu.HBM)] * 4,
+        in_specs=[pl.BlockSpec(memory_space=pl.ANY)] * 4,
         out_specs=VMEM,
         scratch_shapes=[
             pltpu.VMEM((2 * slots, 128), F32),
@@ -81,18 +81,19 @@
         compiler_params=PARAMS,
         name="pack",
     )(
-        pupils.reshape(2 * slots, 128),
-        starts.reshape(-1, 128),
-        counts.reshape(-1, 128),
-        weights.reshape(-1, 128),
+        *(
+            pltpu.with_memory_space_constraint(x, pltpu.HBM)
+            for x in (
+                pupils.reshape(2 * slots, 128),
+                starts.reshape(-1, 128),
+                counts.reshape(-1, 128),
+                weights.reshape(-1, 128),
+            )
+        )
     )
 
 
-def build_kernel(add, *refs):
-    if add:
-        chunk, before, out, lhs_hi, lhs_lo = refs
-    else:
-        chunk, out, lhs_hi, lhs_lo = refs
+def factors(chunk):
     count = (chunk.shape[0] - 8) // 2
     real = chunk[:count, :]
     imag = chunk[count : 2 * count, :]
@@ -103,20 +104,29 @@
         ],
         axis=0,
     )
-    right_hi, right_lo = split(right)
     left = jnp.concatenate([real.T, imag.T], axis=1)
-    left_hi, left_lo = split(left)
-    left_hi = left_hi.reshape(8, 16, 2 * count)
-    left_lo = left_lo.reshape(8, 16, 2 * count)
     places = [chunk[2 * count + t : 2 * count + t + 1, :] for t in range(count // 128)]
     place = jnp.broadcast_to(jnp.concatenate(places + places, axis=1), (16, 2 * count))
+    return split(left), split(right), place
+
+
+def at_block(part, place, b):
+    mask = jnp.where(place == b, 1.0, 0.0).astype(BF16)[None]
+    return (part.reshape(8, 16, -1) * mask).reshape(part.shape)
+
+
+def build_kernel(add, *refs):
+    if add:
+        chunk, before, out, lhs_hi, lhs_lo = refs
+    else:
+        chunk, out, lhs_hi, lhs_lo = refs
+    (left_hi, left_lo), (right_hi, right_lo), place = factors(chunk)
 
     def one_group(g, carry):
         for j in range(GROUP):
             b = (g * GROUP + j).astype(F32)
-            mask = jnp.where(place == b, 1.0, 0.0).astype(BF16)[None]
-            lhs_hi[j * 128 : (j + 1) * 128, :] = (left_hi * mask).reshape(128, 2 * count)
-            lhs_lo[j * 128 : (j + 1) * 128, :] = (left_lo * mask).reshape(128, 2 * count)
+            lhs_hi[j * 128 : (j + 1) * 128, :] = at_block(left_hi, place, b)
+            lhs_lo[j * 128 : (j + 1) * 128, :] = at_block(left_lo, place, b)
         at = pl.ds(pl.multiple_of(g * GROUP * 128, GROUP * 128), GROUP * 128)
         hi = lhs_hi[...]
         total = dot(hi, right_hi) + dot(hi, right_lo) + dot(lhs_lo[...], right_hi)
@@ -142,6 +152,29 @@
         ),
         name="band_terms",
     )(*args)
+
+
+def edge_kernel(chunk, before, after_out, before_out):
+    (left_hi, left_lo), (right_hi, right_lo), place = factors(chunk)
+    hi = jnp.concatenate([at_block(left_hi, place, float(b)) for b in (0, RB - 2, RB - 1)], axis=0)
+    lo = jnp.concatenate([at_block(left_lo, place, float(b)) for b in (0, RB - 2, RB - 1)], axis=0)
+    total = dot(hi, right_hi) + dot(hi, right_lo) + dot(lo, right_hi)
+    after_out[...] = before[RB * 128 - 192 :, :] + total[192:]
+    before_out[...] = before[:BLOCK, :] + total[:BLOCK]
+
+
+def build_edges(chunk, before):
+    return pl.pallas_call(
+        edge_kernel,
+        out_shape=(
+            jax.ShapeDtypeStruct((3 * BLOCK, 256), F32),
+            jax.ShapeDtypeStruct((BLOCK, 256), F32),
+        ),
+        in_specs=[VMEM] * 2,
+        out_specs=(VMEM, VMEM),
+        compiler_params=PARAMS,
+        name="edge_terms",
+    )(chunk, before)
 
 
 def swapped(x):
@@ -406,15 +439,29 @@
     return lax.ppermute(x, "blk", pairs)
 
 
+def gathered(own):
+    peers = lax.axis_size("src")
+    chunks = [own]
+    if peers & (peers - 1):
+        for k in range(1, peers):
+            chunks.append(lax.ppermute(own, "src", [(i, (i + k) % peers) for i in range(peers)]))
+        return chunks
+    far = peers // 2
+    while far:
+        pairs = [(i, i ^ far) for i in range(peers)]
+        chunks = chunks + [lax.ppermute(chunk, "src", pairs) for chunk in chunks]
+        far //= 2
+    if len(chunks) == 4:
+        chunks = [chunks[i] for i in (0, 2, 1, 3)]
+    return chunks
+
+
 def per_device(pupils, starts, counts, weights, start_block):
     regions = lax.axis_size("blk")
     peers = lax.axis_size("src")
 
     own = pack(pupils, starts, counts, weights, regions * RB)
-    chunks = [own]
-    for k in range(1, peers):
-        chunks.append(lax.ppermute(own, "src", [(i, (i + k) % peers) for i in range(peers)]))
-
+    chunks = gathered(own)
     edge = 2 * BLOCK
     size = start_block.shape[1]
     x_left = shifted(start_block[:, size - edge :], 1)
@@ -422,10 +469,12 @@
 
     band = build(own, None)
     band, x_left, x_right = lax.optimization_barrier((band, x_left, x_right))
-    for k in range(1, peers):
-        band = build(chunks[k], band)
-    left_band = shifted(band[RB * 128 - 192 :], 1)
-    right_band = shifted(band[:BLOCK], -1)
+    for chunk in chunks[1:-1]:
+        band = build(chunk, band)
+    left_band, right_band = build_edges(chunks[-1], band)
+    left_band = shifted(left_band, 1)
+    right_band = shifted(right_band, -1)
+    band = build(chunks[-1], band)
     z, grams = apply_twice(band, left_band, right_band, start_block, x_left, x_right)
     grams = lax.all_gather(grams, "blk", axis=0)
     return finish(grams, z, 2.0 * size * regions)

time: 72.3 us -> 65.2 us (0.902)
  the two profiles are of different devices: /device:TPU:27 before, /device:TPU:0 now
where the time goes in v4:
time: 65.2 us; the launch traced here: 64.9 us
  Pallas kernels  39.2 us (60%)
  starting transfers between devices  11.4 us (17%)
  blocking collectives  8.97 us (14%)
  waiting for transfers between devices  4.22 us (6%)
  local copies, waits for them, and re-layouts  0.99 us (2%)
    pallas_call x4, Pallas kernels, build(): pl.pallas_call(partial(build_kernel, before is not None), out_shape=jax.S...  16.4 us
    pallas_call x1, Pallas kernels, finish(): pl.pallas_call(partial(finish_kernel, total_rows), out_shape=jax.ShapeDty...  11.6 us
    pallas_call x1, Pallas kernels, apply_twice(): pl.pallas_call(apply_kernel, out_shape=(jax.ShapeDtypeStruct((rows, 256),...  9.36 us
    all_gather x1, blocking collectives, per_device(): grams = lax.all_gather(grams, 'blk', axis=0)  8.97 us
    ppermute x3, starting transfers between devices, gathered(): chunks = chunks + [lax.ppermute(chunk, 'src', pairs) for chunk in chunks]  6.13 us
    ppermute x4, starting transfers between devices, shifted(): return lax.ppermute(x, 'blk', pairs)  5.31 us
    ppermute x3, waiting for transfers between devices, gathered(): chunks = chunks + [lax.ppermute(chunk, 'src', pairs) for chunk in chunks]  4.21 us
  transfers between devices with their start and end apart: 7, of which 1 were waited for; matrix products, arithmetic and copies ran while one was open for 2% of the time, Pallas kernels for 25%

profile of v4, /device:TPU:0, one launch (start us, length us, event | category | flops | bytes accessed | tf_op | source)
XLA Modules:
  0.0 64.9 jit_solution(5918021303118964687)
XLA Ops:
  0.0 1.2 %pack.1.refs_0_ = f32[520,128]{1,0:T(8,128)S(1)} custom-call(f32[512,128]{1,0:T(8,128)} %bitcast.6, s32[2,128]{1,0:T(2,128)} %bitcast.7, s32[2,128]{1,0:T(2,128)} %bitcast.8, f32[2,128]{1,0:T(2,128)} %bitcast.9), custom_call_target="tpu_custom_call" | custom-call | tf_op jit(solution)/shard_map/pack/pallas_call | solution.py:69
  1.2 3.1 %collective-permute-start.2 = (f32[520,128]{1,0:T(8,128)S(1)}, f32[520,128]{1,0:T(8,128)S(1)}, u32[]{:S(2)}, u32[]{:S(2)}) collective-permute-start(f32[520,128]{1,0:T(8,128)S(1)} %pack.1.refs_0_), channel_id=1, source_target_pairs={{0,4},{4,0},{8,12},{12,8},{1,5},{5,1},{9,13},{13,9},{2,6},{6,2},{1... | collective-permute-start | bytes 798728 | tf_op jit(solution)/shard_map/ppermute | solution.py:452
  4.3 2.6 %collective-permute-start = (f32[520,128]{1,0:T(8,128)S(1)}, f32[520,128]{1,0:T(8,128)S(1)}, u32[]{:S(2)}, u32[]{:S(2)}) collective-permute-start(f32[520,128]{1,0:T(8,128)S(1)} %pack.1.refs_0_), channel_id=1, source_target_pairs={{0,8},{4,12},{8,0},{12,4},{1,9},{5,13},{9,1},{13,5},{2,10},{6,14},... | collective-permute-start | bytes 798728 | tf_op jit(solution)/shard_map/ppermute | solution.py:452
  6.9 1.0 %fusion = (f32[2,128,128]{2,1,0:T(8,128)S(1)}, f32[2,128,128]{2,1,0:T(8,128)S(1)}) fusion(f32[2,2048,128]{2,1,0:T(8,128)} %x.1), kind=kLoop, calls=%fused_computation | loop fusion | bytes 524288 | tf_op jit(solution)/shard_map/slice | solution.py:468
  7.9 1.3 %collective-permute-start.3 = (f32[2,128,128]{2,1,0:T(8,128)S(1)}, f32[2,128,128]{2,1,0:T(8,128)S(1)}, u32[]{:S(2)}, u32[]{:S(2)}) collective-permute-start(f32[2,128,128]{2,1,0:T(8,128)S(1)} %get-tuple-element.20), channel_id=1, source_target_pairs={{0,1},{1,2},{2,3},{4,5},{5,6},{6,7},{8,9},{9,10},{10,11},{12,13},{... | collective-permute-start | bytes 393224 | tf_op jit(solution)/shard_map/ppermute | solution.py:439
  9.2 1.3 %collective-permute-start.4 = (f32[2,128,128]{2,1,0:T(8,128)S(1)}, f32[2,128,128]{2,1,0:T(8,128)S(1)}, u32[]{:S(2)}, u32[]{:S(2)}) collective-permute-start(f32[2,128,128]{2,1,0:T(8,128)S(1)} %get-tuple-element.19), channel_id=1, source_target_pairs={{1,0},{2,1},{3,2},{5,4},{6,5},{7,6},{9,8},{10,9},{11,10},{13,12},{... | collective-permute-start | bytes 393224 | tf_op jit(solution)/shard_map/ppermute | solution.py:439
  10.5 4.1 %band_terms.4.refs_1_ = f32[4096,256]{1,0:T(8,128)S(1)} custom-call(f32[520,128]{1,0:T(8,128)S(1)} %pack.1.refs_0_), custom_call_target="tpu_custom_call" | custom-call | flops 3221225472 | bytes 10485760 | tf_op jit(solution)/shard_map/band_terms/pallas_call | solution.py:142
  14.6 0.0 collective-permute-done.3.x_left
  14.6 0.0 collective-permute-done.4.x_right
  14.6 4.2 %collective-permute-done.refs_0_ = f32[520,128]{1,0:T(8,128)S(1)} collective-permute-done((f32[520,128]{1,0:T(8,128)S(1)}, f32[520,128]{1,0:T(8,128)S(1)}, u32[]{:S(2)}, u32[]{:S(2)}) %collective-permute-start) | collective-permute-done | bytes 266272 | tf_op jit(solution)/shard_map/ppermute | solution.py:452
  18.8 0.4 collective-permute-start.1
  19.3 0.0 collective-permute-done.2.refs_0_
  19.3 4.1 %band_terms.5.refs_1_ = f32[4096,256]{1,0:T(8,128)S(1)} custom-call(f32[520,128]{1,0:T(8,128)S(1)} %collective-permute-done.2.refs_0_, f32[4096,256]{1,0:T(8,128)S(1)} %band_terms.4.refs_1_), custom_call_target="tpu_custom_call", output_to_operand_aliasing={{}: (1, {})} | custom-call | flops 3221225472 | bytes 10485760 | tf_op jit(solution)/shard_map/band_terms/pallas_call | solution.py:142
  23.4 4.1 %band_terms.6.refs_1_.before = f32[4096,256]{1,0:T(8,128)S(1)} custom-call(f32[520,128]{1,0:T(8,128)S(1)} %collective-permute-done.refs_0_, f32[4096,256]{1,0:T(8,128)S(1)} %band_terms.5.refs_1_), custom_call_target="tpu_custom_call", output_to_operand_aliasing={{}: (1, {})} | custom-call | flops 3221225472 | bytes 10485760 | tf_op jit(solution)/shard_map/band_terms/pallas_call | solution.py:142
  27.5 0.0 collective-permute-done.1.refs_0_.chunk
  27.5 0.6 edge_terms.1
  28.1 1.3 %collective-permute-start.5 = (f32[192,256]{1,0:T(8,128)S(1)}, f32[192,256]{1,0:T(8,128)S(1)}, u32[]{:S(2)}, u32[]{:S(2)}) collective-permute-start(f32[192,256]{1,0:T(8,128)S(1)} %get-tuple-element.13), channel_id=1, source_target_pairs={{0,1},{1,2},{2,3},{4,5},{5,6},{6,7},{8,9},{9,10},{10,11},{12,13},{... | collective-permute-start | bytes 589832 | tf_op jit(solution)/shard_map/ppermute | solution.py:439
  29.4 0.0 copy-start
  29.4 1.4 %collective-permute-start.6 = (f32[64,256]{1,0:T(8,128)S(1)}, f32[64,256]{1,0:T(8,128)S(1)}, u32[]{:S(2)}, u32[]{:S(2)}) collective-permute-start(f32[64,256]{1,0:T(8,128)S(1)} %get-tuple-element.14), channel_id=1, source_target_pairs={{1,0},{2,1},{3,2},{5,4},{6,5},{7,6},{9,8},{10,9},{11,10},{13,12},{... | collective-permute-start | bytes 196616 | tf_op jit(solution)/shard_map/ppermute | solution.py:439
  30.8 4.1 %band_terms.7.band = f32[4096,256]{1,0:T(8,128)S(1)} custom-call(f32[520,128]{1,0:T(8,128)S(1)} %collective-permute-done.1.refs_0_.chunk, f32[4096,256]{1,0:T(8,128)S(1)} %band_terms.6.refs_1_.before), custom_call_target="tpu_custom_call", output_to_operand_aliasing={{}: (1, {})} | custom-call | flops 3221225472 | bytes 10485760 | tf_op jit(solution)/shard_map/band_terms/pallas_call | solution.py:142
  35.0 0.0 collective-permute-done.6.right_band
  35.0 0.0 collective-permute-done.5.left_band
  35.0 0.0 copy-done
  35.0 9.4 %apply_twice.1 = (f32[2048,256]{1,0:T(8,128)S(1)}, f32[136,128]{1,0:T(8,128)S(1)}) custom-call(f32[4096,256]{1,0:T(8,128)S(1)} %band_terms.7.band, f32[192,256]{1,0:T(8,128)S(1)} %collective-permute-done.5.left_band, f32[64,256]{1,0:T(8,128)S(1)} %collective-permute-done.6.right_band, f32[2,2048,128]{2,1,0:T(8,128)S(1)} %copy-done, ...), custom_call_target="tpu_custom_call" | custom-call | flops 3221225472 | bytes 12582912 | tf_op jit(solution)/shard_map/apply_twice/pallas_call | solution.py:288
  44.4 9.0 %all-gather = f32[544,128]{1,0:T(8,128)S(1)} all-gather(f32[136,128]{1,0:T(8,128)S(1)} %get-tuple-element.17), channel_id=2, replica_groups=mesh['groups'=2,'src'=4,'blk'=4] {'blk'}, dimensions={0}, use_global_device_ids=true | all-gather | bytes 348160 | tf_op jit(solution)/shard_map/all_gather | solution.py:479
  53.3 11.6 %finish.1 = f32[2,2048,128]{2,1,0:T(8,128)} custom-call(f32[4,136,128]{2,1,0:T(8,128)S(1)} %bitcast.5, f32[2048,256]{1,0:T(8,128)S(1)} %get-tuple-element.18.z), custom_call_target="tpu_custom_call" | custom-call | tf_op jit(solution)/shard_map/finish/pallas_call | solution.py:425
Async XLA Ops:
  1.2 18.0 %collective-permute-start.2 = (f32[520,128]{1,0:T(8,128)S(1)}, f32[520,128]{1,0:T(8,128)S(1)}, u32[]{:S(2)}, u32[]{:S(2)}) collective-permute-start(f32[520,128]{1,0:T(8,128)S(1)} %pack.1.refs_0_), channel_id=1, source_target_pairs={{0,4},{4,0},{8,12},{12,8},{1,5},{5,1},{9,13},{13,9},{2,6},{6,2},{1... | collective-permute-start | bytes 798728 | tf_op jit(solution)/shard_map/ppermute | solution.py:452
  4.3 14.5 %collective-permute-start = (f32[520,128]{1,0:T(8,128)S(1)}, f32[520,128]{1,0:T(8,128)S(1)}, u32[]{:S(2)}, u32[]{:S(2)}) collective-permute-start(f32[520,128]{1,0:T(8,128)S(1)} %pack.1.refs_0_), channel_id=1, source_target_pairs={{0,8},{4,12},{8,0},{12,4},{1,9},{5,13},{9,1},{13,5},{2,10},{6,14},... | collective-permute-start | bytes 798728 | tf_op jit(solution)/shard_map/ppermute | solution.py:452
  7.9 6.7 %collective-permute-start.3 = (f32[2,128,128]{2,1,0:T(8,128)S(1)}, f32[2,128,128]{2,1,0:T(8,128)S(1)}, u32[]{:S(2)}, u32[]{:S(2)}) collective-permute-start(f32[2,128,128]{2,1,0:T(8,128)S(1)} %get-tuple-element.20), channel_id=1, source_target_pairs={{0,1},{1,2},{2,3},{4,5},{5,6},{6,7},{8,9},{9,10},{10,11},{12,13},{... | collective-permute-start | bytes 393224 | tf_op jit(solution)/shard_map/ppermute | solution.py:439
  9.2 5.4 %collective-permute-start.4 = (f32[2,128,128]{2,1,0:T(8,128)S(1)}, f32[2,128,128]{2,1,0:T(8,128)S(1)}, u32[]{:S(2)}, u32[]{:S(2)}) collective-permute-start(f32[2,128,128]{2,1,0:T(8,128)S(1)} %get-tuple-element.19), channel_id=1, source_target_pairs={{1,0},{2,1},{3,2},{5,4},{6,5},{7,6},{9,8},{10,9},{11,10},{13,12},{... | collective-permute-start | bytes 393224 | tf_op jit(solution)/shard_map/ppermute | solution.py:439
  18.8 8.7 %collective-permute-start.1 = (f32[520,128]{1,0:T(8,128)S(1)}, f32[520,128]{1,0:T(8,128)S(1)}, u32[]{:S(2)}, u32[]{:S(2)}) collective-permute-start(f32[520,128]{1,0:T(8,128)S(1)} %collective-permute-done.refs_0_), channel_id=1, source_target_pairs={{0,4},{4,0},{8,12},{12,8},{1,5},{5,1},{9,13},{13,9},{2,6},{6,2},{1... | collective-permute-start | bytes 798728 | tf_op jit(solution)/shard_map/ppermute | solution.py:452
  28.1 6.9 %collective-permute-start.5 = (f32[192,256]{1,0:T(8,128)S(1)}, f32[192,256]{1,0:T(8,128)S(1)}, u32[]{:S(2)}, u32[]{:S(2)}) collective-permute-start(f32[192,256]{1,0:T(8,128)S(1)} %get-tuple-element.13), channel_id=1, source_target_pairs={{0,1},{1,2},{2,3},{4,5},{5,6},{6,7},{8,9},{9,10},{10,11},{12,13},{... | collective-permute-start | bytes 589832 | tf_op jit(solution)/shard_map/ppermute | solution.py:439
  29.4 5.6 %copy-start = (f32[2,2048,128]{2,1,0:T(8,128)S(1)}, f32[2,2048,128]{2,1,0:T(8,128)}, u32[]{:S(2)}) copy-start(f32[2,2048,128]{2,1,0:T(8,128)} %x.1) | copy-start | bytes 6291460
  29.4 5.6 %collective-permute-start.6 = (f32[64,256]{1,0:T(8,128)S(1)}, f32[64,256]{1,0:T(8,128)S(1)}, u32[]{:S(2)}, u32[]{:S(2)}) collective-permute-start(f32[64,256]{1,0:T(8,128)S(1)} %get-tuple-element.14), channel_id=1, source_target_pairs={{1,0},{2,1},{3,2},{5,4},{6,5},{7,6},{9,8},{10,9},{11,10},{13,12},{... | collective-permute-start | bytes 196616 | tf_op jit(solution)/shard_map/ppermute | solution.py:439

commit v5 on v4

--- a/solution.py
+++ b/solution.py
@@ -115,11 +115,10 @@
     return (part.reshape(8, 16, -1) * mask).reshape(part.shape)
 
 
-def build_kernel(add, *refs):
-    if add:
-        chunk, before, out, lhs_hi, lhs_lo = refs
-    else:
-        chunk, out, lhs_hi, lhs_lo = refs
+def build_kernel(add, last, chunk, *refs):
+    refs = list(refs)
+    before = refs.pop(0) if add else None
+    lhs_lo, lhs_hi = refs.pop(), refs.pop()
     (left_hi, left_lo), (right_hi, right_lo), place = factors(chunk)
 
     def one_group(g, carry):
@@ -130,55 +129,76 @@
         at = pl.ds(pl.multiple_of(g * GROUP * 128, GROUP * 128), GROUP * 128)
         hi = lhs_hi[...]
         total = dot(hi, right_hi) + dot(hi, right_lo) + dot(lhs_lo[...], right_hi)
-        out[at, :] = before[at, :] + total if add else total
+        if add:
+            total = before[at, :] + total
+        if last:
+            refs[0][at, :], refs[1][at, :] = split(total)
+        else:
+            refs[0][at, :] = total
         return carry
 
     lax.fori_loop(0, RB // GROUP, one_group, 0)
 
 
-def build(chunk, before):
+def build(chunk, before, last=False):
     count = (chunk.shape[0] - 8) // 2
-    args = (chunk,) + (() if before is None else (before,))
-    return pl.pallas_call(
-        partial(build_kernel, before is not None),
-        out_shape=jax.ShapeDtypeStruct((RB * 128, 256), F32),
-        in_specs=[VMEM] * len(args),
-        out_specs=VMEM,
+    add = before is not None
+    shape = (RB * 128, 256)
+    out = [jax.ShapeDtypeStruct(shape, BF16)] * 2 if last else [jax.ShapeDtypeStruct(shape, F32)]
+    result = pl.pallas_call(
+        partial(build_kernel, add, last),
+        out_shape=out,
+        in_specs=[VMEM] * (1 + add),
+        out_specs=[VMEM] * len(out),
         scratch_shapes=[pltpu.VMEM((GROUP * 128, 2 * count), BF16)] * 2,
-        input_output_aliases={} if before is None else {1: 0},
+        input_output_aliases={1: 0} if add and not last else {},
         compiler_params=PARAMS,
         cost_estimate=pl.CostEstimate(
-            flops=6 * RB * 128 * 2 * count * 256, bytes_accessed=10 << 20, transcendentals=0
+            flops=1 << 20, bytes_accessed=1 << 16, transcendentals=0
         ),
         name="band_terms",
-    )(*args)
-
-
-def edge_kernel(chunk, before, after_out, before_out):
+    )(chunk, *([before] if add else []))
+    return result if last else result[0]
+
+
+def wide(parts):
+    return jnp.concatenate([parts[0], parts[1]], axis=1)
+
+
+def edge_kernel(chunk, before, x, after_out, before_out):
     (left_hi, left_lo), (right_hi, right_lo), place = factors(chunk)
     hi = jnp.concatenate([at_block(left_hi, place, float(b)) for b in (0, RB - 2, RB - 1)], axis=0)
     lo = jnp.concatenate([at_block(left_lo, place, float(b)) for b in (0, RB - 2, RB - 1)], axis=0)
     total = dot(hi, right_hi) + dot(hi, right_lo) + dot(lo, right_hi)
-    after_out[...] = before[RB * 128 - 192 :, :] + total[192:]
-    before_out[...] = before[:BLOCK, :] + total[:BLOCK]
-
-
-def build_edges(chunk, before):
+    after_out[: 3 * BLOCK, :] = before[RB * 128 - 192 :, :] + total[192:]
+    after_out[3 * BLOCK :, :] = wide(x[:, x.shape[1] - 2 * BLOCK :, :])
+    before_out[:BLOCK, :] = before[:BLOCK, :] + total[:BLOCK]
+    before_out[BLOCK:, :] = wide(x[:, : 2 * BLOCK, :])
+
+
+def build_edges(chunk, before, x):
     return pl.pallas_call(
         edge_kernel,
         out_shape=(
+            jax.ShapeDtypeStruct((5 * BLOCK, 256), F32),
             jax.ShapeDtypeStruct((3 * BLOCK, 256), F32),
-            jax.ShapeDtypeStruct((BLOCK, 256), F32),
         ),
-        in_specs=[VMEM] * 2,
+        in_specs=[VMEM] * 3,
         out_specs=(VMEM, VMEM),
         compiler_params=PARAMS,
         name="edge_terms",
-    )(chunk, before)
-
-
-def swapped(x):
-    return jnp.concatenate([-x[:, M:], x[:, :M]], axis=1)
+    )(chunk, before, x)
+
+
+def real_form(rows):
+    return jnp.concatenate(
+        [rows, jnp.concatenate([-rows[:, M:], rows[:, :M]], axis=1)], axis=0
+    )
+
+
+def times(g_hi, g_lo, hi, lo):
+    hi, lo = real_form(hi), real_form(lo)
+    return dot(g_hi, hi) + dot(g_hi, lo) + dot(g_lo, hi)
 
 
 def gram_of(hi, lo):
@@ -189,92 +209,90 @@
     return a + b + b.T
 
 
-def apply_kernel(band, left_band, right_band, x, x_left, x_right, z, grams,
-                 g_hi, g_lo, x_hi, x_lo, s_hi, s_lo, p, p_hi, p_lo):
-    pairs = RB + 3
-    zero = jnp.zeros((BLOCK, 256), BF16)
-
-    def put_g(e_rows, value):
-        hi, lo = split(value)
-        g_hi[e_rows, :] = hi
-        g_lo[e_rows, :] = lo
-
-    g_hi[0:BLOCK, :] = zero
-    g_lo[0:BLOCK, :] = zero
-    put_g(pl.ds(BLOCK, 3 * BLOCK), left_band[...])
-    put_g(pl.ds((RB + 2) * 128, BLOCK), right_band[...])
-    g_hi[(RB + 2) * 128 + BLOCK :, :] = zero
-    g_lo[(RB + 2) * 128 + BLOCK :, :] = zero
-
-    def put_x(at, value):
-        hi, lo = split(value)
-        x_hi[at, :] = hi
-        x_lo[at, :] = lo
-        hi, lo = split(swapped(value))
-        s_hi[at, :] = hi
-        s_lo[at, :] = lo
-
-    put_x(pl.ds(0, 2 * BLOCK), jnp.concatenate([x_left[0], x_left[1]], axis=1))
-    put_x(pl.ds((RB + 2) * BLOCK, 2 * BLOCK), jnp.concatenate([x_right[0], x_right[1]], axis=1))
-
-    def prepare(i, carry):
-        at = pl.ds(pl.multiple_of(i * 256, 256), 256)
-        put_g(pl.ds(pl.multiple_of(256 + i * 256, 256), 256), band[at, :])
-        half = pl.ds(pl.multiple_of(i * 128, 128), 128)
-        put_x(
-            pl.ds(pl.multiple_of(i * 128 + 128, 128), 128),
-            jnp.concatenate([x[0, half, :], x[1, half, :]], axis=1),
-        )
-        return carry
-
-    lax.fori_loop(0, RB // 2, prepare, 0)
-
-    def pair(e):
-        at = pl.ds(pl.multiple_of(e * 128, 128), 128)
-        win = pl.ds(pl.multiple_of(e * BLOCK, BLOCK), 128)
-        w_hi = jnp.concatenate([x_hi[win, :], s_hi[win, :]], axis=0)
-        w_lo = jnp.concatenate([x_lo[win, :], s_lo[win, :]], axis=0)
-        hi = g_hi[at, :]
-        return dot(hi, w_hi) + dot(hi, w_lo) + dot(g_lo[at, :], w_hi)
-
-    def first(e, carry):
-        both = pair(e)
-        p[pl.ds(pl.multiple_of(e * BLOCK, BLOCK), BLOCK), :] = both[:BLOCK] + carry
+def prepare_kernel(x, hi_out, lo_out):
+    for i in range(0, x.shape[1], 256):
+        hi_out[i : i + 256, :], lo_out[i : i + 256, :] = split(wide(x[:, i : i + 256, :]))
+
+
+def prepare(x):
+    shape = jax.ShapeDtypeStruct((x.shape[1], 256), BF16)
+    return pl.pallas_call(
+        prepare_kernel,
+        out_shape=(shape, shape),
+        in_specs=[VMEM],
+        out_specs=(VMEM, VMEM),
+        compiler_params=PARAMS,
+        cost_estimate=pl.CostEstimate(flops=1 << 20, bytes_accessed=4 << 20, transcendentals=0),
+        name="prepare",
+    )(x)
+
+
+def apply_kernel(g_hi, g_lo, left, right, x_hi, x_lo, z_hi, z_lo, grams, p_hi, p_lo):
+    rows = RB * BLOCK
+    left_hi, left_lo = split(left[: 3 * BLOCK, :])
+    right_hi, right_lo = split(right[:BLOCK, :])
+
+    def put(e, block):
+        at = pl.ds(pl.multiple_of(e * BLOCK, BLOCK), BLOCK)
+        p_hi[at, :], p_lo[at, :] = split(block)
+
+    def join(a, b):
+        return jnp.concatenate([a, b], axis=0)
+
+    head = split(left[3 * BLOCK :, :])
+    tail = split(right[BLOCK:, :])
+    spill = times(left_hi[:BLOCK], left_lo[:BLOCK], head[0], head[1])
+    both = times(
+        left_hi[BLOCK:],
+        left_lo[BLOCK:],
+        join(head[0][BLOCK:], x_hi[:BLOCK, :]),
+        join(head[1][BLOCK:], x_lo[:BLOCK, :]),
+    )
+    first_block = spill + both[:BLOCK]
+    put(0, first_block)
+
+    def first(b, carry):
+        spill, top = carry
+        at = pl.ds(pl.multiple_of(b * 128, 128), 128)
+        win = pl.ds(pl.multiple_of(b * BLOCK, BLOCK), 128)
+        both = times(g_hi[at, :], g_lo[at, :], x_hi[win, :], x_lo[win, :])
+        block = both[:BLOCK] + spill
+        put(b + 1, block)
+        return both[BLOCK:], jnp.maximum(top, jnp.abs(block))
+
+    spill, top = lax.fori_loop(
+        0, RB - 1, first, (both[BLOCK:], jnp.abs(first_block)), unroll=UNROLL
+    )
+    both = times(
+        g_hi[(RB - 1) * 128 :, :],
+        g_lo[(RB - 1) * 128 :, :],
+        join(x_hi[rows - BLOCK :, :], tail[0][:BLOCK]),
+        join(x_lo[rows - BLOCK :, :], tail[1][:BLOCK]),
+    )
+    block = both[:BLOCK] + spill
+    put(RB, block)
+    last_block = both[BLOCK:] + times(right_hi, right_lo, tail[0], tail[1])
+    put(RB + 1, last_block)
+    top = jnp.maximum(jnp.maximum(top, jnp.abs(block)), jnp.abs(last_block))
+    top = jnp.max(top, axis=0, keepdims=True)
+    top = jnp.maximum(top[:, :M], top[:, M:])
+    scale = jnp.where(top > 0, 1.0 / jnp.where(top > 0, top, 1.0), 0.0)
+    scale = jnp.concatenate([scale, scale], axis=1)
+
+    inner = pl.ds(BLOCK, rows)
+    gram_1 = gram_of(p_hi[inner, :], p_lo[inner, :])
+
+    def second(b, spill):
+        at = pl.ds(pl.multiple_of(b * 128, 128), 128)
+        win = pl.ds(pl.multiple_of((b + 1) * BLOCK, BLOCK), 128)
+        both = times(g_hi[at, :], g_lo[at, :], p_hi[win, :], p_lo[win, :])
+        out = pl.ds(pl.multiple_of(b * BLOCK, BLOCK), BLOCK)
+        z_hi[out, :], z_lo[out, :] = split((both[:BLOCK] + spill) * scale)
         return both[BLOCK:]
 
-    lax.fori_loop(0, pairs, first, jnp.zeros((BLOCK, 256), F32), unroll=UNROLL)
-
-    def prepare_again(i, carry):
-        at = pl.ds(pl.multiple_of(i * 128, 128), 128)
-        put_x(at, p[at, :])
-        return carry
-
-    lax.fori_loop(0, (RB + 4) // 2, prepare_again, 0)
-    rows = RB * BLOCK
-    inner = pl.ds(2 * BLOCK, rows)
-    gram_1 = gram_of(x_hi[inner, :], x_lo[inner, :])
-
-    def second(e, carry):
-        both = pair(e)
-        z[pl.ds(pl.multiple_of((e - 2) * BLOCK, BLOCK), BLOCK), :] = both[:BLOCK] + carry
-        return both[BLOCK:]
-
-    lax.fori_loop(2, RB + 2, second, pair(1)[BLOCK:], unroll=UNROLL)
-
-    top = jnp.max(jnp.abs(z[...]), axis=0, keepdims=True)
-    top = jnp.maximum(top[:, :M], top[:, M:])
-    scale = jnp.where(top > 0, 1.0 / jnp.where(top > 0, top, 1.0), 1.0)
-    scale = jnp.concatenate([scale, scale], axis=1)
-
-    def prepare_z(i, carry):
-        at = pl.ds(pl.multiple_of(i * 128, 128), 128)
-        hi, lo = split(z[at, :] * scale)
-        p_hi[at, :] = hi
-        p_lo[at, :] = lo
-        return carry
-
-    lax.fori_loop(0, rows // 128, prepare_z, 0)
-    gram_2 = gram_of(p_hi[...], p_lo[...])
+    spill = times(left_hi[2 * BLOCK :], left_lo[2 * BLOCK :], p_hi[:128, :], p_lo[:128, :])
+    lax.fori_loop(0, RB, second, spill, unroll=UNROLL)
+    gram_2 = gram_of(z_hi[...], z_lo[...])
     row = lax.broadcasted_iota(jnp.int32, (M, M), 0)
     col = lax.broadcasted_iota(jnp.int32, (M, M), 1)
     grams[:M, :] = jnp.where(row >= col, gram_1, gram_2)
@@ -282,27 +300,24 @@
     grams[M:, :] = jnp.concatenate([diagonal, top, jnp.zeros((6, M), F32)], axis=0)
 
 
-def apply_twice(band, left_band, right_band, x, x_left, x_right):
+def apply_twice(g_hi, g_lo, left, right, x_hi, x_lo):
     rows = RB * BLOCK
-    wide = (RB + 4) * BLOCK
     return pl.pallas_call(
         apply_kernel,
         out_shape=(
-            jax.ShapeDtypeStruct((rows, 256), F32),
+            jax.ShapeDtypeStruct((rows, 256), BF16),
+            jax.ShapeDtypeStruct((rows, 256), BF16),
             jax.ShapeDtypeStruct((M + 8, M), F32),
         ),
         in_specs=[VMEM] * 6,
-        out_specs=(VMEM, VMEM),
-        scratch_shapes=[pltpu.VMEM(((RB + 3) * 128, 256), BF16)] * 2
-        + [pltpu.VMEM((wide, 256), BF16)] * 4
-        + [pltpu.VMEM((wide, 256), F32)]
-        + [pltpu.VMEM((rows, 256), BF16)] * 2,
+        out_specs=(VMEM, VMEM, VMEM),
+        scratch_shapes=[pltpu.VMEM((rows + 2 * BLOCK, 256), BF16)] * 2,
         compiler_params=PARAMS,
         cost_estimate=pl.CostEstimate(
             flops=12 * RB * 128 * 256 * 256, bytes_accessed=12 << 20, transcendentals=0
         ),
         name="apply_twice",
-    )(band, left_band, right_band, x, x_left, x_right)
+    )(g_hi, g_lo, left, right, x_hi, x_lo)
 
 
 def inverse_factor(a, work):
@@ -370,7 +385,7 @@
     return work[:, M:]
 
 
-def finish_kernel(total_rows, grams, z, out, work):
+def finish_kernel(total_rows, grams, own, z_hi, z_lo, out, work):
     peers = grams.shape[0]
     row = lax.broadcasted_iota(jnp.int32, (M, M), 0)
     col = lax.broadcasted_iota(jnp.int32, (M, M), 1)
@@ -398,7 +413,7 @@
     scale = lax.rsqrt(row_of(gram))
     second = inverse_factor(gram * scale * as_column(scale), work) * scale
     inverse = dot_f32(second, inverse)
-    change = (inverse * (norm * (total_rows**0.5))).T
+    change = (inverse * (norm * own[M + 1 : M + 2, :] * (total_rows**0.5))).T
     c_hi, c_lo = split(change)
     right = jnp.concatenate(
         [
@@ -411,26 +426,26 @@
 
     def rows_of(i, carry):
         at = pl.ds(pl.multiple_of(i * step, step), step)
-        value = z[at, :]
+        hi, lo = z_hi[at, :], z_lo[at, :]
         for part in range(2):
-            hi, lo = split(value[:, part * M : (part + 1) * M])
-            both = dot(jnp.concatenate([hi, lo], axis=1), right)
+            cols = slice(part * M, part * M + M)
+            both = dot(jnp.concatenate([hi[:, cols], lo[:, cols]], axis=1), right)
             out[part, at, :] = both[:, :M] + both[:, M:]
         return carry
 
-    lax.fori_loop(0, z.shape[0] // step, rows_of, 0, unroll=2)
-
-
-def finish(grams, z, total_rows):
+    lax.fori_loop(0, z_hi.shape[0] // step, rows_of, 0, unroll=True)
+
+
+def finish(grams, own, z_hi, z_lo, total_rows):
     return pl.pallas_call(
         partial(finish_kernel, total_rows),
-        out_shape=jax.ShapeDtypeStruct((2, z.shape[0], M), F32),
-        in_specs=[VMEM] * 2,
+        out_shape=jax.ShapeDtypeStruct((2, z_hi.shape[0], M), F32),
+        in_specs=[VMEM] * 4,
         out_specs=VMEM,
         scratch_shapes=[pltpu.VMEM((M, 2 * M), F32)],
         compiler_params=PARAMS,
         name="finish",
-    )(grams, z)
+    )(grams, own, z_hi, z_lo)
 
 
 def shifted(x, by):
@@ -439,45 +454,45 @@
     return lax.ppermute(x, "blk", pairs)
 
 
-def gathered(own):
+def swapped(x, far):
     peers = lax.axis_size("src")
-    chunks = [own]
+    return lax.ppermute(x, "src", [(i, i ^ far) for i in range(peers)])
+
+
+def gathered(own, ready):
+    peers = lax.axis_size("src")
     if peers & (peers - 1):
-        for k in range(1, peers):
-            chunks.append(lax.ppermute(own, "src", [(i, (i + k) % peers) for i in range(peers)]))
-        return chunks
+        chunks = [
+            lax.ppermute(own, "src", [(i, (i + k) % peers) for i in range(peers)])
+            for k in range(1, peers)
+        ]
+        return chunks, ready
     far = peers // 2
+    chunks = []
     while far:
-        pairs = [(i, i ^ far) for i in range(peers)]
-        chunks = chunks + [lax.ppermute(chunk, "src", pairs) for chunk in chunks]
+        if chunks:
+            chunks, ready = lax.optimization_barrier((chunks, ready))
+        chunks = chunks + [swapped(c, far) for c in [own] + chunks]
         far //= 2
-    if len(chunks) == 4:
-        chunks = [chunks[i] for i in (0, 2, 1, 3)]
-    return chunks
+    return chunks, ready
 
 
 def per_device(pupils, starts, counts, weights, start_block):
     regions = lax.axis_size("blk")
-    peers = lax.axis_size("src")
+    size = start_block.shape[1]
 
     own = pack(pupils, starts, counts, weights, regions * RB)
-    chunks = gathered(own)
-    edge = 2 * BLOCK
-    size = start_block.shape[1]
-    x_left = shifted(start_block[:, size - edge :], 1)
-    x_right = shifted(start_block[:, :edge], -1)
-
-    band = build(own, None)
-    band, x_left, x_right = lax.optimization_barrier((band, x_left, x_right))
-    for chunk in chunks[1:-1]:
+    ready = (build(own, None), *prepare(start_block))
+    chunks, ready = gathered(own, ready)
+    band, x_hi, x_lo = ready
+    for chunk in chunks[:-1]:
         band = build(chunk, band)
-    left_band, right_band = build_edges(chunks[-1], band)
-    left_band = shifted(left_band, 1)
-    right_band = shifted(right_band, -1)
-    band = build(chunks[-1], band)
-    z, grams = apply_twice(band, left_band, right_band, start_block, x_left, x_right)
-    grams = lax.all_gather(grams, "blk", axis=0)
-    return finish(grams, z, 2.0 * size * regions)
+    after, before = build_edges(chunks[-1], band, start_block)
+    left, right = shifted(after, 1), shifted(before, -1)
+    g_hi, g_lo = build(chunks[-1], band, last=True)
+    z_hi, z_lo, own_grams = apply_twice(g_hi, g_lo, left, right, x_hi, x_lo)
+    grams = lax.all_gather(own_grams, "blk", axis=0)
+    return finish(grams, own_grams, z_hi, z_lo, 2.0 * size * regions)
 
 
 def solution(mesh):

time: 65.2 us -> 61.9 us (0.949)
  starting transfers between devices: 11.4 us -> 9.24 us
  waiting for transfers between devices: 4.22 us -> 6.19 us
  Pallas kernels: 39.2 us -> 37.7 us
  local copies, waits for them, and re-layouts: 0.99 us -> 0.01 us
    ppermute x4 -> x2, starting transfers between devices: 5.31 us -> 2.94 us  [shifted(): return lax.ppermute(x, 'blk', pairs)]
    ppermute x3, waiting for transfers between devices: 4.21 us -> 6.19 us  [swapped(): return lax.ppermute(x, 'src', [(i, i ^ far) for i in range(peers)])]
    pallas_call x1, Pallas kernels: 9.36 us -> 8.06 us  [apply_twice(): pl.pallas_call(apply_kernel, out_shape=(jax.ShapeDtypeStruct((rows, 256),...]
    slice x1 -> x0, local copies, waits for them, and re-layouts: 0.99 us -> none  [per_device(): x_right = shifted(start_block[:, :edge], -1)]
    pallas_call x5 -> x6, Pallas kernels: 17 us -> 17.3 us  [the longest x4 16.5 us: build(): pl.pallas_call(partial(build_kernel, add, last), out_shape=out, in_specs=...]
  transfers between devices with their start and end apart: 7 -> 5, of which waited for: 1 -> 1; matrix products, arithmetic and copies ran while one was open for 2% -> 0% of each run, Pallas kernels for 25% -> 27%
where the time goes in v5:
time: 61.9 us; the launch traced here: 61.7 us
  Pallas kernels  37.7 us (61%)
  starting transfers between devices  9.24 us (15%)
  blocking collectives  8.47 us (14%)
  waiting for transfers between devices  6.19 us (10%)
    pallas_call x4, Pallas kernels, build(): pl.pallas_call(partial(build_kernel, add, last), out_shape=out, in_specs=...  16.5 us
    pallas_call x1, Pallas kernels, finish(): pl.pallas_call(partial(finish_kernel, total_rows), out_shape=jax.ShapeDty...  11.1 us
    all_gather x1, blocking collectives, per_device(): grams = lax.all_gather(own_grams, 'blk', axis=0)  8.47 us
    pallas_call x1, Pallas kernels, apply_twice(): pl.pallas_call(apply_kernel, out_shape=(jax.ShapeDtypeStruct((rows, 256),...  8.06 us
    ppermute x3, starting transfers between devices, swapped(): return lax.ppermute(x, 'src', [(i, i ^ far) for i in range(peers)])  6.29 us
    ppermute x3, waiting for transfers between devices, swapped(): return lax.ppermute(x, 'src', [(i, i ^ far) for i in range(peers)])  6.19 us
    ppermute x2, starting transfers between devices, shifted(): return lax.ppermute(x, 'blk', pairs)  2.94 us
  transfers between devices with their start and end apart: 5, of which 1 were waited for; matrix products, arithmetic and copies ran while one was open for 0% of the time, Pallas kernels for 27%

profile of v5, /device:TPU:0, one launch (start us, length us, event | category | flops | bytes accessed | tf_op | source)
XLA Modules:
  0.0 61.7 jit_solution(14868188495204004722)
XLA Ops:
  0.0 1.2 %pack.1.chunk = f32[520,128]{1,0:T(8,128)S(1)} custom-call(f32[512,128]{1,0:T(8,128)} %bitcast.6, s32[2,128]{1,0:T(2,128)} %bitcast.7, s32[2,128]{1,0:T(2,128)} %bitcast.8, f32[2,128]{1,0:T(2,128)} %bitcast.9), custom_call_target="tpu_custom_call" | custom-call | tf_op jit(solution)/shard_map/pack/pallas_call | solution.py:69
  1.2 0.0 copy-start
  1.2 4.1 %collective-permute-start = (f32[520,128]{1,0:T(8,128)S(1)}, f32[520,128]{1,0:T(8,128)S(1)}, u32[]{:S(2)}, u32[]{:S(2)}) collective-permute-start(f32[520,128]{1,0:T(8,128)S(1)} %pack.1.chunk), channel_id=1, source_target_pairs={{0,8},{4,12},{8,0},{12,4},{1,9},{5,13},{9,1},{13,5},{2,10},{6,14},... | collective-permute-start | bytes 798728 | tf_op jit(solution)/shard_map/ppermute | solution.py:459
  5.3 1.6 %collective-permute-start.2 = (f32[520,128]{1,0:T(8,128)S(1)}, f32[520,128]{1,0:T(8,128)S(1)}, u32[]{:S(2)}, u32[]{:S(2)}) collective-permute-start(f32[520,128]{1,0:T(8,128)S(1)} %pack.1.chunk), channel_id=1, source_target_pairs={{0,4},{4,0},{8,12},{12,8},{1,5},{5,1},{9,13},{13,9},{2,6},{6,2},{1... | collective-permute-start | bytes 798728 | tf_op jit(solution)/shard_map/ppermute | solution.py:459
  6.9 4.1 %band_terms.4.refs_0_ = f32[4096,256]{1,0:T(8,128)S(1)} custom-call(f32[520,128]{1,0:T(8,128)S(1)} %pack.1.chunk), custom_call_target="tpu_custom_call" | custom-call | flops 1048576 | bytes 65536 | tf_op jit(solution)/shard_map/band_terms/pallas_call | solution.py:148
  11.0 0.0 copy-done
  11.0 0.3 prepare.1
  11.4 6.2 %collective-permute-done.chunk = f32[520,128]{1,0:T(8,128)S(1)} collective-permute-done((f32[520,128]{1,0:T(8,128)S(1)}, f32[520,128]{1,0:T(8,128)S(1)}, u32[]{:S(2)}, u32[]{:S(2)}) %collective-permute-start) | collective-permute-done | bytes 266272 | tf_op jit(solution)/shard_map/ppermute | solution.py:459
  17.5 0.6 collective-permute-start.1
  18.2 4.1 %band_terms.5.refs_0_ = f32[4096,256]{1,0:T(8,128)S(1)} custom-call(f32[520,128]{1,0:T(8,128)S(1)} %collective-permute-done.chunk, f32[4096,256]{1,0:T(8,128)S(1)} %band_terms.4.refs_0_), custom_call_target="tpu_custom_call", output_to_operand_aliasing={{}: (1, {})} | custom-call | flops 1048576 | bytes 65536 | tf_op jit(solution)/shard_map/band_terms/pallas_call | solution.py:148
  22.3 0.0 collective-permute-done.2.chunk
  22.3 4.1 %band_terms.6.refs_0_.before = f32[4096,256]{1,0:T(8,128)S(1)} custom-call(f32[520,128]{1,0:T(8,128)S(1)} %collective-permute-done.2.chunk, f32[4096,256]{1,0:T(8,128)S(1)} %band_terms.5.refs_0_), custom_call_target="tpu_custom_call", output_to_operand_aliasing={{}: (1, {})} | custom-call | flops 1048576 | bytes 65536 | tf_op jit(solution)/shard_map/band_terms/pallas_call | solution.py:148
  26.4 0.0 collective-permute-done.1.chunk
  26.4 0.6 edge_terms.1
  27.0 1.7 %collective-permute-start.3 = (f32[320,256]{1,0:T(8,128)S(1)}, f32[320,256]{1,0:T(8,128)S(1)}, u32[]{:S(2)}, u32[]{:S(2)}) collective-permute-start(f32[320,256]{1,0:T(8,128)S(1)} %get-tuple-element.24), channel_id=1, source_target_pairs={{0,1},{1,2},{2,3},{4,5},{5,6},{6,7},{8,9},{9,10},{10,11},{12,13},{... | collective-permute-start | bytes 983048 | tf_op jit(solution)/shard_map/ppermute | solution.py:454
  28.7 1.3 %collective-permute-start.4 = (f32[192,256]{1,0:T(8,128)S(1)}, f32[192,256]{1,0:T(8,128)S(1)}, u32[]{:S(2)}, u32[]{:S(2)}) collective-permute-start(f32[192,256]{1,0:T(8,128)S(1)} %get-tuple-element.25), channel_id=1, source_target_pairs={{1,0},{2,1},{3,2},{5,4},{6,5},{7,6},{9,8},{10,9},{11,10},{13,12},{... | collective-permute-start | bytes 589832 | tf_op jit(solution)/shard_map/ppermute | solution.py:454
  30.0 4.1 %band_terms.7 = (bf16[4096,256]{1,0:T(8,128)(2,1)S(1)}, bf16[4096,256]{1,0:T(8,128)(2,1)S(1)}) custom-call(f32[520,128]{1,0:T(8,128)S(1)} %collective-permute-done.1.chunk, f32[4096,256]{1,0:T(8,128)S(1)} %band_terms.6.refs_0_.before), custom_call_target="tpu_custom_call" | custom-call | flops 1048576 | bytes 65536 | tf_op jit(solution)/shard_map/band_terms/pallas_call | solution.py:148
  34.1 0.0 collective-permute-done.4.right
  34.1 0.0 collective-permute-done.3.left
  34.1 8.1 %apply_twice.1 = (bf16[2048,256]{1,0:T(8,128)(2,1)S(1)}, bf16[2048,256]{1,0:T(8,128)(2,1)S(1)}, f32[136,128]{1,0:T(8,128)S(1)}) custom-call(bf16[4096,256]{1,0:T(8,128)(2,1)S(1)} %get-tuple-element.22.g_hi, bf16[4096,256]{1,0:T(8,128)(2,1)S(1)} %get-tuple-element.23.g_lo, f32[320,256]{1,0:T(8,128)S(1)} %collective-permute-done.3.left, ...), custom_call_target="tpu_custom_call" | custom-call | flops 3221225472 | bytes 12582912 | tf_op jit(solution)/shard_map/apply_twice/pallas_call | solution.py:305
  42.2 8.5 %all-gather = f32[544,128]{1,0:T(8,128)S(1)} all-gather(f32[136,128]{1,0:T(8,128)S(1)} %get-tuple-element.28.own), channel_id=2, replica_groups=mesh['groups'=2,'src'=4,'blk'=4] {'blk'}, dimensions={0}, use_global_device_ids=true | all-gather | bytes 348160 | tf_op jit(solution)/shard_map/all_gather | solution.py:494
  50.6 11.1 %finish.1 = f32[2,2048,128]{2,1,0:T(8,128)} custom-call(f32[4,136,128]{2,1,0:T(8,128)S(1)} %bitcast.5, f32[136,128]{1,0:T(8,128)S(1)} %get-tuple-element.28.own, bf16[2048,256]{1,0:T(8,128)(2,1)S(1)} %get-tuple-element.29.z_hi, bf16[2048,256]{1,0:T(8,128)(2,1)S(1)} %get-tuple-element.30.z_lo), custom_call_target="tpu_custom_call" | custom-call | tf_op jit(solution)/shard_map/finish/pallas_call | solution.py:440
Async XLA Ops:
  1.2 9.8 %copy-start = (f32[2,2048,128]{2,1,0:T(8,128)S(1)}, f32[2,2048,128]{2,1,0:T(8,128)}, u32[]{:S(2)}) copy-start(f32[2,2048,128]{2,1,0:T(8,128)} %x.3) | copy-start | bytes 6291460
  1.2 16.3 %collective-permute-start = (f32[520,128]{1,0:T(8,128)S(1)}, f32[520,128]{1,0:T(8,128)S(1)}, u32[]{:S(2)}, u32[]{:S(2)}) collective-permute-start(f32[520,128]{1,0:T(8,128)S(1)} %pack.1.chunk), channel_id=1, source_target_pairs={{0,8},{4,12},{8,0},{12,4},{1,9},{5,13},{9,1},{13,5},{2,10},{6,14},... | collective-permute-start | bytes 798728 | tf_op jit(solution)/shard_map/ppermute | solution.py:459
  5.3 17.0 %collective-permute-start.2 = (f32[520,128]{1,0:T(8,128)S(1)}, f32[520,128]{1,0:T(8,128)S(1)}, u32[]{:S(2)}, u32[]{:S(2)}) collective-permute-start(f32[520,128]{1,0:T(8,128)S(1)} %pack.1.chunk), channel_id=1, source_target_pairs={{0,4},{4,0},{8,12},{12,8},{1,5},{5,1},{9,13},{13,9},{2,6},{6,2},{1... | collective-permute-start | bytes 798728 | tf_op jit(solution)/shard_map/ppermute | solution.py:459
  17.5 8.9 %collective-permute-start.1 = (f32[520,128]{1,0:T(8,128)S(1)}, f32[520,128]{1,0:T(8,128)S(1)}, u32[]{:S(2)}, u32[]{:S(2)}) collective-permute-start(f32[520,128]{1,0:T(8,128)S(1)} %collective-permute-done.chunk), channel_id=1, source_target_pairs={{0,4},{4,0},{8,12},{12,8},{1,5},{5,1},{9,13},{13,9},{2,6},{6,2},{1... | collective-permute-start | bytes 798728 | tf_op jit(solution)/shard_map/ppermute | solution.py:459
  27.0 7.1 %collective-permute-start.3 = (f32[320,256]{1,0:T(8,128)S(1)}, f32[320,256]{1,0:T(8,128)S(1)}, u32[]{:S(2)}, u32[]{:S(2)}) collective-permute-start(f32[320,256]{1,0:T(8,128)S(1)} %get-tuple-element.24), channel_id=1, source_target_pairs={{0,1},{1,2},{2,3},{4,5},{5,6},{6,7},{8,9},{9,10},{10,11},{12,13},{... | collective-permute-start | bytes 983048 | tf_op jit(solution)/shard_map/ppermute | solution.py:454
  28.7 5.4 %collective-permute-start.4 = (f32[192,256]{1,0:T(8,128)S(1)}, f32[192,256]{1,0:T(8,128)S(1)}, u32[]{:S(2)}, u32[]{:S(2)}) collective-permute-start(f32[192,256]{1,0:T(8,128)S(1)} %get-tuple-element.25), channel_id=1, source_target_pairs={{1,0},{2,1},{3,2},{5,4},{6,5},{7,6},{9,8},{10,9},{11,10},{13,12},{... | collective-permute-start | bytes 589832 | tf_op jit(solution)/shard_map/ppermute | solution.py:454

commit v6 on v5

--- a/solution.py
+++ b/solution.py
@@ -97,17 +97,22 @@
     count = (chunk.shape[0] - 8) // 2
     real = chunk[:count, :]
     imag = chunk[count : 2 * count, :]
-    right = jnp.concatenate(
-        [
-            jnp.concatenate([real, -imag], axis=1),
-            jnp.concatenate([imag, real], axis=1),
-        ],
-        axis=0,
-    )
-    left = jnp.concatenate([real.T, imag.T], axis=1)
+    left = jnp.concatenate([real.T, imag.T], axis=1).astype(BF16)
+    right = []
+    for scale, real, imag in zip((0.5, 1.0), split(real), split(imag)):
+        right.append(
+            jnp.concatenate(
+                [
+                    jnp.concatenate([real, -imag], axis=1),
+                    jnp.concatenate([imag, real], axis=1),
+                ],
+                axis=0,
+            )
+            * jnp.asarray(scale, BF16)
+        )
     places = [chunk[2 * count + t : 2 * count + t + 1, :] for t in range(count // 128)]
     place = jnp.broadcast_to(jnp.concatenate(places + places, axis=1), (16, 2 * count))
-    return split(left), split(right), place
+    return left, right[0], right[1], place
 
 
 def at_block(part, place, b):
@@ -115,24 +120,32 @@
     return (part.reshape(8, 16, -1) * mask).reshape(part.shape)
 
 
+def hermitian(q):
+    real, imag = q[:, :128], q[:, 128:]
+    return jnp.concatenate([real + real.T, imag - imag.T], axis=1)
+
+
 def build_kernel(add, last, chunk, *refs):
     refs = list(refs)
     before = refs.pop(0) if add else None
-    lhs_lo, lhs_hi = refs.pop(), refs.pop()
-    (left_hi, left_lo), (right_hi, right_lo), place = factors(chunk)
+    lhs = refs.pop()
+    left, right_hi, right_lo, place = factors(chunk)
 
     def one_group(g, carry):
         for j in range(GROUP):
             b = (g * GROUP + j).astype(F32)
-            lhs_hi[j * 128 : (j + 1) * 128, :] = at_block(left_hi, place, b)
-            lhs_lo[j * 128 : (j + 1) * 128, :] = at_block(left_lo, place, b)
+            lhs[j * 128 : (j + 1) * 128, :] = at_block(left, place, b)
         at = pl.ds(pl.multiple_of(g * GROUP * 128, GROUP * 128), GROUP * 128)
-        hi = lhs_hi[...]
-        total = dot(hi, right_hi) + dot(hi, right_lo) + dot(lhs_lo[...], right_hi)
+        hi = lhs[...]
+        total = dot(hi, right_hi) + dot(hi, right_lo)
         if add:
             total = before[at, :] + total
         if last:
-            refs[0][at, :], refs[1][at, :] = split(total)
+            for j in range(GROUP):
+                one = pl.ds(pl.multiple_of((g * GROUP + j) * 128, 128), 128)
+                refs[0][one, :], refs[1][one, :] = split(
+                    hermitian(total[j * 128 : (j + 1) * 128, :])
+                )
         else:
             refs[0][at, :] = total
         return carry
@@ -150,7 +163,7 @@
         out_shape=out,
         in_specs=[VMEM] * (1 + add),
         out_specs=[VMEM] * len(out),
-        scratch_shapes=[pltpu.VMEM((GROUP * 128, 2 * count), BF16)] * 2,
+        scratch_shapes=[pltpu.VMEM((GROUP * 128, 2 * count), BF16)],
         input_output_aliases={1: 0} if add and not last else {},
         compiler_params=PARAMS,
         cost_estimate=pl.CostEstimate(
@@ -166,13 +179,18 @@
 
 
 def edge_kernel(chunk, before, x, after_out, before_out):
-    (left_hi, left_lo), (right_hi, right_lo), place = factors(chunk)
-    hi = jnp.concatenate([at_block(left_hi, place, float(b)) for b in (0, RB - 2, RB - 1)], axis=0)
-    lo = jnp.concatenate([at_block(left_lo, place, float(b)) for b in (0, RB - 2, RB - 1)], axis=0)
-    total = dot(hi, right_hi) + dot(hi, right_lo) + dot(lo, right_hi)
-    after_out[: 3 * BLOCK, :] = before[RB * 128 - 192 :, :] + total[192:]
+    left, right_hi, right_lo, place = factors(chunk)
+    blocks = (0, RB - 2, RB - 1)
+    left = jnp.concatenate([at_block(left, place, float(b)) for b in blocks], axis=0)
+    total = dot(left, right_hi) + dot(left, right_lo)
+    first, second, third = [
+        hermitian(before[b * 128 : (b + 1) * 128, :] + total[i * 128 : (i + 1) * 128, :])
+        for i, b in enumerate(blocks)
+    ]
+    after_out[:BLOCK, :] = second[BLOCK:, :]
+    after_out[BLOCK : 3 * BLOCK, :] = third
     after_out[3 * BLOCK :, :] = wide(x[:, x.shape[1] - 2 * BLOCK :, :])
-    before_out[:BLOCK, :] = before[:BLOCK, :] + total[:BLOCK]
+    before_out[:BLOCK, :] = first[:BLOCK, :]
     before_out[BLOCK:, :] = wide(x[:, : 2 * BLOCK, :])
 
 

time: 61.9 us -> 59.9 us (0.968)
  Pallas kernels: 37.7 us -> 33.4 us
  waiting for transfers between devices: 6.19 us -> 8.4 us
    pallas_call x4, Pallas kernels: 16.5 us -> 12.2 us  [build(): pl.pallas_call(partial(build_kernel, add, last), out_shape=out, in_specs=...]
    ppermute x3, waiting for transfers between devices: 6.19 us -> 8.22 us  [swapped(): return lax.ppermute(x, 'src', [(i, i ^ far) for i in range(peers)])]
  transfers between devices with their start and end apart: 5 -> 5, of which waited for: 1 -> 3; matrix products, arithmetic and copies ran while one was open for 0% -> 0% of each run, Pallas kernels for 27% -> 21%
where the time goes in v6:
time: 59.9 us; the launch traced here: 59.7 us
  Pallas kernels  33.4 us (56%)
  starting transfers between devices  8.9 us (15%)
  blocking collectives  8.87 us (15%)
  waiting for transfers between devices  8.4 us (14%)
    pallas_call x4, Pallas kernels, build(): pl.pallas_call(partial(build_kernel, add, last), out_shape=out, in_specs=...  12.2 us
    pallas_call x1, Pallas kernels, finish(): pl.pallas_call(partial(finish_kernel, total_rows), out_shape=jax.ShapeDty...  11.1 us
    all_gather x1, blocking collectives, per_device(): grams = lax.all_gather(own_grams, 'blk', axis=0)  8.87 us
    ppermute x3, waiting for transfers between devices, swapped(): return lax.ppermute(x, 'src', [(i, i ^ far) for i in range(peers)])  8.22 us
    pallas_call x1, Pallas kernels, apply_twice(): pl.pallas_call(apply_kernel, out_shape=(jax.ShapeDtypeStruct((rows, 256),...  8.04 us
    ppermute x3, starting transfers between devices, swapped(): return lax.ppermute(x, 'src', [(i, i ^ far) for i in range(peers)])  6.29 us
    ppermute x2, starting transfers between devices, shifted(): return lax.ppermute(x, 'blk', pairs)  2.6 us
    pallas_call x1, Pallas kernels, pack(): pl.pallas_call(partial(pack_kernel, total_blocks), out_shape=jax.ShapeDty...  1.22 us
  transfers between devices with their start and end apart: 5, of which 3 were waited for; matrix products, arithmetic and copies ran while one was open for 0% of the time, Pallas kernels for 21%

profile of v6, /device:TPU:0, one launch (start us, length us, event | category | flops | bytes accessed | tf_op | source)
XLA Modules:
  0.0 59.7 jit_solution(1284376805033318668)
XLA Ops:
  0.0 1.2 %pack.1.chunk = f32[520,128]{1,0:T(8,128)S(1)} custom-call(f32[512,128]{1,0:T(8,128)} %bitcast.6, s32[2,128]{1,0:T(2,128)} %bitcast.7, s32[2,128]{1,0:T(2,128)} %bitcast.8, f32[2,128]{1,0:T(2,128)} %bitcast.9), custom_call_target="tpu_custom_call" | custom-call | tf_op jit(solution)/shard_map/pack/pallas_call | solution.py:69
  1.2 0.0 copy-start
  1.2 4.1 %collective-permute-start = (f32[520,128]{1,0:T(8,128)S(1)}, f32[520,128]{1,0:T(8,128)S(1)}, u32[]{:S(2)}, u32[]{:S(2)}) collective-permute-start(f32[520,128]{1,0:T(8,128)S(1)} %pack.1.chunk), channel_id=1, source_target_pairs={{0,8},{4,12},{8,0},{12,4},{1,9},{5,13},{9,1},{13,5},{2,10},{6,14},... | collective-permute-start | bytes 798728 | tf_op jit(solution)/shard_map/ppermute | solution.py:477
  5.3 1.6 %collective-permute-start.2 = (f32[520,128]{1,0:T(8,128)S(1)}, f32[520,128]{1,0:T(8,128)S(1)}, u32[]{:S(2)}, u32[]{:S(2)}) collective-permute-start(f32[520,128]{1,0:T(8,128)S(1)} %pack.1.chunk), channel_id=1, source_target_pairs={{0,4},{4,0},{8,12},{12,8},{1,5},{5,1},{9,13},{13,9},{2,6},{6,2},{1... | collective-permute-start | bytes 798728 | tf_op jit(solution)/shard_map/ppermute | solution.py:477
  6.9 3.0 %band_terms.4.refs_0_ = f32[4096,256]{1,0:T(8,128)S(1)} custom-call(f32[520,128]{1,0:T(8,128)S(1)} %pack.1.chunk), custom_call_target="tpu_custom_call" | custom-call | flops 1048576 | bytes 65536 | tf_op jit(solution)/shard_map/band_terms/pallas_call | solution.py:161
  9.9 0.0 copy-done
  9.9 0.3 prepare.1
  10.2 7.3 %collective-permute-done.chunk = f32[520,128]{1,0:T(8,128)S(1)} collective-permute-done((f32[520,128]{1,0:T(8,128)S(1)}, f32[520,128]{1,0:T(8,128)S(1)}, u32[]{:S(2)}, u32[]{:S(2)}) %collective-permute-start) | collective-permute-done | bytes 266272 | tf_op jit(solution)/shard_map/ppermute | solution.py:477
  17.5 0.6 %collective-permute-start.1 = (f32[520,128]{1,0:T(8,128)S(1)}, f32[520,128]{1,0:T(8,128)S(1)}, u32[]{:S(2)}, u32[]{:S(2)}) collective-permute-start(f32[520,128]{1,0:T(8,128)S(1)} %collective-permute-done.chunk), channel_id=1, source_target_pairs={{0,4},{4,0},{8,12},{12,8},{1,5},{5,1},{9,13},{13,9},{2,6},{6,2},{1... | collective-permute-start | bytes 798728 | tf_op jit(solution)/shard_map/ppermute | solution.py:477
  18.2 3.0 %band_terms.5.refs_0_ = f32[4096,256]{1,0:T(8,128)S(1)} custom-call(f32[520,128]{1,0:T(8,128)S(1)} %collective-permute-done.chunk, f32[4096,256]{1,0:T(8,128)S(1)} %band_terms.4.refs_0_), custom_call_target="tpu_custom_call", output_to_operand_aliasing={{}: (1, {})} | custom-call | flops 1048576 | bytes 65536 | tf_op jit(solution)/shard_map/band_terms/pallas_call | solution.py:161
  21.2 0.0 collective-permute-done.2.chunk
  21.2 3.0 %band_terms.6.refs_0_.before = f32[4096,256]{1,0:T(8,128)S(1)} custom-call(f32[520,128]{1,0:T(8,128)S(1)} %collective-permute-done.2.chunk, f32[4096,256]{1,0:T(8,128)S(1)} %band_terms.5.refs_0_), custom_call_target="tpu_custom_call", output_to_operand_aliasing={{}: (1, {})} | custom-call | flops 1048576 | bytes 65536 | tf_op jit(solution)/shard_map/band_terms/pallas_call | solution.py:161
  24.2 0.9 %collective-permute-done.1.chunk = f32[520,128]{1,0:T(8,128)S(1)} collective-permute-done((f32[520,128]{1,0:T(8,128)S(1)}, f32[520,128]{1,0:T(8,128)S(1)}, u32[]{:S(2)}, u32[]{:S(2)}) %collective-permute-start.1) | collective-permute-done | bytes 266272 | tf_op jit(solution)/shard_map/ppermute | solution.py:477
  25.1 0.5 edge_terms.1
  25.6 1.3 %collective-permute-start.3 = (f32[320,256]{1,0:T(8,128)S(1)}, f32[320,256]{1,0:T(8,128)S(1)}, u32[]{:S(2)}, u32[]{:S(2)}) collective-permute-start(f32[320,256]{1,0:T(8,128)S(1)} %get-tuple-element.24), channel_id=1, source_target_pairs={{0,1},{1,2},{2,3},{4,5},{5,6},{6,7},{8,9},{9,10},{10,11},{12,13},{... | collective-permute-start | bytes 983048 | tf_op jit(solution)/shard_map/ppermute | solution.py:472
  26.9 1.3 %collective-permute-start.4 = (f32[192,256]{1,0:T(8,128)S(1)}, f32[192,256]{1,0:T(8,128)S(1)}, u32[]{:S(2)}, u32[]{:S(2)}) collective-permute-start(f32[192,256]{1,0:T(8,128)S(1)} %get-tuple-element.25), channel_id=1, source_target_pairs={{1,0},{2,1},{3,2},{5,4},{6,5},{7,6},{9,8},{10,9},{11,10},{13,12},{... | collective-permute-start | bytes 589832 | tf_op jit(solution)/shard_map/ppermute | solution.py:472
  28.2 3.3 %band_terms.7 = (bf16[4096,256]{1,0:T(8,128)(2,1)S(1)}, bf16[4096,256]{1,0:T(8,128)(2,1)S(1)}) custom-call(f32[520,128]{1,0:T(8,128)S(1)} %collective-permute-done.1.chunk, f32[4096,256]{1,0:T(8,128)S(1)} %band_terms.6.refs_0_.before), custom_call_target="tpu_custom_call" | custom-call | flops 1048576 | bytes 65536 | tf_op jit(solution)/shard_map/band_terms/pallas_call | solution.py:161
  31.5 0.2 collective-permute-done.4.right
  31.7 0.0 collective-permute-done.3.left
  31.7 8.0 %apply_twice.1 = (bf16[2048,256]{1,0:T(8,128)(2,1)S(1)}, bf16[2048,256]{1,0:T(8,128)(2,1)S(1)}, f32[136,128]{1,0:T(8,128)S(1)}) custom-call(bf16[4096,256]{1,0:T(8,128)(2,1)S(1)} %get-tuple-element.22.g_hi, bf16[4096,256]{1,0:T(8,128)(2,1)S(1)} %get-tuple-element.23.g_lo, f32[320,256]{1,0:T(8,128)S(1)} %collective-permute-done.3.left, ...), custom_call_target="tpu_custom_call" | custom-call | flops 3221225472 | bytes 12582912 | tf_op jit(solution)/shard_map/apply_twice/pallas_call | solution.py:323
  39.7 8.9 %all-gather = f32[544,128]{1,0:T(8,128)S(1)} all-gather(f32[136,128]{1,0:T(8,128)S(1)} %get-tuple-element.28.own), channel_id=2, replica_groups=mesh['groups'=2,'src'=4,'blk'=4] {'blk'}, dimensions={0}, use_global_device_ids=true | all-gather | bytes 348160 | tf_op jit(solution)/shard_map/all_gather | solution.py:512
  48.6 11.1 %finish.1 = f32[2,2048,128]{2,1,0:T(8,128)} custom-call(f32[4,136,128]{2,1,0:T(8,128)S(1)} %bitcast.5, f32[136,128]{1,0:T(8,128)S(1)} %get-tuple-element.28.own, bf16[2048,256]{1,0:T(8,128)(2,1)S(1)} %get-tuple-element.29.z_hi, bf16[2048,256]{1,0:T(8,128)(2,1)S(1)} %get-tuple-element.30.z_lo), custom_call_target="tpu_custom_call" | custom-call | tf_op jit(solution)/shard_map/finish/pallas_call | solution.py:458
Async XLA Ops:
  1.2 8.7 %copy-start = (f32[2,2048,128]{2,1,0:T(8,128)S(1)}, f32[2,2048,128]{2,1,0:T(8,128)}, u32[]{:S(2)}) copy-start(f32[2,2048,128]{2,1,0:T(8,128)} %x.3) | copy-start | bytes 6291460
  1.2 16.3 %collective-permute-start = (f32[520,128]{1,0:T(8,128)S(1)}, f32[520,128]{1,0:T(8,128)S(1)}, u32[]{:S(2)}, u32[]{:S(2)}) collective-permute-start(f32[520,128]{1,0:T(8,128)S(1)} %pack.1.chunk), channel_id=1, source_target_pairs={{0,8},{4,12},{8,0},{12,4},{1,9},{5,13},{9,1},{13,5},{2,10},{6,14},... | collective-permute-start | bytes 798728 | tf_op jit(solution)/shard_map/ppermute | solution.py:477
  5.3 15.8 %collective-permute-start.2 = (f32[520,128]{1,0:T(8,128)S(1)}, f32[520,128]{1,0:T(8,128)S(1)}, u32[]{:S(2)}, u32[]{:S(2)}) collective-permute-start(f32[520,128]{1,0:T(8,128)S(1)} %pack.1.chunk), channel_id=1, source_target_pairs={{0,4},{4,0},{8,12},{12,8},{1,5},{5,1},{9,13},{13,9},{2,6},{6,2},{1... | collective-permute-start | bytes 798728 | tf_op jit(solution)/shard_map/ppermute | solution.py:477
  17.5 7.5 %collective-permute-start.1 = (f32[520,128]{1,0:T(8,128)S(1)}, f32[520,128]{1,0:T(8,128)S(1)}, u32[]{:S(2)}, u32[]{:S(2)}) collective-permute-start(f32[520,128]{1,0:T(8,128)S(1)} %collective-permute-done.chunk), channel_id=1, source_target_pairs={{0,4},{4,0},{8,12},{12,8},{1,5},{5,1},{9,13},{13,9},{2,6},{6,2},{1... | collective-permute-start | bytes 798728 | tf_op jit(solution)/shard_map/ppermute | solution.py:477
  25.6 6.1 %collective-permute-start.3 = (f32[320,256]{1,0:T(8,128)S(1)}, f32[320,256]{1,0:T(8,128)S(1)}, u32[]{:S(2)}, u32[]{:S(2)}) collective-permute-start(f32[320,256]{1,0:T(8,128)S(1)} %get-tuple-element.24), channel_id=1, source_target_pairs={{0,1},{1,2},{2,3},{4,5},{5,6},{6,7},{8,9},{9,10},{10,11},{12,13},{... | collective-permute-start | bytes 983048 | tf_op jit(solution)/shard_map/ppermute | solution.py:472
  26.9 4.8 %collective-permute-start.4 = (f32[192,256]{1,0:T(8,128)S(1)}, f32[192,256]{1,0:T(8,128)S(1)}, u32[]{:S(2)}, u32[]{:S(2)}) collective-permute-start(f32[192,256]{1,0:T(8,128)S(1)} %get-tuple-element.25), channel_id=1, source_target_pairs={{1,0},{2,1},{3,2},{5,4},{6,5},{7,6},{9,8},{10,9},{11,10},{13,12},{... | collective-permute-start | bytes 589832 | tf_op jit(solution)/shard_map/ppermute | solution.py:472

commit v7 on v6

--- a/solution.py
+++ b/solution.py
@@ -9,8 +9,7 @@
 
 BLOCK = 64
 RB = 32
-GROUP = 8
-UNROLL = 8
+GROUP = 2
 OUTER = 64
 M = 128
 F32 = jnp.float32
@@ -150,7 +149,7 @@
             refs[0][at, :] = total
         return carry
 
-    lax.fori_loop(0, RB // GROUP, one_group, 0)
+    lax.fori_loop(0, RB // GROUP, one_group, 0, unroll=RB // GROUP)
 
 
 def build(chunk, before, last=False):
@@ -220,11 +219,12 @@
 
 
 def gram_of(hi, lo):
-    a = dot_t(hi, hi)
-    b = dot_t(hi, lo)
-    a = a[:M, :M] + a[M:, M:]
-    b = b[:M, :M] + b[M:, M:]
-    return a + b + b.T
+    half = jnp.asarray(0.5, BF16)
+    q = 0.0
+    for cols in (slice(0, M), slice(M, 2 * M)):
+        q += dot_t(hi[:, cols], jnp.concatenate([hi[:, cols] * half, lo[:, cols]], axis=1))
+    q = q[:, :M] + q[:, M:]
+    return q + q.T
 
 
 def prepare_kernel(x, hi_out, lo_out):
@@ -278,9 +278,8 @@
         put(b + 1, block)
         return both[BLOCK:], jnp.maximum(top, jnp.abs(block))
 
-    spill, top = lax.fori_loop(
-        0, RB - 1, first, (both[BLOCK:], jnp.abs(first_block)), unroll=UNROLL
-    )
+    carry = first(0, (both[BLOCK:], jnp.abs(first_block)))
+    spill, top = lax.fori_loop(1, RB - 1, first, carry, unroll=RB - 2)
     both = times(
         g_hi[(RB - 1) * 128 :, :],
         g_lo[(RB - 1) * 128 :, :],
@@ -309,7 +308,7 @@
         return both[BLOCK:]
 
     spill = times(left_hi[2 * BLOCK :], left_lo[2 * BLOCK :], p_hi[:128, :], p_lo[:128, :])
-    lax.fori_loop(0, RB, second, spill, unroll=UNROLL)
+    lax.fori_loop(0, RB, second, spill, unroll=RB // 2)
     gram_2 = gram_of(z_hi[...], z_lo[...])
     row = lax.broadcasted_iota(jnp.int32, (M, M), 0)
     col = lax.broadcasted_iota(jnp.int32, (M, M), 1)
@@ -349,21 +348,25 @@
     def line(x, j):
         return x[j : j + 1, :]
 
-    def wide(x, j):
+    def tall(x, j):
         return jnp.broadcast_to(line(x, j), (8, M))
+
+    def spread(x, at):
+        return [jnp.broadcast_to(x[:, at + k : at + k + 1], (8, M)) for k in range(8)]
 
     for top in range(0, M, OUTER):
         left = [work[top + 8 * g : top + 8 * g + 8, :M] for g in range(groups)]
         right = [work[top + 8 * g : top + 8 * g + 8, M:] for g in range(groups)]
+        ahead = spread(left[0], top)
         for q in range(groups):
             at = top + 8 * q
-            cols = {
-                g: [jnp.broadcast_to(left[g][:, at + k : at + k + 1], (8, M)) for k in range(8)]
-                for g in range(q, groups)
-            }
+            cols = {q: ahead, **{g: spread(left[g], at) for g in range(q + 1, groups)}}
+            more = q + 1 < groups
+            if more:
+                ahead, mine = spread(left[q + 1], at + 8), spread(left[q], at + 8)
             scales = jnp.zeros((8, M), F32)
             for j in range(0, 8, 2):
-                a0, a1, a2 = wide(cols[q][j], j), wide(cols[q][j], j + 1), wide(cols[q][j + 1], j + 1)
+                a0, a1, a2 = tall(cols[q][j], j), tall(cols[q][j], j + 1), tall(cols[q][j + 1], j + 1)
                 det = a0 * a2 - a1 * a1
                 inverse = pltpu.reciprocal(det, approx=False)
                 root = lax.rsqrt(a0)
@@ -374,6 +377,9 @@
                 row_1 = [line(cols[q][k], j + 1) for k in range(8)]
                 left_0, left_1 = line(left[q], j), line(left[q], j + 1)
                 right_0, right_1 = line(right[q], j), line(right[q], j + 1)
+                if more:
+                    mine_0 = [line(x, j) for x in mine]
+                    mine_1 = [line(x, j + 1) for x in mine]
                 for g in range(q, groups):
                     c0, c1 = cols[g][j], cols[g][j + 1]
                     y0 = a2 * c0 - a1 * c1
@@ -388,6 +394,10 @@
                         x0 = jnp.where(sub == j + 1, ratio, x0)
                     left[g] = left[g] - (x0 * left_0 + x1 * left_1)
                     right[g] = right[g] - (x0 * right_0 + x1 * right_1)
+                    if more and g <= q + 1:
+                        part = mine if g == q else ahead
+                        for k in range(8):
+                            part[k] = part[k] - (x0 * mine_0[k] + x1 * mine_1[k])
             left[q] = left[q] * scales
             right[q] = right[q] * scales
         for g in range(groups):

time: 59.9 us -> 55.9 us (0.933)
  Pallas kernels: 33.4 us -> 27.3 us
  waiting for transfers between devices: 8.4 us -> 10.3 us
    pallas_call x1, Pallas kernels: 8.04 us -> 5.62 us  [apply_twice(): pl.pallas_call(apply_kernel, out_shape=(jax.ShapeDtypeStruct((rows, 256),...]
    pallas_call x4, Pallas kernels: 12.2 us -> 10.1 us  [build(): pl.pallas_call(partial(build_kernel, add, last), out_shape=out, in_specs=...]
    pallas_call x1, Pallas kernels: 11.1 us -> 9.5 us  [finish(): pl.pallas_call(partial(finish_kernel, total_rows), out_shape=jax.ShapeDty...]
    ppermute x3, waiting for transfers between devices: 8.22 us -> 9.63 us  [swapped(): return lax.ppermute(x, 'src', [(i, i ^ far) for i in range(peers)])]
  transfers between devices with their start and end apart: 5 -> 5, of which waited for: 3 -> 3; matrix products, arithmetic and copies ran while one was open for 0% -> 0% of each run, Pallas kernels for 21% -> 19%
where the time goes in v7:
time: 55.9 us; the launch traced here: 55.7 us
  Pallas kernels  27.3 us (49%)
  waiting for transfers between devices  10.3 us (18%)
  starting transfers between devices  9.08 us (16%)
  blocking collectives  8.89 us (16%)
    pallas_call x4, Pallas kernels, build(): pl.pallas_call(partial(build_kernel, add, last), out_shape=out, in_specs=...  10.1 us
    ppermute x3, waiting for transfers between devices, swapped(): return lax.ppermute(x, 'src', [(i, i ^ far) for i in range(peers)])  9.63 us
    pallas_call x1, Pallas kernels, finish(): pl.pallas_call(partial(finish_kernel, total_rows), out_shape=jax.ShapeDty...  9.5 us
    all_gather x1, blocking collectives, per_device(): grams = lax.all_gather(own_grams, 'blk', axis=0)  8.89 us
    ppermute x3, starting transfers between devices, swapped(): return lax.ppermute(x, 'src', [(i, i ^ far) for i in range(peers)])  6.29 us
    pallas_call x1, Pallas kernels, apply_twice(): pl.pallas_call(apply_kernel, out_shape=(jax.ShapeDtypeStruct((rows, 256),...  5.62 us
    ppermute x2, starting transfers between devices, shifted(): return lax.ppermute(x, 'blk', pairs)  2.78 us
    pallas_call x1, Pallas kernels, pack(): pl.pallas_call(partial(pack_kernel, total_blocks), out_shape=jax.ShapeDty...  1.22 us
  transfers between devices with their start and end apart: 5, of which 3 were waited for; matrix products, arithmetic and copies ran while one was open for 0% of the time, Pallas kernels for 19%

profile of v7, /device:TPU:0, one launch (start us, length us, event | category | flops | bytes accessed | tf_op | source)
XLA Modules:
  0.0 55.7 jit_solution(1554344191609087611)
XLA Ops:
  0.0 1.2 %pack.1.chunk = f32[520,128]{1,0:T(8,128)S(1)} custom-call(f32[512,128]{1,0:T(8,128)} %bitcast.6, s32[2,128]{1,0:T(2,128)} %bitcast.7, s32[2,128]{1,0:T(2,128)} %bitcast.8, f32[2,128]{1,0:T(2,128)} %bitcast.9), custom_call_target="tpu_custom_call" | custom-call | tf_op jit(solution)/shard_map/pack/pallas_call | solution.py:68
  1.2 0.0 copy-start
  1.2 4.1 %collective-permute-start = (f32[520,128]{1,0:T(8,128)S(1)}, f32[520,128]{1,0:T(8,128)S(1)}, u32[]{:S(2)}, u32[]{:S(2)}) collective-permute-start(f32[520,128]{1,0:T(8,128)S(1)} %pack.1.chunk), channel_id=1, source_target_pairs={{0,8},{4,12},{8,0},{12,4},{1,9},{5,13},{9,1},{13,5},{2,10},{6,14},... | collective-permute-start | bytes 798728 | tf_op jit(solution)/shard_map/ppermute | solution.py:487
  5.3 1.6 %collective-permute-start.2 = (f32[520,128]{1,0:T(8,128)S(1)}, f32[520,128]{1,0:T(8,128)S(1)}, u32[]{:S(2)}, u32[]{:S(2)}) collective-permute-start(f32[520,128]{1,0:T(8,128)S(1)} %pack.1.chunk), channel_id=1, source_target_pairs={{0,4},{4,0},{8,12},{12,8},{1,5},{5,1},{9,13},{13,9},{2,6},{6,2},{1... | collective-permute-start | bytes 798728 | tf_op jit(solution)/shard_map/ppermute | solution.py:487
  6.9 2.4 %band_terms.4.refs_0_ = f32[4096,256]{1,0:T(8,128)S(1)} custom-call(f32[520,128]{1,0:T(8,128)S(1)} %pack.1.chunk), custom_call_target="tpu_custom_call" | custom-call | flops 1048576 | bytes 65536 | tf_op jit(solution)/shard_map/band_terms/pallas_call | solution.py:160
  9.3 0.0 copy-done
  9.3 0.3 prepare.1
  9.6 7.9 %collective-permute-done.chunk = f32[520,128]{1,0:T(8,128)S(1)} collective-permute-done((f32[520,128]{1,0:T(8,128)S(1)}, f32[520,128]{1,0:T(8,128)S(1)}, u32[]{:S(2)}, u32[]{:S(2)}) %collective-permute-start) | collective-permute-done | bytes 266272 | tf_op jit(solution)/shard_map/ppermute | solution.py:487
  17.5 0.6 %collective-permute-start.1 = (f32[520,128]{1,0:T(8,128)S(1)}, f32[520,128]{1,0:T(8,128)S(1)}, u32[]{:S(2)}, u32[]{:S(2)}) collective-permute-start(f32[520,128]{1,0:T(8,128)S(1)} %collective-permute-done.chunk), channel_id=1, source_target_pairs={{0,4},{4,0},{8,12},{12,8},{1,5},{5,1},{9,13},{13,9},{2,6},{6,2},{1... | collective-permute-start | bytes 798728 | tf_op jit(solution)/shard_map/ppermute | solution.py:487
  18.2 2.6 %band_terms.5.refs_0_ = f32[4096,256]{1,0:T(8,128)S(1)} custom-call(f32[520,128]{1,0:T(8,128)S(1)} %collective-permute-done.chunk, f32[4096,256]{1,0:T(8,128)S(1)} %band_terms.4.refs_0_), custom_call_target="tpu_custom_call", output_to_operand_aliasing={{}: (1, {})} | custom-call | flops 1048576 | bytes 65536 | tf_op jit(solution)/shard_map/band_terms/pallas_call | solution.py:160
  20.8 0.0 collective-permute-done.2.chunk
  20.8 2.6 %band_terms.6.refs_0_.before = f32[4096,256]{1,0:T(8,128)S(1)} custom-call(f32[520,128]{1,0:T(8,128)S(1)} %collective-permute-done.2.chunk, f32[4096,256]{1,0:T(8,128)S(1)} %band_terms.5.refs_0_), custom_call_target="tpu_custom_call", output_to_operand_aliasing={{}: (1, {})} | custom-call | flops 1048576 | bytes 65536 | tf_op jit(solution)/shard_map/band_terms/pallas_call | solution.py:160
  23.3 1.7 %collective-permute-done.1.chunk = f32[520,128]{1,0:T(8,128)S(1)} collective-permute-done((f32[520,128]{1,0:T(8,128)S(1)}, f32[520,128]{1,0:T(8,128)S(1)}, u32[]{:S(2)}, u32[]{:S(2)}) %collective-permute-start.1) | collective-permute-done | bytes 266272 | tf_op jit(solution)/shard_map/ppermute | solution.py:487
  25.1 0.5 edge_terms.1
  25.6 1.3 %collective-permute-start.3 = (f32[320,256]{1,0:T(8,128)S(1)}, f32[320,256]{1,0:T(8,128)S(1)}, u32[]{:S(2)}, u32[]{:S(2)}) collective-permute-start(f32[320,256]{1,0:T(8,128)S(1)} %get-tuple-element.24), channel_id=1, source_target_pairs={{0,1},{1,2},{2,3},{4,5},{5,6},{6,7},{8,9},{9,10},{10,11},{12,13},{... | collective-permute-start | bytes 983048 | tf_op jit(solution)/shard_map/ppermute | solution.py:482
  26.9 1.5 %collective-permute-start.4 = (f32[192,256]{1,0:T(8,128)S(1)}, f32[192,256]{1,0:T(8,128)S(1)}, u32[]{:S(2)}, u32[]{:S(2)}) collective-permute-start(f32[192,256]{1,0:T(8,128)S(1)} %get-tuple-element.25), channel_id=1, source_target_pairs={{1,0},{2,1},{3,2},{5,4},{6,5},{7,6},{9,8},{10,9},{11,10},{13,12},{... | collective-permute-start | bytes 589832 | tf_op jit(solution)/shard_map/ppermute | solution.py:482
  28.4 2.6 %band_terms.7 = (bf16[4096,256]{1,0:T(8,128)(2,1)S(1)}, bf16[4096,256]{1,0:T(8,128)(2,1)S(1)}) custom-call(f32[520,128]{1,0:T(8,128)S(1)} %collective-permute-done.1.chunk, f32[4096,256]{1,0:T(8,128)S(1)} %band_terms.6.refs_0_.before), custom_call_target="tpu_custom_call" | custom-call | flops 1048576 | bytes 65536 | tf_op jit(solution)/shard_map/band_terms/pallas_call | solution.py:160
  31.0 0.7 %collective-permute-done.4.right = f32[192,256]{1,0:T(8,128)S(1)} collective-permute-done((f32[192,256]{1,0:T(8,128)S(1)}, f32[192,256]{1,0:T(8,128)S(1)}, u32[]{:S(2)}, u32[]{:S(2)}) %collective-permute-start.4) | collective-permute-done | bytes 196640 | tf_op jit(solution)/shard_map/ppermute | solution.py:482
  31.7 0.0 collective-permute-done.3.left
  31.7 5.6 %apply_twice.1 = (bf16[2048,256]{1,0:T(8,128)(2,1)S(1)}, bf16[2048,256]{1,0:T(8,128)(2,1)S(1)}, f32[136,128]{1,0:T(8,128)S(1)}) custom-call(bf16[4096,256]{1,0:T(8,128)(2,1)S(1)} %get-tuple-element.22.g_hi, bf16[4096,256]{1,0:T(8,128)(2,1)S(1)} %get-tuple-element.23.g_lo, f32[320,256]{1,0:T(8,128)S(1)} %collective-permute-done.3.left, ...), custom_call_target="tpu_custom_call" | custom-call | flops 3221225472 | bytes 12582912 | tf_op jit(solution)/shard_map/apply_twice/pallas_call | solution.py:322
  37.3 8.9 %all-gather = f32[544,128]{1,0:T(8,128)S(1)} all-gather(f32[136,128]{1,0:T(8,128)S(1)} %get-tuple-element.28.own), channel_id=2, replica_groups=mesh['groups'=2,'src'=4,'blk'=4] {'blk'}, dimensions={0}, use_global_device_ids=true | all-gather | bytes 348160 | tf_op jit(solution)/shard_map/all_gather | solution.py:522
  46.2 9.5 %finish.1 = f32[2,2048,128]{2,1,0:T(8,128)} custom-call(f32[4,136,128]{2,1,0:T(8,128)S(1)} %bitcast.5, f32[136,128]{1,0:T(8,128)S(1)} %get-tuple-element.28.own, bf16[2048,256]{1,0:T(8,128)(2,1)S(1)} %get-tuple-element.29.z_hi, bf16[2048,256]{1,0:T(8,128)(2,1)S(1)} %get-tuple-element.30.z_lo), custom_call_target="tpu_custom_call" | custom-call | tf_op jit(solution)/shard_map/finish/pallas_call | solution.py:468
Async XLA Ops:
  1.2 8.1 %copy-start = (f32[2,2048,128]{2,1,0:T(8,128)S(1)}, f32[2,2048,128]{2,1,0:T(8,128)}, u32[]{:S(2)}) copy-start(f32[2,2048,128]{2,1,0:T(8,128)} %x.3) | copy-start | bytes 6291460
  1.2 16.3 %collective-permute-start = (f32[520,128]{1,0:T(8,128)S(1)}, f32[520,128]{1,0:T(8,128)S(1)}, u32[]{:S(2)}, u32[]{:S(2)}) collective-permute-start(f32[520,128]{1,0:T(8,128)S(1)} %pack.1.chunk), channel_id=1, source_target_pairs={{0,8},{4,12},{8,0},{12,4},{1,9},{5,13},{9,1},{13,5},{2,10},{6,14},... | collective-permute-start | bytes 798728 | tf_op jit(solution)/shard_map/ppermute | solution.py:487
  5.3 15.4 %collective-permute-start.2 = (f32[520,128]{1,0:T(8,128)S(1)}, f32[520,128]{1,0:T(8,128)S(1)}, u32[]{:S(2)}, u32[]{:S(2)}) collective-permute-start(f32[520,128]{1,0:T(8,128)S(1)} %pack.1.chunk), channel_id=1, source_target_pairs={{0,4},{4,0},{8,12},{12,8},{1,5},{5,1},{9,13},{13,9},{2,6},{6,2},{1... | collective-permute-start | bytes 798728 | tf_op jit(solution)/shard_map/ppermute | solution.py:487
  17.5 7.5 %collective-permute-start.1 = (f32[520,128]{1,0:T(8,128)S(1)}, f32[520,128]{1,0:T(8,128)S(1)}, u32[]{:S(2)}, u32[]{:S(2)}) collective-permute-start(f32[520,128]{1,0:T(8,128)S(1)} %collective-permute-done.chunk), channel_id=1, source_target_pairs={{0,4},{4,0},{8,12},{12,8},{1,5},{5,1},{9,13},{13,9},{2,6},{6,2},{1... | collective-permute-start | bytes 798728 | tf_op jit(solution)/shard_map/ppermute | solution.py:487
  25.6 6.1 %collective-permute-start.3 = (f32[320,256]{1,0:T(8,128)S(1)}, f32[320,256]{1,0:T(8,128)S(1)}, u32[]{:S(2)}, u32[]{:S(2)}) collective-permute-start(f32[320,256]{1,0:T(8,128)S(1)} %get-tuple-element.24), channel_id=1, source_target_pairs={{0,1},{1,2},{2,3},{4,5},{5,6},{6,7},{8,9},{9,10},{10,11},{12,13},{... | collective-permute-start | bytes 983048 | tf_op jit(solution)/shard_map/ppermute | solution.py:482
  26.9 4.8 %collective-permute-start.4 = (f32[192,256]{1,0:T(8,128)S(1)}, f32[192,256]{1,0:T(8,128)S(1)}, u32[]{:S(2)}, u32[]{:S(2)}) collective-permute-start(f32[192,256]{1,0:T(8,128)S(1)} %get-tuple-element.25), channel_id=1, source_target_pairs={{1,0},{2,1},{3,2},{5,4},{6,5},{7,6},{9,8},{10,9},{11,10},{13,12},{... | collective-permute-start | bytes 589832 | tf_op jit(solution)/shard_map/ppermute | solution.py:482

commit v8 on v7

--- a/solution.py
+++ b/solution.py
@@ -16,7 +16,7 @@
 BF16 = jnp.bfloat16
 HIGHEST = lax.Precision.HIGHEST
 VMEM = pl.BlockSpec(memory_space=pltpu.VMEM)
-PARAMS = pltpu.CompilerParams(vmem_limit_bytes=40 * 1024 * 1024)
+PARAMS = pltpu.CompilerParams(vmem_limit_bytes=16 * 1024 * 1024)
 
 
 def split(x):
@@ -61,6 +61,7 @@
         out[128 * (tiles + t) : 128 * (tiles + t) + 128, :] = imag
     out[256 * tiles :, :] = jnp.zeros((8, 128), F32)
     out[256 * tiles : 256 * tiles + tiles, :] = lax.rem(start, RB).astype(F32)
+    out[256 * tiles + 7 :, :] = lax.rem(lax.div(start[:1, :], RB), 2).astype(F32)
 
 
 def pack(pupils, starts, counts, weights, total_blocks):
@@ -177,36 +178,6 @@
     return jnp.concatenate([parts[0], parts[1]], axis=1)
 
 
-def edge_kernel(chunk, before, x, after_out, before_out):
-    left, right_hi, right_lo, place = factors(chunk)
-    blocks = (0, RB - 2, RB - 1)
-    left = jnp.concatenate([at_block(left, place, float(b)) for b in blocks], axis=0)
-    total = dot(left, right_hi) + dot(left, right_lo)
-    first, second, third = [
-        hermitian(before[b * 128 : (b + 1) * 128, :] + total[i * 128 : (i + 1) * 128, :])
-        for i, b in enumerate(blocks)
-    ]
-    after_out[:BLOCK, :] = second[BLOCK:, :]
-    after_out[BLOCK : 3 * BLOCK, :] = third
-    after_out[3 * BLOCK :, :] = wide(x[:, x.shape[1] - 2 * BLOCK :, :])
-    before_out[:BLOCK, :] = first[:BLOCK, :]
-    before_out[BLOCK:, :] = wide(x[:, : 2 * BLOCK, :])
-
-
-def build_edges(chunk, before, x):
-    return pl.pallas_call(
-        edge_kernel,
-        out_shape=(
-            jax.ShapeDtypeStruct((5 * BLOCK, 256), F32),
-            jax.ShapeDtypeStruct((3 * BLOCK, 256), F32),
-        ),
-        in_specs=[VMEM] * 3,
-        out_specs=(VMEM, VMEM),
-        compiler_params=PARAMS,
-        name="edge_terms",
-    )(chunk, before, x)
-
-
 def real_form(rows):
     return jnp.concatenate(
         [rows, jnp.concatenate([-rows[:, M:], rows[:, :M]], axis=1)], axis=0
@@ -225,6 +196,54 @@
         q += dot_t(hi[:, cols], jnp.concatenate([hi[:, cols] * half, lo[:, cols]], axis=1))
     q = q[:, :M] + q[:, M:]
     return q + q.T
+
+
+def in_odd_region(chunk):
+    row = chunk[chunk.shape[0] - 1 :, :]
+    return jnp.concatenate([row, row], axis=1) == 1.0
+
+
+def edge_kernel(chunk, before, x, first_out, second_out):
+    left, right_hi, right_lo, place = factors(chunk)
+    blocks = (0, RB - 2, RB - 1)
+    left = jnp.concatenate([at_block(left, place, float(b)) for b in blocks], axis=0)
+    total = dot(left, right_hi) + dot(left, right_lo)
+    head, next_last, last = [
+        hermitian(before[b * 128 : (b + 1) * 128, :] + total[i * 128 : (i + 1) * 128, :])
+        for i, b in enumerate(blocks)
+    ]
+    size = x.shape[1]
+    start = wide(x[:, : 2 * BLOCK, :])
+    stop = wide(x[:, size - 2 * BLOCK :, :])
+    held = jnp.concatenate([stop[BLOCK:], jnp.zeros((BLOCK, 256), F32)], axis=0)
+    own = times(*split(last), *split(held))
+    to_after = jnp.concatenate(
+        [
+            own[:BLOCK] + times(*split(next_last[BLOCK:]), *split(stop)),
+            own[BLOCK:],
+            last[BLOCK:],
+        ],
+        axis=0,
+    )
+    to_before = jnp.concatenate(
+        [times(*split(head[:BLOCK]), *split(start)), start[:BLOCK], jnp.zeros((BLOCK, 256), F32)],
+        axis=0,
+    )
+    is_odd = in_odd_region(chunk)
+    first_out[...] = jnp.where(is_odd, to_after, to_before)
+    second_out[...] = jnp.where(is_odd, to_before, to_after)
+
+
+def build_edges(chunk, before, x):
+    shape = jax.ShapeDtypeStruct((3 * BLOCK, 256), F32)
+    return pl.pallas_call(
+        edge_kernel,
+        out_shape=(shape, shape),
+        in_specs=[VMEM] * 3,
+        out_specs=(VMEM, VMEM),
+        compiler_params=PARAMS,
+        name="edge_terms",
+    )(chunk, before, x)
 
 
 def prepare_kernel(x, hi_out, lo_out):
@@ -245,10 +264,18 @@
     )(x)
 
 
-def apply_kernel(g_hi, g_lo, left, right, x_hi, x_lo, z_hi, z_lo, grams, p_hi, p_lo):
+def apply_kernel(own, g_hi, g_lo, swap_1, swap_2, x_hi, x_lo, z_hi, z_lo, grams, p_hi, p_lo):
     rows = RB * BLOCK
-    left_hi, left_lo = split(left[: 3 * BLOCK, :])
-    right_hi, right_lo = split(right[:BLOCK, :])
+    is_odd = in_odd_region(own)
+    left = jnp.where(is_odd, swap_2[...], swap_1[...])
+    right = jnp.where(is_odd, swap_1[...], swap_2[...])
+    into = left[2 * BLOCK :]
+    into_hi, into_lo = split(into)
+    none = jnp.zeros((BLOCK, 128), F32)
+    out_of = [jnp.concatenate([none, part], axis=0).T[:BLOCK] for part in (into[:, :M], into[:, M:])]
+    out_hi, out_lo = split(jnp.concatenate([out_of[0], -out_of[1]], axis=1))
+    tail = split(right[BLOCK : 2 * BLOCK])
+    nothing = jnp.zeros((BLOCK, 256), BF16)
 
     def put(e, block):
         at = pl.ds(pl.multiple_of(e * BLOCK, BLOCK), BLOCK)
@@ -257,16 +284,13 @@
     def join(a, b):
         return jnp.concatenate([a, b], axis=0)
 
-    head = split(left[3 * BLOCK :, :])
-    tail = split(right[BLOCK:, :])
-    spill = times(left_hi[:BLOCK], left_lo[:BLOCK], head[0], head[1])
     both = times(
-        left_hi[BLOCK:],
-        left_lo[BLOCK:],
-        join(head[0][BLOCK:], x_hi[:BLOCK, :]),
-        join(head[1][BLOCK:], x_lo[:BLOCK, :]),
-    )
-    first_block = spill + both[:BLOCK]
+        join(out_hi, into_hi),
+        join(out_lo, into_lo),
+        join(nothing, x_hi[:BLOCK, :]),
+        join(nothing, x_lo[:BLOCK, :]),
+    ) + left[: 2 * BLOCK]
+    first_block = both[:BLOCK]
     put(0, first_block)
 
     def first(b, carry):
@@ -283,12 +307,12 @@
     both = times(
         g_hi[(RB - 1) * 128 :, :],
         g_lo[(RB - 1) * 128 :, :],
-        join(x_hi[rows - BLOCK :, :], tail[0][:BLOCK]),
-        join(x_lo[rows - BLOCK :, :], tail[1][:BLOCK]),
+        join(x_hi[rows - BLOCK :, :], tail[0]),
+        join(x_lo[rows - BLOCK :, :], tail[1]),
     )
     block = both[:BLOCK] + spill
     put(RB, block)
-    last_block = both[BLOCK:] + times(right_hi, right_lo, tail[0], tail[1])
+    last_block = both[BLOCK:] + right[:BLOCK]
     put(RB + 1, last_block)
     top = jnp.maximum(jnp.maximum(top, jnp.abs(block)), jnp.abs(last_block))
     top = jnp.max(top, axis=0, keepdims=True)
@@ -307,7 +331,7 @@
         z_hi[out, :], z_lo[out, :] = split((both[:BLOCK] + spill) * scale)
         return both[BLOCK:]
 
-    spill = times(left_hi[2 * BLOCK :], left_lo[2 * BLOCK :], p_hi[:128, :], p_lo[:128, :])
+    spill = times(into_hi, into_lo, p_hi[:128, :], p_lo[:128, :])
     lax.fori_loop(0, RB, second, spill, unroll=RB // 2)
     gram_2 = gram_of(z_hi[...], z_lo[...])
     row = lax.broadcasted_iota(jnp.int32, (M, M), 0)
@@ -317,7 +341,7 @@
     grams[M:, :] = jnp.concatenate([diagonal, top, jnp.zeros((6, M), F32)], axis=0)
 
 
-def apply_twice(g_hi, g_lo, left, right, x_hi, x_lo):
+def apply_twice(own, g_hi, g_lo, swap_1, swap_2, x_hi, x_lo):
     rows = RB * BLOCK
     return pl.pallas_call(
         apply_kernel,
@@ -326,7 +350,7 @@
             jax.ShapeDtypeStruct((rows, 256), BF16),
             jax.ShapeDtypeStruct((M + 8, M), F32),
         ),
-        in_specs=[VMEM] * 6,
+        in_specs=[VMEM] * 7,
         out_specs=(VMEM, VMEM, VMEM),
         scratch_shapes=[pltpu.VMEM((rows + 2 * BLOCK, 256), BF16)] * 2,
         compiler_params=PARAMS,
@@ -334,7 +358,7 @@
             flops=12 * RB * 128 * 256 * 256, bytes_accessed=12 << 20, transcendentals=0
         ),
         name="apply_twice",
-    )(g_hi, g_lo, left, right, x_hi, x_lo)
+    )(own, g_hi, g_lo, swap_1, swap_2, x_hi, x_lo)
 
 
 def inverse_factor(a, work):
@@ -413,8 +437,9 @@
     return work[:, M:]
 
 
-def finish_kernel(total_rows, grams, own, z_hi, z_lo, out, work):
-    peers = grams.shape[0]
+def finish_kernel(total_rows, *refs):
+    grams, (z_hi, z_lo, out, work) = refs[:-4], refs[-4:]
+    own = grams[0]
     row = lax.broadcasted_iota(jnp.int32, (M, M), 0)
     col = lax.broadcasted_iota(jnp.int32, (M, M), 1)
     eye = jnp.where(row == col, 1.0, 0.0)
@@ -425,16 +450,16 @@
     def row_of(x):
         return jnp.sum(eye * x, axis=0, keepdims=True)
 
-    total = grams[0, :M, :]
-    for r in range(1, peers):
-        total = total + grams[r, :M, :]
+    total = own[:M, :]
+    for one in grams[1:]:
+        total = total + one[:M, :]
     gram = jnp.where(row >= col, total, total.T)
     norm = lax.rsqrt(row_of(gram))
     inverse = inverse_factor(gram * norm * as_column(norm), work)
     total = jnp.zeros((M, M), F32)
-    for r in range(peers):
-        size = norm * grams[r, M + 1 : M + 2, :]
-        second = jnp.where(row == col, grams[r, M : M + 1, :], grams[r, :M, :])
+    for one in grams:
+        size = norm * one[M + 1 : M + 2, :]
+        second = jnp.where(row == col, one[M : M + 1, :], one[:M, :])
         total = total + second * size * as_column(size)
     gram = jnp.where(row <= col, total, total.T)
     gram = dot_f32(dot_f32(inverse, gram), inverse.T)
@@ -464,43 +489,41 @@
     lax.fori_loop(0, z_hi.shape[0] // step, rows_of, 0, unroll=True)
 
 
-def finish(grams, own, z_hi, z_lo, total_rows):
+def finish(grams, z_hi, z_lo, total_rows):
     return pl.pallas_call(
         partial(finish_kernel, total_rows),
         out_shape=jax.ShapeDtypeStruct((2, z_hi.shape[0], M), F32),
-        in_specs=[VMEM] * 4,
+        in_specs=[VMEM] * (len(grams) + 2),
         out_specs=VMEM,
         scratch_shapes=[pltpu.VMEM((M, 2 * M), F32)],
         compiler_params=PARAMS,
         name="finish",
-    )(grams, own, z_hi, z_lo)
-
-
-def shifted(x, by):
-    peers = lax.axis_size("blk")
-    pairs = [(i, i + by) for i in range(peers) if 0 <= i + by < peers]
-    return lax.ppermute(x, "blk", pairs)
-
-
-def swapped(x, far):
-    peers = lax.axis_size("src")
-    return lax.ppermute(x, "src", [(i, i ^ far) for i in range(peers)])
-
-
-def gathered(own, ready):
-    peers = lax.axis_size("src")
+    )(*grams, z_hi, z_lo)
+
+
+def neighbours(x, begin):
+    pairs = [(i, i + 1) for i in range(begin, lax.axis_size("blk") - 1, 2)]
+    return lax.ppermute(x, "blk", pairs + [(j, i) for i, j in pairs])
+
+
+def swapped(x, far, axis="src"):
+    return lax.ppermute(x, axis, [(i, i ^ far) for i in range(lax.axis_size(axis))])
+
+
+def gathered(own, ready, axis="src"):
+    peers = lax.axis_size(axis)
     if peers & (peers - 1):
         chunks = [
-            lax.ppermute(own, "src", [(i, (i + k) % peers) for i in range(peers)])
+            lax.ppermute(own, axis, [(i, (i + k) % peers) for i in range(peers)])
             for k in range(1, peers)
         ]
         return chunks, ready
     far = peers // 2
     chunks = []
     while far:
-        if chunks:
+        if chunks and ready:
             chunks, ready = lax.optimization_barrier((chunks, ready))
-        chunks = chunks + [swapped(c, far) for c in [own] + chunks]
+        chunks = chunks + [swapped(c, far, axis) for c in [own] + chunks]
         far //= 2
     return chunks, ready
 
@@ -515,12 +538,12 @@
     band, x_hi, x_lo = ready
     for chunk in chunks[:-1]:
         band = build(chunk, band)
-    after, before = build_edges(chunks[-1], band, start_block)
-    left, right = shifted(after, 1), shifted(before, -1)
+    swap_1, swap_2 = build_edges(chunks[-1], band, start_block)
+    swap_1, swap_2 = neighbours(swap_1, 1), neighbours(swap_2, 0)
     g_hi, g_lo = build(chunks[-1], band, last=True)
-    z_hi, z_lo, own_grams = apply_twice(g_hi, g_lo, left, right, x_hi, x_lo)
-    grams = lax.all_gather(own_grams, "blk", axis=0)
-    return finish(grams, own_grams, z_hi, z_lo, 2.0 * size * regions)
+    z_hi, z_lo, grams = apply_twice(own, g_hi, g_lo, swap_1, swap_2, x_hi, x_lo)
+    grams = [grams] + gathered(grams, (), "blk")[0]
+    return finish(grams, z_hi, z_lo, 2.0 * size * regions)
 
 
 def solution(mesh):

time: 55.9 us -> 53.7 us (0.961)
  blocking collectives: 8.89 us -> 0 us
  waiting for transfers between devices: 10.3 us -> 13.4 us
  starting transfers between devices: 9.08 us -> 12 us
  Pallas kernels: 27.3 us -> 28 us
    all_gather x1 -> x0, blocking collectives: 8.89 us -> none  [per_device(): grams = lax.all_gather(own_grams, 'blk', axis=0)]
    ppermute x5 -> x8, waiting for transfers between devices: 10.3 us -> 13.4 us  [the longest x6 13.3 us: swapped(): lax.ppermute(x, axis, [(i, i ^ far) for i in range(lax.axis_size(axis))])]
    ppermute x5 -> x8, starting transfers between devices: 9.08 us -> 12 us  [the longest x6 8.45 us: swapped(): lax.ppermute(x, axis, [(i, i ^ far) for i in range(lax.axis_size(axis))])]
  transfers between devices with their start and end apart: 5 -> 8, of which waited for: 3 -> 4; matrix products, arithmetic and copies ran while one was open for 0% -> 0% of each run, Pallas kernels for 19% -> 20%
where the time goes in v8:
time: 53.7 us; the launch traced here: 53.4 us
  Pallas kernels  28 us (52%)
  waiting for transfers between devices  13.4 us (25%)
  starting transfers between devices  12 us (22%)
    ppermute x6, waiting for transfers between devices, swapped(): lax.ppermute(x, axis, [(i, i ^ far) for i in range(lax.axis_size(axis))])  13.3 us
    pallas_call x4, Pallas kernels, build(): pl.pallas_call(partial(build_kernel, add, last), out_shape=out, in_specs=...  10.1 us
    pallas_call x1, Pallas kernels, finish(): pl.pallas_call(partial(finish_kernel, total_rows), out_shape=jax.ShapeDty...  9.52 us
    ppermute x6, starting transfers between devices, swapped(): lax.ppermute(x, axis, [(i, i ^ far) for i in range(lax.axis_size(axis))])  8.45 us
    pallas_call x1, Pallas kernels, apply_twice(): pl.pallas_call(apply_kernel, out_shape=(jax.ShapeDtypeStruct((rows, 256),...  5.77 us
    ppermute x2, starting transfers between devices, neighbours(): return lax.ppermute(x, 'blk', pairs + [(j, i) for i, j in pairs])  3.51 us
    pallas_call x1, Pallas kernels, pack(): pl.pallas_call(partial(pack_kernel, total_blocks), out_shape=jax.ShapeDty...  1.22 us
  transfers between devices with their start and end apart: 8, of which 4 were waited for; matrix products, arithmetic and copies ran while one was open for 0% of the time, Pallas kernels for 20%

profile of v8, /device:TPU:0, one launch (start us, length us, event | category | flops | bytes accessed | tf_op | source)
XLA Modules:
  0.0 53.4 jit_solution(1918508225406400649)
XLA Ops:
  0.0 1.2 %pack.1.chunk.own = f32[520,128]{1,0:T(8,128)S(1)} custom-call(f32[512,128]{1,0:T(8,128)} %bitcast.4, s32[2,128]{1,0:T(2,128)} %bitcast.5, s32[2,128]{1,0:T(2,128)} %bitcast.6, f32[2,128]{1,0:T(2,128)} %bitcast.7), custom_call_target="tpu_custom_call" | custom-call | tf_op jit(solution)/shard_map/pack/pallas_call | solution.py:69
  1.2 0.0 copy-start
  1.2 4.1 %collective-permute-start = (f32[520,128]{1,0:T(8,128)S(1)}, f32[520,128]{1,0:T(8,128)S(1)}, u32[]{:S(2)}, u32[]{:S(2)}) collective-permute-start(f32[520,128]{1,0:T(8,128)S(1)} %pack.1.chunk.own), channel_id=1, source_target_pairs={{0,8},{4,12},{8,0},{12,4},{1,9},{5,13},{9,1},{13,5},{2,10},{6,14},... | collective-permute-start | bytes 798728 | tf_op jit(solution)/shard_map/ppermute | solution.py:510
  5.3 1.6 %collective-permute-start.2 = (f32[520,128]{1,0:T(8,128)S(1)}, f32[520,128]{1,0:T(8,128)S(1)}, u32[]{:S(2)}, u32[]{:S(2)}) collective-permute-start(f32[520,128]{1,0:T(8,128)S(1)} %pack.1.chunk.own), channel_id=1, source_target_pairs={{0,4},{4,0},{8,12},{12,8},{1,5},{5,1},{9,13},{13,9},{2,6},{6,2},{1... | collective-permute-start | bytes 798728 | tf_op jit(solution)/shard_map/ppermute | solution.py:510
  6.9 2.4 %band_terms.4.refs_0_ = f32[4096,256]{1,0:T(8,128)S(1)} custom-call(f32[520,128]{1,0:T(8,128)S(1)} %pack.1.chunk.own), custom_call_target="tpu_custom_call" | custom-call | flops 1048576 | bytes 65536 | tf_op jit(solution)/shard_map/band_terms/pallas_call | solution.py:161
  9.3 0.0 copy-done
  9.3 0.3 prepare.1
  9.6 7.9 %collective-permute-done.chunk = f32[520,128]{1,0:T(8,128)S(1)} collective-permute-done((f32[520,128]{1,0:T(8,128)S(1)}, f32[520,128]{1,0:T(8,128)S(1)}, u32[]{:S(2)}, u32[]{:S(2)}) %collective-permute-start) | collective-permute-done | bytes 266272 | tf_op jit(solution)/shard_map/ppermute | solution.py:510
  17.5 0.6 %collective-permute-start.1 = (f32[520,128]{1,0:T(8,128)S(1)}, f32[520,128]{1,0:T(8,128)S(1)}, u32[]{:S(2)}, u32[]{:S(2)}) collective-permute-start(f32[520,128]{1,0:T(8,128)S(1)} %collective-permute-done.chunk), channel_id=1, source_target_pairs={{0,4},{4,0},{8,12},{12,8},{1,5},{5,1},{9,13},{13,9},{2,6},{6,2},{1... | collective-permute-start | bytes 798728 | tf_op jit(solution)/shard_map/ppermute | solution.py:510
  18.2 2.6 %band_terms.5.refs_0_ = f32[4096,256]{1,0:T(8,128)S(1)} custom-call(f32[520,128]{1,0:T(8,128)S(1)} %collective-permute-done.chunk, f32[4096,256]{1,0:T(8,128)S(1)} %band_terms.4.refs_0_), custom_call_target="tpu_custom_call", output_to_operand_aliasing={{}: (1, {})} | custom-call | flops 1048576 | bytes 65536 | tf_op jit(solution)/shard_map/band_terms/pallas_call | solution.py:161
  20.8 0.0 collective-permute-done.2.chunk
  20.8 2.6 %band_terms.6.refs_0_.before = f32[4096,256]{1,0:T(8,128)S(1)} custom-call(f32[520,128]{1,0:T(8,128)S(1)} %collective-permute-done.2.chunk, f32[4096,256]{1,0:T(8,128)S(1)} %band_terms.5.refs_0_), custom_call_target="tpu_custom_call", output_to_operand_aliasing={{}: (1, {})} | custom-call | flops 1048576 | bytes 65536 | tf_op jit(solution)/shard_map/band_terms/pallas_call | solution.py:161
  23.3 1.7 %collective-permute-done.1.chunk = f32[520,128]{1,0:T(8,128)S(1)} collective-permute-done((f32[520,128]{1,0:T(8,128)S(1)}, f32[520,128]{1,0:T(8,128)S(1)}, u32[]{:S(2)}, u32[]{:S(2)}) %collective-permute-start.1) | collective-permute-done | bytes 266272 | tf_op jit(solution)/shard_map/ppermute | solution.py:510
  25.1 1.0 %edge_terms.1 = (f32[192,256]{1,0:T(8,128)S(1)}, f32[192,256]{1,0:T(8,128)S(1)}) custom-call(f32[520,128]{1,0:T(8,128)S(1)} %collective-permute-done.1.chunk, f32[4096,256]{1,0:T(8,128)S(1)} %band_terms.6.refs_0_.before, f32[2,2048,128]{2,1,0:T(8,128)S(1)} %copy-done), custom_call_target="tpu_custom_call" | custom-call | tf_op jit(solution)/shard_map/edge_terms/pallas_call | solution.py:239
  26.1 0.9 %collective-permute-start.3 = (f32[192,256]{1,0:T(8,128)S(1)}, f32[192,256]{1,0:T(8,128)S(1)}, u32[]{:S(2)}, u32[]{:S(2)}) collective-permute-start(f32[192,256]{1,0:T(8,128)S(1)} %get-tuple-element.24), channel_id=1, source_target_pairs={{1,2},{2,1},{5,6},{6,5},{9,10},{10,9},{13,14},{14,13},{17,18},{18,... | collective-permute-start | bytes 589832 | tf_op jit(solution)/shard_map/ppermute | solution.py:506
  26.9 2.7 %collective-permute-start.4 = (f32[192,256]{1,0:T(8,128)S(1)}, f32[192,256]{1,0:T(8,128)S(1)}, u32[]{:S(2)}, u32[]{:S(2)}) collective-permute-start(f32[192,256]{1,0:T(8,128)S(1)} %get-tuple-element.25), channel_id=1, source_target_pairs={{0,1},{2,3},{1,0},{3,2},{4,5},{6,7},{5,4},{7,6},{8,9},{10,11},{9,8... | collective-permute-start | bytes 589832 | tf_op jit(solution)/shard_map/ppermute | solution.py:506
  29.6 2.6 %band_terms.7 = (bf16[4096,256]{1,0:T(8,128)(2,1)S(1)}, bf16[4096,256]{1,0:T(8,128)(2,1)S(1)}) custom-call(f32[520,128]{1,0:T(8,128)S(1)} %collective-permute-done.1.chunk, f32[4096,256]{1,0:T(8,128)S(1)} %band_terms.6.refs_0_.before), custom_call_target="tpu_custom_call" | custom-call | flops 1048576 | bytes 65536 | tf_op jit(solution)/shard_map/band_terms/pallas_call | solution.py:161
  32.2 0.0 collective-permute-done.3.swap_1
  32.2 0.0 collective-permute-done.4.swap_2
  32.2 5.8 %apply_twice.1 = (bf16[2048,256]{1,0:T(8,128)(2,1)S(1)}, bf16[2048,256]{1,0:T(8,128)(2,1)S(1)}, f32[136,128]{1,0:T(8,128)S(1)}) custom-call(f32[520,128]{1,0:T(8,128)S(1)} %pack.1.chunk.own, bf16[4096,256]{1,0:T(8,128)(2,1)S(1)} %get-tuple-element.22.g_hi, bf16[4096,256]{1,0:T(8,128)(2,1)S(1)} %get-tuple-element.23.g_lo, ...), custom_call_target="tpu_custom_call" | custom-call | flops 3221225472 | bytes 12582912 | tf_op jit(solution)/shard_map/apply_twice/pallas_call | solution.py:346
  38.0 2.2 %collective-permute-start.5 = (f32[136,128]{1,0:T(8,128)S(1)}, f32[136,128]{1,0:T(8,128)S(1)}, u32[]{:S(2)}, u32[]{:S(2)}) collective-permute-start(f32[136,128]{1,0:T(8,128)S(1)} %get-tuple-element.28.refs_0_), channel_id=1, source_target_pairs={{0,2},{1,3},{2,0},{3,1},{4,6},{5,7},{6,4},{7,5},{8,10},{9,11},{10,... | collective-permute-start | bytes 208904 | tf_op jit(solution)/shard_map/ppermute | solution.py:510
  40.2 0.0 collective-permute-start.6
  40.2 2.5 %collective-permute-done.5.refs_1_ = f32[136,128]{1,0:T(8,128)S(1)} collective-permute-done((f32[136,128]{1,0:T(8,128)S(1)}, f32[136,128]{1,0:T(8,128)S(1)}, u32[]{:S(2)}, u32[]{:S(2)}) %collective-permute-start.5) | collective-permute-done | bytes 69664 | tf_op jit(solution)/shard_map/ppermute | solution.py:510
  42.6 0.0 collective-permute-start.7
  42.6 0.0 collective-permute-done.6.refs_2_
  42.6 1.3 %collective-permute-done.7.refs_3_ = f32[136,128]{1,0:T(8,128)S(1)} collective-permute-done((f32[136,128]{1,0:T(8,128)S(1)}, f32[136,128]{1,0:T(8,128)S(1)}, u32[]{:S(2)}, u32[]{:S(2)}) %collective-permute-start.7) | collective-permute-done | bytes 69664 | tf_op jit(solution)/shard_map/ppermute | solution.py:510
  43.9 9.5 %finish.1 = f32[2,2048,128]{2,1,0:T(8,128)} custom-call(f32[136,128]{1,0:T(8,128)S(1)} %get-tuple-element.28.refs_0_, f32[136,128]{1,0:T(8,128)S(1)} %collective-permute-done.5.refs_1_, f32[136,128]{1,0:T(8,128)S(1)} %collective-permute-done.6.refs_2_, f32[136,128]{1,0:T(8,128)S(1)} %collective-permute-done.7.refs_3_, ...), custom_call_target="tpu_custom_call" | custom-call | tf_op jit(solution)/shard_map/finish/pallas_call | solution.py:493
Async XLA Ops:
  1.2 8.1 %copy-start = (f32[2,2048,128]{2,1,0:T(8,128)S(1)}, f32[2,2048,128]{2,1,0:T(8,128)}, u32[]{:S(2)}) copy-start(f32[2,2048,128]{2,1,0:T(8,128)} %x.3) | copy-start | bytes 6291460
  1.2 16.3 %collective-permute-start = (f32[520,128]{1,0:T(8,128)S(1)}, f32[520,128]{1,0:T(8,128)S(1)}, u32[]{:S(2)}, u32[]{:S(2)}) collective-permute-start(f32[520,128]{1,0:T(8,128)S(1)} %pack.1.chunk.own), channel_id=1, source_target_pairs={{0,8},{4,12},{8,0},{12,4},{1,9},{5,13},{9,1},{13,5},{2,10},{6,14},... | collective-permute-start | bytes 798728 | tf_op jit(solution)/shard_map/ppermute | solution.py:510
  5.3 15.4 %collective-permute-start.2 = (f32[520,128]{1,0:T(8,128)S(1)}, f32[520,128]{1,0:T(8,128)S(1)}, u32[]{:S(2)}, u32[]{:S(2)}) collective-permute-start(f32[520,128]{1,0:T(8,128)S(1)} %pack.1.chunk.own), channel_id=1, source_target_pairs={{0,4},{4,0},{8,12},{12,8},{1,5},{5,1},{9,13},{13,9},{2,6},{6,2},{1... | collective-permute-start | bytes 798728 | tf_op jit(solution)/shard_map/ppermute | solution.py:510
  17.5 7.5 %collective-permute-start.1 = (f32[520,128]{1,0:T(8,128)S(1)}, f32[520,128]{1,0:T(8,128)S(1)}, u32[]{:S(2)}, u32[]{:S(2)}) collective-permute-start(f32[520,128]{1,0:T(8,128)S(1)} %collective-permute-done.chunk), channel_id=1, source_target_pairs={{0,4},{4,0},{8,12},{12,8},{1,5},{5,1},{9,13},{13,9},{2,6},{6,2},{1... | collective-permute-start | bytes 798728 | tf_op jit(solution)/shard_map/ppermute | solution.py:510
  26.1 6.1 %collective-permute-start.3 = (f32[192,256]{1,0:T(8,128)S(1)}, f32[192,256]{1,0:T(8,128)S(1)}, u32[]{:S(2)}, u32[]{:S(2)}) collective-permute-start(f32[192,256]{1,0:T(8,128)S(1)} %get-tuple-element.24), channel_id=1, source_target_pairs={{1,2},{2,1},{5,6},{6,5},{9,10},{10,9},{13,14},{14,13},{17,18},{18,... | collective-permute-start | bytes 589832 | tf_op jit(solution)/shard_map/ppermute | solution.py:506
  26.9 5.3 %collective-permute-start.4 = (f32[192,256]{1,0:T(8,128)S(1)}, f32[192,256]{1,0:T(8,128)S(1)}, u32[]{:S(2)}, u32[]{:S(2)}) collective-permute-start(f32[192,256]{1,0:T(8,128)S(1)} %get-tuple-element.25), channel_id=1, source_target_pairs={{0,1},{2,3},{1,0},{3,2},{4,5},{6,7},{5,4},{7,6},{8,9},{10,11},{9,8... | collective-permute-start | bytes 589832 | tf_op jit(solution)/shard_map/ppermute | solution.py:506
  38.0 4.6 %collective-permute-start.5 = (f32[136,128]{1,0:T(8,128)S(1)}, f32[136,128]{1,0:T(8,128)S(1)}, u32[]{:S(2)}, u32[]{:S(2)}) collective-permute-start(f32[136,128]{1,0:T(8,128)S(1)} %get-tuple-element.28.refs_0_), channel_id=1, source_target_pairs={{0,2},{1,3},{2,0},{3,1},{4,6},{5,7},{6,4},{7,5},{8,10},{9,11},{10,... | collective-permute-start | bytes 208904 | tf_op jit(solution)/shard_map/ppermute | solution.py:510
  40.2 2.5 %collective-permute-start.6 = (f32[136,128]{1,0:T(8,128)S(1)}, f32[136,128]{1,0:T(8,128)S(1)}, u32[]{:S(2)}, u32[]{:S(2)}) collective-permute-start(f32[136,128]{1,0:T(8,128)S(1)} %get-tuple-element.28.refs_0_), channel_id=1, source_target_pairs={{0,1},{1,0},{2,3},{3,2},{4,5},{5,4},{6,7},{7,6},{8,9},{9,8},{10,11... | collective-permute-start | bytes 208904 | tf_op jit(solution)/shard_map/ppermute | solution.py:510
  42.6 1.3 %collective-permute-start.7 = (f32[136,128]{1,0:T(8,128)S(1)}, f32[136,128]{1,0:T(8,128)S(1)}, u32[]{:S(2)}, u32[]{:S(2)}) collective-permute-start(f32[136,128]{1,0:T(8,128)S(1)} %collective-permute-done.5.refs_1_), channel_id=1, source_target_pairs={{0,1},{1,0},{2,3},{3,2},{4,5},{5,4},{6,7},{7,6},{8,9},{9,8},{10,11... | collective-permute-start | bytes 208904 | tf_op jit(solution)/shard_map/ppermute | solution.py:510

commit v9 on v8

--- a/solution.py
+++ b/solution.py
@@ -264,7 +264,61 @@
     )(x)
 
 
-def apply_kernel(own, g_hi, g_lo, swap_1, swap_2, x_hi, x_lo, z_hi, z_lo, grams, p_hi, p_lo):
+def join(a, b):
+    return jnp.concatenate([a, b], axis=0)
+
+
+def put(hi, lo, e, block):
+    at = pl.ds(pl.multiple_of(e * BLOCK, BLOCK), BLOCK)
+    hi[at, :], lo[at, :] = split(block)
+
+
+def first_kernel(g_hi, g_lo, x_hi, x_lo, p_hi, p_lo, ends):
+    rows = RB * BLOCK
+    nothing = jnp.zeros((BLOCK, 256), BF16)
+
+    def pair(b):
+        at = pl.ds(pl.multiple_of(b * 128, 128), 128)
+        win = pl.ds(pl.multiple_of(b * BLOCK, BLOCK), 128)
+        return times(g_hi[at, :], g_lo[at, :], x_hi[win, :], x_lo[win, :])
+
+    def one(b, carry):
+        spill, top = carry
+        both = pair(b)
+        block = both[:BLOCK] + spill
+        put(p_hi, p_lo, b + 1, block)
+        return both[BLOCK:], jnp.maximum(top, jnp.abs(block))
+
+    both = pair(0)
+    ends[:BLOCK, :] = both[:BLOCK]
+    carry = both[BLOCK:], jnp.zeros((BLOCK, 256), F32)
+    spill, top = lax.fori_loop(1, RB - 1, one, carry, unroll=RB - 2)
+    both = times(
+        g_hi[(RB - 1) * 128 :, :],
+        g_lo[(RB - 1) * 128 :, :],
+        join(x_hi[rows - BLOCK :, :], nothing),
+        join(x_lo[rows - BLOCK :, :], nothing),
+    )
+    ends[BLOCK : 2 * BLOCK, :] = both[:BLOCK] + spill
+    ends[2 * BLOCK : 3 * BLOCK, :] = both[BLOCK:]
+    ends[3 * BLOCK :, :] = jnp.broadcast_to(jnp.max(top, axis=0, keepdims=True), (8, 256))
+
+
+def first_product(g_hi, g_lo, x_hi, x_lo):
+    shape = jax.ShapeDtypeStruct(((RB + 2) * BLOCK, 256), BF16)
+    return pl.pallas_call(
+        first_kernel,
+        out_shape=(shape, shape, jax.ShapeDtypeStruct((3 * BLOCK + 8, 256), F32)),
+        in_specs=[VMEM] * 4,
+        out_specs=(VMEM, VMEM, VMEM),
+        compiler_params=PARAMS,
+        cost_estimate=pl.CostEstimate(flops=1 << 20, bytes_accessed=1 << 16, transcendentals=0),
+        name="first_product",
+    )(g_hi, g_lo, x_hi, x_lo)
+
+
+def second_kernel(own, g_hi, g_lo, swap_1, swap_2, x_hi, x_lo, ends, p_hi_in, p_lo_in,
+                  z_hi, z_lo, grams, p_hi, p_lo):
     rows = RB * BLOCK
     is_odd = in_odd_region(own)
     left = jnp.where(is_odd, swap_2[...], swap_1[...])
@@ -276,46 +330,27 @@
     out_hi, out_lo = split(jnp.concatenate([out_of[0], -out_of[1]], axis=1))
     tail = split(right[BLOCK : 2 * BLOCK])
     nothing = jnp.zeros((BLOCK, 256), BF16)
-
-    def put(e, block):
-        at = pl.ds(pl.multiple_of(e * BLOCK, BLOCK), BLOCK)
-        p_hi[at, :], p_lo[at, :] = split(block)
-
-    def join(a, b):
-        return jnp.concatenate([a, b], axis=0)
-
     both = times(
         join(out_hi, into_hi),
         join(out_lo, into_lo),
         join(nothing, x_hi[:BLOCK, :]),
         join(nothing, x_lo[:BLOCK, :]),
     ) + left[: 2 * BLOCK]
-    first_block = both[:BLOCK]
-    put(0, first_block)
-
-    def first(b, carry):
-        spill, top = carry
-        at = pl.ds(pl.multiple_of(b * 128, 128), 128)
-        win = pl.ds(pl.multiple_of(b * BLOCK, BLOCK), 128)
-        both = times(g_hi[at, :], g_lo[at, :], x_hi[win, :], x_lo[win, :])
-        block = both[:BLOCK] + spill
-        put(b + 1, block)
-        return both[BLOCK:], jnp.maximum(top, jnp.abs(block))
-
-    carry = first(0, (both[BLOCK:], jnp.abs(first_block)))
-    spill, top = lax.fori_loop(1, RB - 1, first, carry, unroll=RB - 2)
-    both = times(
+    after = times(
         g_hi[(RB - 1) * 128 :, :],
         g_lo[(RB - 1) * 128 :, :],
-        join(x_hi[rows - BLOCK :, :], tail[0]),
-        join(x_lo[rows - BLOCK :, :], tail[1]),
-    )
-    block = both[:BLOCK] + spill
-    put(RB, block)
-    last_block = both[BLOCK:] + right[:BLOCK]
-    put(RB + 1, last_block)
-    top = jnp.maximum(jnp.maximum(top, jnp.abs(block)), jnp.abs(last_block))
-    top = jnp.max(top, axis=0, keepdims=True)
+        join(nothing, tail[0]),
+        join(nothing, tail[1]),
+    )
+    top = ends[3 * BLOCK : 3 * BLOCK + 1, :]
+    for e, block in (
+        (0, both[:BLOCK]),
+        (1, both[BLOCK:] + ends[:BLOCK, :]),
+        (RB, after[:BLOCK] + ends[BLOCK : 2 * BLOCK, :]),
+        (RB + 1, after[BLOCK:] + ends[2 * BLOCK : 3 * BLOCK, :] + right[:BLOCK]),
+    ):
+        put(p_hi, p_lo, e, block)
+        top = jnp.maximum(top, jnp.max(jnp.abs(block), axis=0, keepdims=True))
     top = jnp.maximum(top[:, :M], top[:, M:])
     scale = jnp.where(top > 0, 1.0 / jnp.where(top > 0, top, 1.0), 0.0)
     scale = jnp.concatenate([scale, scale], axis=1)
@@ -332,7 +367,7 @@
         return both[BLOCK:]
 
     spill = times(into_hi, into_lo, p_hi[:128, :], p_lo[:128, :])
-    lax.fori_loop(0, RB, second, spill, unroll=RB // 2)
+    lax.fori_loop(0, RB, second, spill, unroll=RB)
     gram_2 = gram_of(z_hi[...], z_lo[...])
     row = lax.broadcasted_iota(jnp.int32, (M, M), 0)
     col = lax.broadcasted_iota(jnp.int32, (M, M), 1)
@@ -341,24 +376,21 @@
     grams[M:, :] = jnp.concatenate([diagonal, top, jnp.zeros((6, M), F32)], axis=0)
 
 
-def apply_twice(own, g_hi, g_lo, swap_1, swap_2, x_hi, x_lo):
-    rows = RB * BLOCK
+def second_product(own, g_hi, g_lo, swap_1, swap_2, x_hi, x_lo, ends, p_hi, p_lo):
+    part = jax.ShapeDtypeStruct((RB * BLOCK, 256), BF16)
+    whole = jax.ShapeDtypeStruct(p_hi.shape, BF16)
     return pl.pallas_call(
-        apply_kernel,
-        out_shape=(
-            jax.ShapeDtypeStruct((rows, 256), BF16),
-            jax.ShapeDtypeStruct((rows, 256), BF16),
-            jax.ShapeDtypeStruct((M + 8, M), F32),
+        second_kernel,
+        out_shape=(part, part, jax.ShapeDtypeStruct((M + 8, M), F32), whole, whole),
+        in_specs=[VMEM] * 10,
+        out_specs=(VMEM,) * 5,
+        input_output_aliases={8: 3, 9: 4},
+        compiler_params=PARAMS,
+        cost_estimate=pl.CostEstimate(
+            flops=6 * RB * 128 * 256 * 256, bytes_accessed=8 << 20, transcendentals=0
         ),
-        in_specs=[VMEM] * 7,
-        out_specs=(VMEM, VMEM, VMEM),
-        scratch_shapes=[pltpu.VMEM((rows + 2 * BLOCK, 256), BF16)] * 2,
-        compiler_params=PARAMS,
-        cost_estimate=pl.CostEstimate(
-            flops=12 * RB * 128 * 256 * 256, bytes_accessed=12 << 20, transcendentals=0
-        ),
-        name="apply_twice",
-    )(own, g_hi, g_lo, swap_1, swap_2, x_hi, x_lo)
+        name="second_product",
+    )(own, g_hi, g_lo, swap_1, swap_2, x_hi, x_lo, ends, p_hi, p_lo)[:3]
 
 
 def inverse_factor(a, work):
@@ -539,9 +571,13 @@
     for chunk in chunks[:-1]:
         band = build(chunk, band)
     swap_1, swap_2 = build_edges(chunks[-1], band, start_block)
-    swap_1, swap_2 = neighbours(swap_1, 1), neighbours(swap_2, 0)
+    swap_2 = neighbours(swap_2, 0)
+    swap_1 = neighbours(swap_1, 1)
     g_hi, g_lo = build(chunks[-1], band, last=True)
-    z_hi, z_lo, grams = apply_twice(own, g_hi, g_lo, swap_1, swap_2, x_hi, x_lo)
+    p_hi, p_lo, ends = first_product(g_hi, g_lo, x_hi, x_lo)
+    z_hi, z_lo, grams = second_product(
+        own, g_hi, g_lo, swap_1, swap_2, x_hi, x_lo, ends, p_hi, p_lo
+    )
     grams = [grams] + gathered(grams, (), "blk")[0]
     return finish(grams, z_hi, z_lo, 2.0 * size * regions)
 

time: 53.7 us -> 52.7 us (0.981)
  starting transfers between devices: 12 us -> 10.1 us
  waiting for transfers between devices: 13.4 us -> 15 us
  Pallas kernels: 28 us -> 27.4 us
    ppermute x6, starting transfers between devices: 8.45 us -> 6.55 us  [swapped(): lax.ppermute(x, axis, [(i, i ^ far) for i in range(lax.axis_size(axis))])]
    ppermute x6, waiting for transfers between devices: 13.3 us -> 15 us  [swapped(): lax.ppermute(x, axis, [(i, i ^ far) for i in range(lax.axis_size(axis))])]
    pallas_call x1 -> x2, Pallas kernels: 5.77 us -> 5.18 us  [the longest x1 3.3 us: second_product(): pl.pallas_call(second_kernel, out_shape=(part, part, jax.ShapeDtypeStruct...]
  transfers between devices with their start and end apart: 8 -> 8, of which waited for: 4 -> 4; matrix products, arithmetic and copies ran while one was open for 0% -> 0% of each run, Pallas kernels for 20% -> 23%
where the time goes in v9:
time: 52.7 us; the launch traced here: 52.6 us
  Pallas kernels  27.4 us (52%)
  waiting for transfers between devices  15 us (28%)
  starting transfers between devices  10.1 us (19%)
    ppermute x6, waiting for transfers between devices, swapped(): lax.ppermute(x, axis, [(i, i ^ far) for i in range(lax.axis_size(axis))])  15 us
    pallas_call x4, Pallas kernels, build(): pl.pallas_call(partial(build_kernel, add, last), out_shape=out, in_specs=...  10.1 us
    pallas_call x1, Pallas kernels, finish(): pl.pallas_call(partial(finish_kernel, total_rows), out_shape=jax.ShapeDty...  9.52 us
    ppermute x6, starting transfers between devices, swapped(): lax.ppermute(x, axis, [(i, i ^ far) for i in range(lax.axis_size(axis))])  6.55 us
    ppermute x2, starting transfers between devices, neighbours(): return lax.ppermute(x, 'blk', pairs + [(j, i) for i, j in pairs])  3.51 us
    pallas_call x1, Pallas kernels, second_product(): pl.pallas_call(second_kernel, out_shape=(part, part, jax.ShapeDtypeStruct...  3.3 us
    pallas_call x1, Pallas kernels, first_product(): pl.pallas_call(first_kernel, out_shape=(shape, shape, jax.ShapeDtypeStruc...  1.88 us
    pallas_call x1, Pallas kernels, pack(): pl.pallas_call(partial(pack_kernel, total_blocks), out_shape=jax.ShapeDty...  1.22 us
  transfers between devices with their start and end apart: 8, of which 4 were waited for; matrix products, arithmetic and copies ran while one was open for 0% of the time, Pallas kernels for 23%

profile of v9, /device:TPU:0, one launch (start us, length us, event | category | flops | bytes accessed | tf_op | source)
XLA Modules:
  0.0 52.6 jit_solution(1798968086740565103)
XLA Ops:
  0.0 1.2 %pack.1.chunk.own = f32[520,128]{1,0:T(8,128)S(1)} custom-call(f32[512,128]{1,0:T(8,128)} %bitcast.4, s32[2,128]{1,0:T(2,128)} %bitcast.5, s32[2,128]{1,0:T(2,128)} %bitcast.6, f32[2,128]{1,0:T(2,128)} %bitcast.7), custom_call_target="tpu_custom_call" | custom-call | tf_op jit(solution)/shard_map/pack/pallas_call | solution.py:69
  1.2 0.0 copy-start
  1.2 4.1 %collective-permute-start = (f32[520,128]{1,0:T(8,128)S(1)}, f32[520,128]{1,0:T(8,128)S(1)}, u32[]{:S(2)}, u32[]{:S(2)}) collective-permute-start(f32[520,128]{1,0:T(8,128)S(1)} %pack.1.chunk.own), channel_id=1, source_target_pairs={{0,8},{4,12},{8,0},{12,4},{1,9},{5,13},{9,1},{13,5},{2,10},{6,14},... | collective-permute-start | bytes 798728 | tf_op jit(solution)/shard_map/ppermute | solution.py:542
  5.3 1.6 %collective-permute-start.2 = (f32[520,128]{1,0:T(8,128)S(1)}, f32[520,128]{1,0:T(8,128)S(1)}, u32[]{:S(2)}, u32[]{:S(2)}) collective-permute-start(f32[520,128]{1,0:T(8,128)S(1)} %pack.1.chunk.own), channel_id=1, source_target_pairs={{0,4},{4,0},{8,12},{12,8},{1,5},{5,1},{9,13},{13,9},{2,6},{6,2},{1... | collective-permute-start | bytes 798728 | tf_op jit(solution)/shard_map/ppermute | solution.py:542
  6.9 2.4 %band_terms.4.refs_0_ = f32[4096,256]{1,0:T(8,128)S(1)} custom-call(f32[520,128]{1,0:T(8,128)S(1)} %pack.1.chunk.own), custom_call_target="tpu_custom_call" | custom-call | flops 1048576 | bytes 65536 | tf_op jit(solution)/shard_map/band_terms/pallas_call | solution.py:161
  9.3 0.0 copy-done
  9.3 0.3 prepare.1
  9.6 7.9 %collective-permute-done.chunk = f32[520,128]{1,0:T(8,128)S(1)} collective-permute-done((f32[520,128]{1,0:T(8,128)S(1)}, f32[520,128]{1,0:T(8,128)S(1)}, u32[]{:S(2)}, u32[]{:S(2)}) %collective-permute-start) | collective-permute-done | bytes 266272 | tf_op jit(solution)/shard_map/ppermute | solution.py:542
  17.5 0.6 %collective-permute-start.1 = (f32[520,128]{1,0:T(8,128)S(1)}, f32[520,128]{1,0:T(8,128)S(1)}, u32[]{:S(2)}, u32[]{:S(2)}) collective-permute-start(f32[520,128]{1,0:T(8,128)S(1)} %collective-permute-done.chunk), channel_id=1, source_target_pairs={{0,4},{4,0},{8,12},{12,8},{1,5},{5,1},{9,13},{13,9},{2,6},{6,2},{1... | collective-permute-start | bytes 798728 | tf_op jit(solution)/shard_map/ppermute | solution.py:542
  18.2 2.6 %band_terms.5.refs_0_ = f32[4096,256]{1,0:T(8,128)S(1)} custom-call(f32[520,128]{1,0:T(8,128)S(1)} %collective-permute-done.chunk, f32[4096,256]{1,0:T(8,128)S(1)} %band_terms.4.refs_0_), custom_call_target="tpu_custom_call", output_to_operand_aliasing={{}: (1, {})} | custom-call | flops 1048576 | bytes 65536 | tf_op jit(solution)/shard_map/band_terms/pallas_call | solution.py:161
  20.8 0.0 collective-permute-done.2.chunk
  20.8 2.6 %band_terms.6.refs_0_.before = f32[4096,256]{1,0:T(8,128)S(1)} custom-call(f32[520,128]{1,0:T(8,128)S(1)} %collective-permute-done.2.chunk, f32[4096,256]{1,0:T(8,128)S(1)} %band_terms.5.refs_0_), custom_call_target="tpu_custom_call", output_to_operand_aliasing={{}: (1, {})} | custom-call | flops 1048576 | bytes 65536 | tf_op jit(solution)/shard_map/band_terms/pallas_call | solution.py:161
  23.3 1.7 %collective-permute-done.1.chunk = f32[520,128]{1,0:T(8,128)S(1)} collective-permute-done((f32[520,128]{1,0:T(8,128)S(1)}, f32[520,128]{1,0:T(8,128)S(1)}, u32[]{:S(2)}, u32[]{:S(2)}) %collective-permute-start.1) | collective-permute-done | bytes 266272 | tf_op jit(solution)/shard_map/ppermute | solution.py:542
  25.1 1.0 %edge_terms.1 = (f32[192,256]{1,0:T(8,128)S(1)}, f32[192,256]{1,0:T(8,128)S(1)}) custom-call(f32[520,128]{1,0:T(8,128)S(1)} %collective-permute-done.1.chunk, f32[4096,256]{1,0:T(8,128)S(1)} %band_terms.6.refs_0_.before, f32[2,2048,128]{2,1,0:T(8,128)S(1)} %copy-done), custom_call_target="tpu_custom_call" | custom-call | tf_op jit(solution)/shard_map/edge_terms/pallas_call | solution.py:239
  26.1 0.9 %collective-permute-start.3 = (f32[192,256]{1,0:T(8,128)S(1)}, f32[192,256]{1,0:T(8,128)S(1)}, u32[]{:S(2)}, u32[]{:S(2)}) collective-permute-start(f32[192,256]{1,0:T(8,128)S(1)} %get-tuple-element.27), channel_id=1, source_target_pairs={{1,2},{2,1},{5,6},{6,5},{9,10},{10,9},{13,14},{14,13},{17,18},{18,... | collective-permute-start | bytes 589832 | tf_op jit(solution)/shard_map/ppermute | solution.py:538
  26.9 2.7 %collective-permute-start.4 = (f32[192,256]{1,0:T(8,128)S(1)}, f32[192,256]{1,0:T(8,128)S(1)}, u32[]{:S(2)}, u32[]{:S(2)}) collective-permute-start(f32[192,256]{1,0:T(8,128)S(1)} %get-tuple-element.28), channel_id=1, source_target_pairs={{0,1},{2,3},{1,0},{3,2},{4,5},{6,7},{5,4},{7,6},{8,9},{10,11},{9,8... | collective-permute-start | bytes 589832 | tf_op jit(solution)/shard_map/ppermute | solution.py:538
  29.6 2.6 %band_terms.7 = (bf16[4096,256]{1,0:T(8,128)(2,1)S(1)}, bf16[4096,256]{1,0:T(8,128)(2,1)S(1)}) custom-call(f32[520,128]{1,0:T(8,128)S(1)} %collective-permute-done.1.chunk, f32[4096,256]{1,0:T(8,128)S(1)} %band_terms.6.refs_0_.before), custom_call_target="tpu_custom_call" | custom-call | flops 1048576 | bytes 65536 | tf_op jit(solution)/shard_map/band_terms/pallas_call | solution.py:161
  32.2 1.9 %first_product.1 = (bf16[2176,256]{1,0:T(8,128)(2,1)S(1)}, bf16[2176,256]{1,0:T(8,128)(2,1)S(1)}, f32[200,256]{1,0:T(8,128)S(1)}) custom-call(bf16[4096,256]{1,0:T(8,128)(2,1)S(1)} %get-tuple-element.25.g_hi, bf16[4096,256]{1,0:T(8,128)(2,1)S(1)} %get-tuple-element.26.g_lo, bf16[2048,256]{1,0:T(8,128)(2,1)S(1)} %get-tuple-element.29.x_hi, ...), custom_call_target="tpu_custom_call" | custom-call | flops 1048576 | bytes 65536 | tf_op jit(solution)/shard_map/first_product/pallas_call | solution.py:309
  34.1 0.0 collective-permute-done.3.swap_1
  34.1 0.0 collective-permute-done.4.swap_2
  34.1 3.3 %second_product.1 = (bf16[2048,256]{1,0:T(8,128)(2,1)S(1)}, bf16[2048,256]{1,0:T(8,128)(2,1)S(1)}, f32[136,128]{1,0:T(8,128)S(1)}, bf16[2176,256]{1,0:T(8,128)(2,1)S(1)}, bf16[2176,256]{1,0:T(8,128)(2,1)S(1)}) custom-call(f32[520,128]{1,0:T(8,128)S(1)} %pack.1.chunk.own, ...), custom_call_target="tpu_custom_call", output_to_operand_aliasing={{3}: (8, {}), {4}: (9, {})} | custom-call | flops 1610612736 | bytes 8388608 | tf_op jit(solution)/shard_map/second_product/pallas_call | solution.py:382
  37.4 0.2 collective-permute-start.5
  37.7 0.0 collective-permute-start.6
  37.7 4.1 %collective-permute-done.5.refs_1_ = f32[136,128]{1,0:T(8,128)S(1)} collective-permute-done((f32[136,128]{1,0:T(8,128)S(1)}, f32[136,128]{1,0:T(8,128)S(1)}, u32[]{:S(2)}, u32[]{:S(2)}) %collective-permute-start.5) | collective-permute-done | bytes 69664 | tf_op jit(solution)/shard_map/ppermute | solution.py:542
  41.8 0.0 collective-permute-start.7
  41.8 0.0 collective-permute-done.6.refs_2_
  41.8 1.3 %collective-permute-done.7.refs_3_ = f32[136,128]{1,0:T(8,128)S(1)} collective-permute-done((f32[136,128]{1,0:T(8,128)S(1)}, f32[136,128]{1,0:T(8,128)S(1)}, u32[]{:S(2)}, u32[]{:S(2)}) %collective-permute-start.7) | collective-permute-done | bytes 69664 | tf_op jit(solution)/shard_map/ppermute | solution.py:542
  43.1 9.5 %finish.1 = f32[2,2048,128]{2,1,0:T(8,128)} custom-call(f32[136,128]{1,0:T(8,128)S(1)} %get-tuple-element.34.refs_0_, f32[136,128]{1,0:T(8,128)S(1)} %collective-permute-done.5.refs_1_, f32[136,128]{1,0:T(8,128)S(1)} %collective-permute-done.6.refs_2_, f32[136,128]{1,0:T(8,128)S(1)} %collective-permute-done.7.refs_3_, ...), custom_call_target="tpu_custom_call" | custom-call | tf_op jit(solution)/shard_map/finish/pallas_call | solution.py:525
Async XLA Ops:
  1.2 8.1 %copy-start = (f32[2,2048,128]{2,1,0:T(8,128)S(1)}, f32[2,2048,128]{2,1,0:T(8,128)}, u32[]{:S(2)}) copy-start(f32[2,2048,128]{2,1,0:T(8,128)} %x.3) | copy-start | bytes 6291460
  1.2 16.3 %collective-permute-start = (f32[520,128]{1,0:T(8,128)S(1)}, f32[520,128]{1,0:T(8,128)S(1)}, u32[]{:S(2)}, u32[]{:S(2)}) collective-permute-start(f32[520,128]{1,0:T(8,128)S(1)} %pack.1.chunk.own), channel_id=1, source_target_pairs={{0,8},{4,12},{8,0},{12,4},{1,9},{5,13},{9,1},{13,5},{2,10},{6,14},... | collective-permute-start | bytes 798728 | tf_op jit(solution)/shard_map/ppermute | solution.py:542
  5.3 15.4 %collective-permute-start.2 = (f32[520,128]{1,0:T(8,128)S(1)}, f32[520,128]{1,0:T(8,128)S(1)}, u32[]{:S(2)}, u32[]{:S(2)}) collective-permute-start(f32[520,128]{1,0:T(8,128)S(1)} %pack.1.chunk.own), channel_id=1, source_target_pairs={{0,4},{4,0},{8,12},{12,8},{1,5},{5,1},{9,13},{13,9},{2,6},{6,2},{1... | collective-permute-start | bytes 798728 | tf_op jit(solution)/shard_map/ppermute | solution.py:542
  17.5 7.5 %collective-permute-start.1 = (f32[520,128]{1,0:T(8,128)S(1)}, f32[520,128]{1,0:T(8,128)S(1)}, u32[]{:S(2)}, u32[]{:S(2)}) collective-permute-start(f32[520,128]{1,0:T(8,128)S(1)} %collective-permute-done.chunk), channel_id=1, source_target_pairs={{0,4},{4,0},{8,12},{12,8},{1,5},{5,1},{9,13},{13,9},{2,6},{6,2},{1... | collective-permute-start | bytes 798728 | tf_op jit(solution)/shard_map/ppermute | solution.py:542
  26.1 8.0 %collective-permute-start.3 = (f32[192,256]{1,0:T(8,128)S(1)}, f32[192,256]{1,0:T(8,128)S(1)}, u32[]{:S(2)}, u32[]{:S(2)}) collective-permute-start(f32[192,256]{1,0:T(8,128)S(1)} %get-tuple-element.27), channel_id=1, source_target_pairs={{1,2},{2,1},{5,6},{6,5},{9,10},{10,9},{13,14},{14,13},{17,18},{18,... | collective-permute-start | bytes 589832 | tf_op jit(solution)/shard_map/ppermute | solution.py:538
  26.9 7.2 %collective-permute-start.4 = (f32[192,256]{1,0:T(8,128)S(1)}, f32[192,256]{1,0:T(8,128)S(1)}, u32[]{:S(2)}, u32[]{:S(2)}) collective-permute-start(f32[192,256]{1,0:T(8,128)S(1)} %get-tuple-element.28), channel_id=1, source_target_pairs={{0,1},{2,3},{1,0},{3,2},{4,5},{6,7},{5,4},{7,6},{8,9},{10,11},{9,8... | collective-permute-start | bytes 589832 | tf_op jit(solution)/shard_map/ppermute | solution.py:538
  37.4 4.4 %collective-permute-start.5 = (f32[136,128]{1,0:T(8,128)S(1)}, f32[136,128]{1,0:T(8,128)S(1)}, u32[]{:S(2)}, u32[]{:S(2)}) collective-permute-start(f32[136,128]{1,0:T(8,128)S(1)} %get-tuple-element.34.refs_0_), channel_id=1, source_target_pairs={{0,2},{1,3},{2,0},{3,1},{4,6},{5,7},{6,4},{7,5},{8,10},{9,11},{10,... | collective-permute-start | bytes 208904 | tf_op jit(solution)/shard_map/ppermute | solution.py:542
  37.7 4.1 %collective-permute-start.6 = (f32[136,128]{1,0:T(8,128)S(1)}, f32[136,128]{1,0:T(8,128)S(1)}, u32[]{:S(2)}, u32[]{:S(2)}) collective-permute-start(f32[136,128]{1,0:T(8,128)S(1)} %get-tuple-element.34.refs_0_), channel_id=1, source_target_pairs={{0,1},{1,0},{2,3},{3,2},{4,5},{5,4},{6,7},{7,6},{8,9},{9,8},{10,11... | collective-permute-start | bytes 208904 | tf_op jit(solution)/shard_map/ppermute | solution.py:542
  41.8 1.3 %collective-permute-start.7 = (f32[136,128]{1,0:T(8,128)S(1)}, f32[136,128]{1,0:T(8,128)S(1)}, u32[]{:S(2)}, u32[]{:S(2)}) collective-permute-start(f32[136,128]{1,0:T(8,128)S(1)} %collective-permute-done.5.refs_1_), channel_id=1, source_target_pairs={{0,1},{1,0},{2,3},{3,2},{4,5},{5,4},{6,7},{7,6},{8,9},{9,8},{10,11... | collective-permute-start | bytes 208904 | tf_op jit(solution)/shard_map/ppermute | solution.py:542

commit v10 on v9

--- a/solution.py
+++ b/solution.py
@@ -11,6 +11,7 @@
 RB = 32
 GROUP = 2
 OUTER = 64
+STEP = 256
 M = 128
 F32 = jnp.float32
 BF16 = jnp.bfloat16
@@ -470,7 +471,7 @@
 
 
 def finish_kernel(total_rows, *refs):
-    grams, (z_hi, z_lo, out, work) = refs[:-4], refs[-4:]
+    grams, (z_hi, z_lo, out, work, held, sems) = refs[:-6], refs[-6:]
     own = grams[0]
     row = lax.broadcasted_iota(jnp.int32, (M, M), 0)
     col = lax.broadcasted_iota(jnp.int32, (M, M), 1)
@@ -507,18 +508,18 @@
         ],
         axis=0,
     )
-    step = 256
-
-    def rows_of(i, carry):
-        at = pl.ds(pl.multiple_of(i * step, step), step)
+    copies = []
+    for i in range(z_hi.shape[0] // STEP):
+        at = pl.ds(i * STEP, STEP)
         hi, lo = z_hi[at, :], z_lo[at, :]
         for part in range(2):
             cols = slice(part * M, part * M + M)
             both = dot(jnp.concatenate([hi[:, cols], lo[:, cols]], axis=1), right)
-            out[part, at, :] = both[:, :M] + both[:, M:]
-        return carry
-
-    lax.fori_loop(0, z_hi.shape[0] // step, rows_of, 0, unroll=True)
+            held[part, at, :] = both[:, :M] + both[:, M:]
+        copies.append(pltpu.make_async_copy(held.at[:, at, :], out.at[:, at, :], sems.at[i]))
+        copies[-1].start()
+    for copy in copies:
+        copy.wait()
 
 
 def finish(grams, z_hi, z_lo, total_rows):
@@ -526,8 +527,12 @@
         partial(finish_kernel, total_rows),
         out_shape=jax.ShapeDtypeStruct((2, z_hi.shape[0], M), F32),
         in_specs=[VMEM] * (len(grams) + 2),
-        out_specs=VMEM,
-        scratch_shapes=[pltpu.VMEM((M, 2 * M), F32)],
+        out_specs=pl.BlockSpec(memory_space=pl.ANY),
+        scratch_shapes=[
+            pltpu.VMEM((M, 2 * M), F32),
+            pltpu.VMEM((2, z_hi.shape[0], M), F32),
+            pltpu.SemaphoreType.DMA((z_hi.shape[0] // STEP,)),
+        ],
         compiler_params=PARAMS,
         name="finish",
     )(*grams, z_hi, z_lo)

time: 52.7 us -> 52.5 us (level)
  transfers between devices with their start and end apart: 8 -> 8, of which waited for: 4 -> 4; matrix products, arithmetic and copies ran while one was open for 0% -> 0% of each run, Pallas kernels for 23% -> 24%
where the time goes in v10:
time: 52.5 us; the launch traced here: 52.3 us
  Pallas kernels  27 us (51%)
  waiting for transfers between devices  15 us (29%)
  starting transfers between devices  10.1 us (19%)
    ppermute x6, waiting for transfers between devices, swapped(): lax.ppermute(x, axis, [(i, i ^ far) for i in range(lax.axis_size(axis))])  15 us
    pallas_call x4, Pallas kernels, build(): pl.pallas_call(partial(build_kernel, add, last), out_shape=out, in_specs=...  10.1 us
    pallas_call x1, Pallas kernels, finish(): pl.pallas_call(partial(finish_kernel, total_rows), out_shape=jax.ShapeDty...  9.08 us
    ppermute x6, starting transfers between devices, swapped(): lax.ppermute(x, axis, [(i, i ^ far) for i in range(lax.axis_size(axis))])  6.55 us
    ppermute x2, starting transfers between devices, neighbours(): return lax.ppermute(x, 'blk', pairs + [(j, i) for i, j in pairs])  3.51 us
    pallas_call x1, Pallas kernels, second_product(): pl.pallas_call(second_kernel, out_shape=(part, part, jax.ShapeDtypeStruct...  3.3 us
    pallas_call x1, Pallas kernels, first_product(): pl.pallas_call(first_kernel, out_shape=(shape, shape, jax.ShapeDtypeStruc...  1.88 us
    pallas_call x1, Pallas kernels, pack(): pl.pallas_call(partial(pack_kernel, total_blocks), out_shape=jax.ShapeDty...  1.22 us
  transfers between devices with their start and end apart: 8, of which 4 were waited for; matrix products, arithmetic and copies ran while one was open for 0% of the time, Pallas kernels for 24%

profile of v10, /device:TPU:0, one launch (start us, length us, event | category | flops | bytes accessed | tf_op | source)
XLA Modules:
  0.0 52.3 jit_solution(12137503655728556903)
XLA Ops:
  0.0 1.2 %pack.1.chunk.own = f32[520,128]{1,0:T(8,128)S(1)} custom-call(f32[512,128]{1,0:T(8,128)} %bitcast.4, s32[2,128]{1,0:T(2,128)} %bitcast.5, s32[2,128]{1,0:T(2,128)} %bitcast.6, f32[2,128]{1,0:T(2,128)} %bitcast.7), custom_call_target="tpu_custom_call" | custom-call | tf_op jit(solution)/shard_map/pack/pallas_call | solution.py:70
  1.2 0.0 copy-start
  1.2 4.1 %collective-permute-start = (f32[520,128]{1,0:T(8,128)S(1)}, f32[520,128]{1,0:T(8,128)S(1)}, u32[]{:S(2)}, u32[]{:S(2)}) collective-permute-start(f32[520,128]{1,0:T(8,128)S(1)} %pack.1.chunk.own), channel_id=1, source_target_pairs={{0,8},{4,12},{8,0},{12,4},{1,9},{5,13},{9,1},{13,5},{2,10},{6,14},... | collective-permute-start | bytes 798728 | tf_op jit(solution)/shard_map/ppermute | solution.py:547
  5.3 1.6 %collective-permute-start.2 = (f32[520,128]{1,0:T(8,128)S(1)}, f32[520,128]{1,0:T(8,128)S(1)}, u32[]{:S(2)}, u32[]{:S(2)}) collective-permute-start(f32[520,128]{1,0:T(8,128)S(1)} %pack.1.chunk.own), channel_id=1, source_target_pairs={{0,4},{4,0},{8,12},{12,8},{1,5},{5,1},{9,13},{13,9},{2,6},{6,2},{1... | collective-permute-start | bytes 798728 | tf_op jit(solution)/shard_map/ppermute | solution.py:547
  6.9 2.4 %band_terms.4.refs_0_ = f32[4096,256]{1,0:T(8,128)S(1)} custom-call(f32[520,128]{1,0:T(8,128)S(1)} %pack.1.chunk.own), custom_call_target="tpu_custom_call" | custom-call | flops 1048576 | bytes 65536 | tf_op jit(solution)/shard_map/band_terms/pallas_call | solution.py:162
  9.3 0.0 copy-done
  9.3 0.3 prepare.1
  9.6 7.9 %collective-permute-done.chunk = f32[520,128]{1,0:T(8,128)S(1)} collective-permute-done((f32[520,128]{1,0:T(8,128)S(1)}, f32[520,128]{1,0:T(8,128)S(1)}, u32[]{:S(2)}, u32[]{:S(2)}) %collective-permute-start) | collective-permute-done | bytes 266272 | tf_op jit(solution)/shard_map/ppermute | solution.py:547
  17.5 0.6 %collective-permute-start.1 = (f32[520,128]{1,0:T(8,128)S(1)}, f32[520,128]{1,0:T(8,128)S(1)}, u32[]{:S(2)}, u32[]{:S(2)}) collective-permute-start(f32[520,128]{1,0:T(8,128)S(1)} %collective-permute-done.chunk), channel_id=1, source_target_pairs={{0,4},{4,0},{8,12},{12,8},{1,5},{5,1},{9,13},{13,9},{2,6},{6,2},{1... | collective-permute-start | bytes 798728 | tf_op jit(solution)/shard_map/ppermute | solution.py:547
  18.2 2.6 %band_terms.5.refs_0_ = f32[4096,256]{1,0:T(8,128)S(1)} custom-call(f32[520,128]{1,0:T(8,128)S(1)} %collective-permute-done.chunk, f32[4096,256]{1,0:T(8,128)S(1)} %band_terms.4.refs_0_), custom_call_target="tpu_custom_call", output_to_operand_aliasing={{}: (1, {})} | custom-call | flops 1048576 | bytes 65536 | tf_op jit(solution)/shard_map/band_terms/pallas_call | solution.py:162
  20.8 0.0 collective-permute-done.2.chunk
  20.8 2.6 %band_terms.6.refs_0_.before = f32[4096,256]{1,0:T(8,128)S(1)} custom-call(f32[520,128]{1,0:T(8,128)S(1)} %collective-permute-done.2.chunk, f32[4096,256]{1,0:T(8,128)S(1)} %band_terms.5.refs_0_), custom_call_target="tpu_custom_call", output_to_operand_aliasing={{}: (1, {})} | custom-call | flops 1048576 | bytes 65536 | tf_op jit(solution)/shard_map/band_terms/pallas_call | solution.py:162
  23.3 1.7 %collective-permute-done.1.chunk = f32[520,128]{1,0:T(8,128)S(1)} collective-permute-done((f32[520,128]{1,0:T(8,128)S(1)}, f32[520,128]{1,0:T(8,128)S(1)}, u32[]{:S(2)}, u32[]{:S(2)}) %collective-permute-start.1) | collective-permute-done | bytes 266272 | tf_op jit(solution)/shard_map/ppermute | solution.py:547
  25.1 1.0 %edge_terms.1 = (f32[192,256]{1,0:T(8,128)S(1)}, f32[192,256]{1,0:T(8,128)S(1)}) custom-call(f32[520,128]{1,0:T(8,128)S(1)} %collective-permute-done.1.chunk, f32[4096,256]{1,0:T(8,128)S(1)} %band_terms.6.refs_0_.before, f32[2,2048,128]{2,1,0:T(8,128)S(1)} %copy-done), custom_call_target="tpu_custom_call" | custom-call | tf_op jit(solution)/shard_map/edge_terms/pallas_call | solution.py:240
  26.1 0.9 %collective-permute-start.3 = (f32[192,256]{1,0:T(8,128)S(1)}, f32[192,256]{1,0:T(8,128)S(1)}, u32[]{:S(2)}, u32[]{:S(2)}) collective-permute-start(f32[192,256]{1,0:T(8,128)S(1)} %get-tuple-element.27), channel_id=1, source_target_pairs={{1,2},{2,1},{5,6},{6,5},{9,10},{10,9},{13,14},{14,13},{17,18},{18,... | collective-permute-start | bytes 589832 | tf_op jit(solution)/shard_map/ppermute | solution.py:543
  26.9 2.7 %collective-permute-start.4 = (f32[192,256]{1,0:T(8,128)S(1)}, f32[192,256]{1,0:T(8,128)S(1)}, u32[]{:S(2)}, u32[]{:S(2)}) collective-permute-start(f32[192,256]{1,0:T(8,128)S(1)} %get-tuple-element.28), channel_id=1, source_target_pairs={{0,1},{2,3},{1,0},{3,2},{4,5},{6,7},{5,4},{7,6},{8,9},{10,11},{9,8... | collective-permute-start | bytes 589832 | tf_op jit(solution)/shard_map/ppermute | solution.py:543
  29.6 2.6 %band_terms.7 = (bf16[4096,256]{1,0:T(8,128)(2,1)S(1)}, bf16[4096,256]{1,0:T(8,128)(2,1)S(1)}) custom-call(f32[520,128]{1,0:T(8,128)S(1)} %collective-permute-done.1.chunk, f32[4096,256]{1,0:T(8,128)S(1)} %band_terms.6.refs_0_.before), custom_call_target="tpu_custom_call" | custom-call | flops 1048576 | bytes 65536 | tf_op jit(solution)/shard_map/band_terms/pallas_call | solution.py:162
  32.2 1.9 %first_product.1 = (bf16[2176,256]{1,0:T(8,128)(2,1)S(1)}, bf16[2176,256]{1,0:T(8,128)(2,1)S(1)}, f32[200,256]{1,0:T(8,128)S(1)}) custom-call(bf16[4096,256]{1,0:T(8,128)(2,1)S(1)} %get-tuple-element.25.g_hi, bf16[4096,256]{1,0:T(8,128)(2,1)S(1)} %get-tuple-element.26.g_lo, bf16[2048,256]{1,0:T(8,128)(2,1)S(1)} %get-tuple-element.29.x_hi, ...), custom_call_target="tpu_custom_call" | custom-call | flops 1048576 | bytes 65536 | tf_op jit(solution)/shard_map/first_product/pallas_call | solution.py:310
  34.1 0.0 collective-permute-done.3.swap_1
  34.1 0.0 collective-permute-done.4.swap_2
  34.1 3.3 %second_product.1 = (bf16[2048,256]{1,0:T(8,128)(2,1)S(1)}, bf16[2048,256]{1,0:T(8,128)(2,1)S(1)}, f32[136,128]{1,0:T(8,128)S(1)}, bf16[2176,256]{1,0:T(8,128)(2,1)S(1)}, bf16[2176,256]{1,0:T(8,128)(2,1)S(1)}) custom-call(f32[520,128]{1,0:T(8,128)S(1)} %pack.1.chunk.own, ...), custom_call_target="tpu_custom_call", output_to_operand_aliasing={{3}: (8, {}), {4}: (9, {})} | custom-call | flops 1610612736 | bytes 8388608 | tf_op jit(solution)/shard_map/second_product/pallas_call | solution.py:383
  37.4 0.2 collective-permute-start.5
  37.7 0.0 collective-permute-start.6
  37.7 4.1 %collective-permute-done.5.refs_1_ = f32[136,128]{1,0:T(8,128)S(1)} collective-permute-done((f32[136,128]{1,0:T(8,128)S(1)}, f32[136,128]{1,0:T(8,128)S(1)}, u32[]{:S(2)}, u32[]{:S(2)}) %collective-permute-start.5) | collective-permute-done | bytes 69664 | tf_op jit(solution)/shard_map/ppermute | solution.py:547
  41.8 0.0 collective-permute-start.7
  41.8 0.0 collective-permute-done.6.refs_2_
  41.8 1.3 %collective-permute-done.7.refs_3_ = f32[136,128]{1,0:T(8,128)S(1)} collective-permute-done((f32[136,128]{1,0:T(8,128)S(1)}, f32[136,128]{1,0:T(8,128)S(1)}, u32[]{:S(2)}, u32[]{:S(2)}) %collective-permute-start.7) | collective-permute-done | bytes 69664 | tf_op jit(solution)/shard_map/ppermute | solution.py:547
  43.1 9.1 %finish.1 = f32[2,2048,128]{2,1,0:T(8,128)} custom-call(f32[136,128]{1,0:T(8,128)S(1)} %get-tuple-element.34.refs_0_, f32[136,128]{1,0:T(8,128)S(1)} %collective-permute-done.5.refs_1_, f32[136,128]{1,0:T(8,128)S(1)} %collective-permute-done.6.refs_2_, f32[136,128]{1,0:T(8,128)S(1)} %collective-permute-done.7.refs_3_, ...), custom_call_target="tpu_custom_call" | custom-call | tf_op jit(solution)/shard_map/finish/pallas_call | solution.py:526
Async XLA Ops:
  1.2 8.1 %copy-start = (f32[2,2048,128]{2,1,0:T(8,128)S(1)}, f32[2,2048,128]{2,1,0:T(8,128)}, u32[]{:S(2)}) copy-start(f32[2,2048,128]{2,1,0:T(8,128)} %x.3) | copy-start | bytes 6291460
  1.2 16.3 %collective-permute-start = (f32[520,128]{1,0:T(8,128)S(1)}, f32[520,128]{1,0:T(8,128)S(1)}, u32[]{:S(2)}, u32[]{:S(2)}) collective-permute-start(f32[520,128]{1,0:T(8,128)S(1)} %pack.1.chunk.own), channel_id=1, source_target_pairs={{0,8},{4,12},{8,0},{12,4},{1,9},{5,13},{9,1},{13,5},{2,10},{6,14},... | collective-permute-start | bytes 798728 | tf_op jit(solution)/shard_map/ppermute | solution.py:547
  5.3 15.4 %collective-permute-start.2 = (f32[520,128]{1,0:T(8,128)S(1)}, f32[520,128]{1,0:T(8,128)S(1)}, u32[]{:S(2)}, u32[]{:S(2)}) collective-permute-start(f32[520,128]{1,0:T(8,128)S(1)} %pack.1.chunk.own), channel_id=1, source_target_pairs={{0,4},{4,0},{8,12},{12,8},{1,5},{5,1},{9,13},{13,9},{2,6},{6,2},{1... | collective-permute-start | bytes 798728 | tf_op jit(solution)/shard_map/ppermute | solution.py:547
  17.5 7.5 %collective-permute-start.1 = (f32[520,128]{1,0:T(8,128)S(1)}, f32[520,128]{1,0:T(8,128)S(1)}, u32[]{:S(2)}, u32[]{:S(2)}) collective-permute-start(f32[520,128]{1,0:T(8,128)S(1)} %collective-permute-done.chunk), channel_id=1, source_target_pairs={{0,4},{4,0},{8,12},{12,8},{1,5},{5,1},{9,13},{13,9},{2,6},{6,2},{1... | collective-permute-start | bytes 798728 | tf_op jit(solution)/shard_map/ppermute | solution.py:547
  26.1 8.0 %collective-permute-start.3 = (f32[192,256]{1,0:T(8,128)S(1)}, f32[192,256]{1,0:T(8,128)S(1)}, u32[]{:S(2)}, u32[]{:S(2)}) collective-permute-start(f32[192,256]{1,0:T(8,128)S(1)} %get-tuple-element.27), channel_id=1, source_target_pairs={{1,2},{2,1},{5,6},{6,5},{9,10},{10,9},{13,14},{14,13},{17,18},{18,... | collective-permute-start | bytes 589832 | tf_op jit(solution)/shard_map/ppermute | solution.py:543
  26.9 7.2 %collective-permute-start.4 = (f32[192,256]{1,0:T(8,128)S(1)}, f32[192,256]{1,0:T(8,128)S(1)}, u32[]{:S(2)}, u32[]{:S(2)}) collective-permute-start(f32[192,256]{1,0:T(8,128)S(1)} %get-tuple-element.28), channel_id=1, source_target_pairs={{0,1},{2,3},{1,0},{3,2},{4,5},{6,7},{5,4},{7,6},{8,9},{10,11},{9,8... | collective-permute-start | bytes 589832 | tf_op jit(solution)/shard_map/ppermute | solution.py:543
  37.4 4.4 %collective-permute-start.5 = (f32[136,128]{1,0:T(8,128)S(1)}, f32[136,128]{1,0:T(8,128)S(1)}, u32[]{:S(2)}, u32[]{:S(2)}) collective-permute-start(f32[136,128]{1,0:T(8,128)S(1)} %get-tuple-element.34.refs_0_), channel_id=1, source_target_pairs={{0,2},{1,3},{2,0},{3,1},{4,6},{5,7},{6,4},{7,5},{8,10},{9,11},{10,... | collective-permute-start | bytes 208904 | tf_op jit(solution)/shard_map/ppermute | solution.py:547
  37.7 4.1 %collective-permute-start.6 = (f32[136,128]{1,0:T(8,128)S(1)}, f32[136,128]{1,0:T(8,128)S(1)}, u32[]{:S(2)}, u32[]{:S(2)}) collective-permute-start(f32[136,128]{1,0:T(8,128)S(1)} %get-tuple-element.34.refs_0_), channel_id=1, source_target_pairs={{0,1},{1,0},{2,3},{3,2},{4,5},{5,4},{6,7},{7,6},{8,9},{9,8},{10,11... | collective-permute-start | bytes 208904 | tf_op jit(solution)/shard_map/ppermute | solution.py:547
  41.8 1.3 %collective-permute-start.7 = (f32[136,128]{1,0:T(8,128)S(1)}, f32[136,128]{1,0:T(8,128)S(1)}, u32[]{:S(2)}, u32[]{:S(2)}) collective-permute-start(f32[136,128]{1,0:T(8,128)S(1)} %collective-permute-done.5.refs_1_), channel_id=1, source_target_pairs={{0,1},{1,0},{2,3},{3,2},{4,5},{5,4},{6,7},{7,6},{8,9},{9,8},{10,11... | collective-permute-start | bytes 208904 | tf_op jit(solution)/shard_map/ppermute | solution.py:547

commit v11 on v10

--- a/solution.py
+++ b/solution.py
@@ -579,6 +579,7 @@
     swap_2 = neighbours(swap_2, 0)
     swap_1 = neighbours(swap_1, 1)
     g_hi, g_lo = build(chunks[-1], band, last=True)
+    swap_2, g_hi, g_lo = lax.optimization_barrier((swap_2, g_hi, g_lo))
     p_hi, p_lo, ends = first_product(g_hi, g_lo, x_hi, x_lo)
     z_hi, z_lo, grams = second_product(
         own, g_hi, g_lo, swap_1, swap_2, x_hi, x_lo, ends, p_hi, p_lo

time: 52.5 us -> 51.6 us (0.983)
  waiting for transfers between devices: 15 us -> 13.5 us
  starting transfers between devices: 10.1 us -> 10.8 us
    ppermute x6, starting transfers between devices: 6.55 us -> 9.83 us  [swapped(): lax.ppermute(x, axis, [(i, i ^ far) for i in range(lax.axis_size(axis))])]
    ppermute x2, starting transfers between devices: 3.51 us -> 0.92 us  [neighbours(): return lax.ppermute(x, 'blk', pairs + [(j, i) for i, j in pairs])]
    ppermute x6, waiting for transfers between devices: 15 us -> 13.5 us  [swapped(): lax.ppermute(x, axis, [(i, i ^ far) for i in range(lax.axis_size(axis))])]
where the time goes in v11:
time: 51.6 us; the launch traced here: 51.5 us
  Pallas kernels  27 us (52%)
  waiting for transfers between devices  13.5 us (26%)
  starting transfers between devices  10.8 us (21%)
    ppermute x6, waiting for transfers between devices, swapped(): lax.ppermute(x, axis, [(i, i ^ far) for i in range(lax.axis_size(axis))])  13.5 us
    pallas_call x4, Pallas kernels, build(): pl.pallas_call(partial(build_kernel, add, last), out_shape=out, in_specs=...  10.1 us
    ppermute x6, starting transfers between devices, swapped(): lax.ppermute(x, axis, [(i, i ^ far) for i in range(lax.axis_size(axis))])  9.83 us
    pallas_call x1, Pallas kernels, finish(): pl.pallas_call(partial(finish_kernel, total_rows), out_shape=jax.ShapeDty...  9.08 us
    pallas_call x1, Pallas kernels, second_product(): pl.pallas_call(second_kernel, out_shape=(part, part, jax.ShapeDtypeStruct...  3.29 us
    pallas_call x1, Pallas kernels, first_product(): pl.pallas_call(first_kernel, out_shape=(shape, shape, jax.ShapeDtypeStruc...  1.89 us
    pallas_call x1, Pallas kernels, pack(): pl.pallas_call(partial(pack_kernel, total_blocks), out_shape=jax.ShapeDty...  1.22 us
  transfers between devices with their start and end apart: 8, of which 4 were waited for; matrix products, arithmetic and copies ran while one was open for 0% of the time, Pallas kernels for 24%

profile of v11, /device:TPU:0, one launch (start us, length us, event | category | flops | bytes accessed | tf_op | source)
XLA Modules:
  0.0 51.5 jit_solution(16506204369258714996)
XLA Ops:
  0.0 1.2 %pack.1.chunk.own = f32[520,128]{1,0:T(8,128)S(1)} custom-call(f32[512,128]{1,0:T(8,128)} %bitcast.4, s32[2,128]{1,0:T(2,128)} %bitcast.5, s32[2,128]{1,0:T(2,128)} %bitcast.6, f32[2,128]{1,0:T(2,128)} %bitcast.7), custom_call_target="tpu_custom_call" | custom-call | tf_op jit(solution)/shard_map/pack/pallas_call | solution.py:70
  1.2 0.0 copy-start
  1.2 4.1 %collective-permute-start = (f32[520,128]{1,0:T(8,128)S(1)}, f32[520,128]{1,0:T(8,128)S(1)}, u32[]{:S(2)}, u32[]{:S(2)}) collective-permute-start(f32[520,128]{1,0:T(8,128)S(1)} %pack.1.chunk.own), channel_id=1, source_target_pairs={{0,8},{4,12},{8,0},{12,4},{1,9},{5,13},{9,1},{13,5},{2,10},{6,14},... | collective-permute-start | bytes 798728 | tf_op jit(solution)/shard_map/ppermute | solution.py:547
  5.3 1.6 %collective-permute-start.2 = (f32[520,128]{1,0:T(8,128)S(1)}, f32[520,128]{1,0:T(8,128)S(1)}, u32[]{:S(2)}, u32[]{:S(2)}) collective-permute-start(f32[520,128]{1,0:T(8,128)S(1)} %pack.1.chunk.own), channel_id=1, source_target_pairs={{0,4},{4,0},{8,12},{12,8},{1,5},{5,1},{9,13},{13,9},{2,6},{6,2},{1... | collective-permute-start | bytes 798728 | tf_op jit(solution)/shard_map/ppermute | solution.py:547
  6.9 2.4 %band_terms.4.refs_0_ = f32[4096,256]{1,0:T(8,128)S(1)} custom-call(f32[520,128]{1,0:T(8,128)S(1)} %pack.1.chunk.own), custom_call_target="tpu_custom_call" | custom-call | flops 1048576 | bytes 65536 | tf_op jit(solution)/shard_map/band_terms/pallas_call | solution.py:162
  9.3 0.0 copy-done
  9.3 0.3 prepare.1
  9.6 7.9 %collective-permute-done.chunk = f32[520,128]{1,0:T(8,128)S(1)} collective-permute-done((f32[520,128]{1,0:T(8,128)S(1)}, f32[520,128]{1,0:T(8,128)S(1)}, u32[]{:S(2)}, u32[]{:S(2)}) %collective-permute-start) | collective-permute-done | bytes 266272 | tf_op jit(solution)/shard_map/ppermute | solution.py:547
  17.5 0.6 %collective-permute-start.1 = (f32[520,128]{1,0:T(8,128)S(1)}, f32[520,128]{1,0:T(8,128)S(1)}, u32[]{:S(2)}, u32[]{:S(2)}) collective-permute-start(f32[520,128]{1,0:T(8,128)S(1)} %collective-permute-done.chunk), channel_id=1, source_target_pairs={{0,4},{4,0},{8,12},{12,8},{1,5},{5,1},{9,13},{13,9},{2,6},{6,2},{1... | collective-permute-start | bytes 798728 | tf_op jit(solution)/shard_map/ppermute | solution.py:547
  18.2 2.6 %band_terms.5.refs_0_ = f32[4096,256]{1,0:T(8,128)S(1)} custom-call(f32[520,128]{1,0:T(8,128)S(1)} %collective-permute-done.chunk, f32[4096,256]{1,0:T(8,128)S(1)} %band_terms.4.refs_0_), custom_call_target="tpu_custom_call", output_to_operand_aliasing={{}: (1, {})} | custom-call | flops 1048576 | bytes 65536 | tf_op jit(solution)/shard_map/band_terms/pallas_call | solution.py:162
  20.8 0.0 collective-permute-done.2.chunk
  20.8 2.6 %band_terms.6.before.refs_0_ = f32[4096,256]{1,0:T(8,128)S(1)} custom-call(f32[520,128]{1,0:T(8,128)S(1)} %collective-permute-done.2.chunk, f32[4096,256]{1,0:T(8,128)S(1)} %band_terms.5.refs_0_), custom_call_target="tpu_custom_call", output_to_operand_aliasing={{}: (1, {})} | custom-call | flops 1048576 | bytes 65536 | tf_op jit(solution)/shard_map/band_terms/pallas_call | solution.py:162
  23.3 1.7 %collective-permute-done.1.chunk = f32[520,128]{1,0:T(8,128)S(1)} collective-permute-done((f32[520,128]{1,0:T(8,128)S(1)}, f32[520,128]{1,0:T(8,128)S(1)}, u32[]{:S(2)}, u32[]{:S(2)}) %collective-permute-start.1) | collective-permute-done | bytes 266272 | tf_op jit(solution)/shard_map/ppermute | solution.py:547
  25.1 1.0 %edge_terms.1 = (f32[192,256]{1,0:T(8,128)S(1)}, f32[192,256]{1,0:T(8,128)S(1)}) custom-call(f32[520,128]{1,0:T(8,128)S(1)} %collective-permute-done.1.chunk, f32[4096,256]{1,0:T(8,128)S(1)} %band_terms.6.before.refs_0_, f32[2,2048,128]{2,1,0:T(8,128)S(1)} %copy-done), custom_call_target="tpu_custom_call" | custom-call | tf_op jit(solution)/shard_map/edge_terms/pallas_call | solution.py:240
  26.1 0.1 collective-permute-start.3
  26.2 0.9 %collective-permute-start.4 = (f32[192,256]{1,0:T(8,128)S(1)}, f32[192,256]{1,0:T(8,128)S(1)}, u32[]{:S(2)}, u32[]{:S(2)}) collective-permute-start(f32[192,256]{1,0:T(8,128)S(1)} %get-tuple-element.33), channel_id=1, source_target_pairs={{1,2},{2,1},{5,6},{6,5},{9,10},{10,9},{13,14},{14,13},{17,18},{18,... | collective-permute-start | bytes 589832 | tf_op jit(solution)/shard_map/ppermute | solution.py:543
  27.0 2.6 %band_terms.7 = (bf16[4096,256]{1,0:T(8,128)(2,1)S(1)}, bf16[4096,256]{1,0:T(8,128)(2,1)S(1)}) custom-call(f32[520,128]{1,0:T(8,128)S(1)} %collective-permute-done.1.chunk, f32[4096,256]{1,0:T(8,128)S(1)} %band_terms.6.before.refs_0_), custom_call_target="tpu_custom_call" | custom-call | flops 1048576 | bytes 65536 | tf_op jit(solution)/shard_map/band_terms/pallas_call | solution.py:162
  29.6 0.0 collective-permute-done.3.swap_2
  29.6 1.9 %first_product.1 = (bf16[2176,256]{1,0:T(8,128)(2,1)S(1)}, bf16[2176,256]{1,0:T(8,128)(2,1)S(1)}, f32[200,256]{1,0:T(8,128)S(1)}) custom-call(bf16[4096,256]{1,0:T(8,128)(2,1)S(1)} %get-tuple-element.31.g_hi, bf16[4096,256]{1,0:T(8,128)(2,1)S(1)} %get-tuple-element.32.g_lo, bf16[2048,256]{1,0:T(8,128)(2,1)S(1)} %get-tuple-element.35.x_hi, ...), custom_call_target="tpu_custom_call" | custom-call | flops 1048576 | bytes 65536 | tf_op jit(solution)/shard_map/first_product/pallas_call | solution.py:310
  31.5 0.0 collective-permute-done.4.swap_1
  31.6 3.3 %second_product.1 = (bf16[2048,256]{1,0:T(8,128)(2,1)S(1)}, bf16[2048,256]{1,0:T(8,128)(2,1)S(1)}, f32[136,128]{1,0:T(8,128)S(1)}, bf16[2176,256]{1,0:T(8,128)(2,1)S(1)}, bf16[2176,256]{1,0:T(8,128)(2,1)S(1)}) custom-call(f32[520,128]{1,0:T(8,128)S(1)} %pack.1.chunk.own, ...), custom_call_target="tpu_custom_call", output_to_operand_aliasing={{3}: (8, {}), {4}: (9, {})} | custom-call | flops 1610612736 | bytes 8388608 | tf_op jit(solution)/shard_map/second_product/pallas_call | solution.py:383
  34.8 3.4 %collective-permute-start.5 = (f32[136,128]{1,0:T(8,128)S(1)}, f32[136,128]{1,0:T(8,128)S(1)}, u32[]{:S(2)}, u32[]{:S(2)}) collective-permute-start(f32[136,128]{1,0:T(8,128)S(1)} %get-tuple-element.40.refs_0_), channel_id=1, source_target_pairs={{0,2},{1,3},{2,0},{3,1},{4,6},{5,7},{6,4},{7,5},{8,10},{9,11},{10,... | collective-permute-start | bytes 208904 | tf_op jit(solution)/shard_map/ppermute | solution.py:547
  38.3 0.0 collective-permute-start.6
  38.3 2.7 %collective-permute-done.5.refs_1_ = f32[136,128]{1,0:T(8,128)S(1)} collective-permute-done((f32[136,128]{1,0:T(8,128)S(1)}, f32[136,128]{1,0:T(8,128)S(1)}, u32[]{:S(2)}, u32[]{:S(2)}) %collective-permute-start.5) | collective-permute-done | bytes 69664 | tf_op jit(solution)/shard_map/ppermute | solution.py:547
  41.0 0.1 collective-permute-start.7
  41.1 0.0 collective-permute-done.6.refs_2_
  41.1 1.1 %collective-permute-done.7.refs_3_ = f32[136,128]{1,0:T(8,128)S(1)} collective-permute-done((f32[136,128]{1,0:T(8,128)S(1)}, f32[136,128]{1,0:T(8,128)S(1)}, u32[]{:S(2)}, u32[]{:S(2)}) %collective-permute-start.7) | collective-permute-done | bytes 69664 | tf_op jit(solution)/shard_map/ppermute | solution.py:547
  42.3 9.1 %finish.1 = f32[2,2048,128]{2,1,0:T(8,128)} custom-call(f32[136,128]{1,0:T(8,128)S(1)} %get-tuple-element.40.refs_0_, f32[136,128]{1,0:T(8,128)S(1)} %collective-permute-done.5.refs_1_, f32[136,128]{1,0:T(8,128)S(1)} %collective-permute-done.6.refs_2_, f32[136,128]{1,0:T(8,128)S(1)} %collective-permute-done.7.refs_3_, ...), custom_call_target="tpu_custom_call" | custom-call | tf_op jit(solution)/shard_map/finish/pallas_call | solution.py:526
Async XLA Ops:
  1.2 8.1 %copy-start = (f32[2,2048,128]{2,1,0:T(8,128)S(1)}, f32[2,2048,128]{2,1,0:T(8,128)}, u32[]{:S(2)}) copy-start(f32[2,2048,128]{2,1,0:T(8,128)} %x.3) | copy-start | bytes 6291460
  1.2 16.3 %collective-permute-start = (f32[520,128]{1,0:T(8,128)S(1)}, f32[520,128]{1,0:T(8,128)S(1)}, u32[]{:S(2)}, u32[]{:S(2)}) collective-permute-start(f32[520,128]{1,0:T(8,128)S(1)} %pack.1.chunk.own), channel_id=1, source_target_pairs={{0,8},{4,12},{8,0},{12,4},{1,9},{5,13},{9,1},{13,5},{2,10},{6,14},... | collective-permute-start | bytes 798728 | tf_op jit(solution)/shard_map/ppermute | solution.py:547
  5.3 15.4 %collective-permute-start.2 = (f32[520,128]{1,0:T(8,128)S(1)}, f32[520,128]{1,0:T(8,128)S(1)}, u32[]{:S(2)}, u32[]{:S(2)}) collective-permute-start(f32[520,128]{1,0:T(8,128)S(1)} %pack.1.chunk.own), channel_id=1, source_target_pairs={{0,4},{4,0},{8,12},{12,8},{1,5},{5,1},{9,13},{13,9},{2,6},{6,2},{1... | collective-permute-start | bytes 798728 | tf_op jit(solution)/shard_map/ppermute | solution.py:547
  17.5 7.5 %collective-permute-start.1 = (f32[520,128]{1,0:T(8,128)S(1)}, f32[520,128]{1,0:T(8,128)S(1)}, u32[]{:S(2)}, u32[]{:S(2)}) collective-permute-start(f32[520,128]{1,0:T(8,128)S(1)} %collective-permute-done.chunk), channel_id=1, source_target_pairs={{0,4},{4,0},{8,12},{12,8},{1,5},{5,1},{9,13},{13,9},{2,6},{6,2},{1... | collective-permute-start | bytes 798728 | tf_op jit(solution)/shard_map/ppermute | solution.py:547
  26.1 3.6 %collective-permute-start.3 = (f32[192,256]{1,0:T(8,128)S(1)}, f32[192,256]{1,0:T(8,128)S(1)}, u32[]{:S(2)}, u32[]{:S(2)}) collective-permute-start(f32[192,256]{1,0:T(8,128)S(1)} %get-tuple-element.28), channel_id=1, source_target_pairs={{0,1},{2,3},{1,0},{3,2},{4,5},{6,7},{5,4},{7,6},{8,9},{10,11},{9,8... | collective-permute-start | bytes 589832 | tf_op jit(solution)/shard_map/ppermute | solution.py:543
  26.2 5.4 %collective-permute-start.4 = (f32[192,256]{1,0:T(8,128)S(1)}, f32[192,256]{1,0:T(8,128)S(1)}, u32[]{:S(2)}, u32[]{:S(2)}) collective-permute-start(f32[192,256]{1,0:T(8,128)S(1)} %get-tuple-element.33), channel_id=1, source_target_pairs={{1,2},{2,1},{5,6},{6,5},{9,10},{10,9},{13,14},{14,13},{17,18},{18,... | collective-permute-start | bytes 589832 | tf_op jit(solution)/shard_map/ppermute | solution.py:543
  34.8 6.1 %collective-permute-start.5 = (f32[136,128]{1,0:T(8,128)S(1)}, f32[136,128]{1,0:T(8,128)S(1)}, u32[]{:S(2)}, u32[]{:S(2)}) collective-permute-start(f32[136,128]{1,0:T(8,128)S(1)} %get-tuple-element.40.refs_0_), channel_id=1, source_target_pairs={{0,2},{1,3},{2,0},{3,1},{4,6},{5,7},{6,4},{7,5},{8,10},{9,11},{10,... | collective-permute-start | bytes 208904 | tf_op jit(solution)/shard_map/ppermute | solution.py:547
  38.3 2.9 %collective-permute-start.6 = (f32[136,128]{1,0:T(8,128)S(1)}, f32[136,128]{1,0:T(8,128)S(1)}, u32[]{:S(2)}, u32[]{:S(2)}) collective-permute-start(f32[136,128]{1,0:T(8,128)S(1)} %get-tuple-element.40.refs_0_), channel_id=1, source_target_pairs={{0,1},{1,0},{2,3},{3,2},{4,5},{5,4},{6,7},{7,6},{8,9},{9,8},{10,11... | collective-permute-start | bytes 208904 | tf_op jit(solution)/shard_map/ppermute | solution.py:547
  41.0 1.3 %collective-permute-start.7 = (f32[136,128]{1,0:T(8,128)S(1)}, f32[136,128]{1,0:T(8,128)S(1)}, u32[]{:S(2)}, u32[]{:S(2)}) collective-permute-start(f32[136,128]{1,0:T(8,128)S(1)} %collective-permute-done.5.refs_1_), channel_id=1, source_target_pairs={{0,1},{1,0},{2,3},{3,2},{4,5},{5,4},{6,7},{7,6},{8,9},{9,8},{10,11... | collective-permute-start | bytes 208904 | tf_op jit(solution)/shard_map/ppermute | solution.py:547
